TPU v7x, 256 devices: a whole 4x4x8 slice. The times are simulated.
256 devices in a mesh: section: 16 (over y, x), tensor: 16 (over z, core).
Axes of the slice: x: 4, y: 4, z: 8, core: 2. Of those that a mesh axis runs over, the one named last changes fastest.
Arguments:
- cot_in: bfloat16 [4096, 2304], P(('section', 'tensor')), may hold values from -6 to 6
- saved_inputs: bfloat16 [3, 4096, 2304], P(None, ('section', 'tensor')), may hold values from -6 to 6
- queries: bfloat16 [3, 4096, 4096], P(None, 'section', 'tensor'), may hold values from -120 to 120
- keys: bfloat16 [3, 4096, 2048], P(None, 'section', 'tensor'), may hold values from -6 to 6
- values: bfloat16 [3, 4096, 2048], P(None, 'section', 'tensor'), may hold values from -6 to 6
- docs: int32 [3, 16, 256], P(None, 'section'), may hold values from 0 to 7, never falling along the last dimension, each value on 1 to 128 neighbouring positions
- plan: int32 [3, 16], P(None, 'section'), may hold values from 0 to 1
- w_value: bfloat16 [2, 16, 2304, 2048], P(None, 'section', None, 'tensor'), may hold values from -0.125 to 0.125
- w_out: bfloat16 [2, 16, 4096, 2304], P(None, 'section', 'tensor'), may hold values from -0.09375 to 0.09375
- norm_gain: bfloat16 [2, 16, 2304], P(None, 'section'), may hold values from 0.099609375 to 1.8984375
Outputs:
- cot_out: bfloat16 [4096, 2304], P(('section', 'tensor'))
- grad_queries: bfloat16 [3, 4096, 4096], P(None, 'section', 'tensor')
- grad_keys: bfloat16 [3, 4096, 2048], P(None, 'section', 'tensor')
Inputs may be any that keep to these rules, and one draw needn't show every extreme that they name: `docs`: document ids never fall along a sequence.
All inputs are finite; a program needn't handle non-finite values.
Results may differ from a plain program's by a relative error of at most 0.035.
Values may be sent and summed in bfloat16 or wider, within the bound.
No kernel may reach another device: no remote copies, remote signals or barrier semaphores. Data moves between devices by JAX's collectives and lax.ppermute only.
A program may use at most 64 MiB of HBM per device.

v0:
```python
import jax
import jax.numpy as jnp
from jax import lax
from jax.sharding import PartitionSpec as P

HD = 128
TICKS = 3


SCALE = 144.0 ** (-0.5)
EPS = 1e-06
NEGATIVE = -1e30


def passed_along(shard, axis, by):
    size = lax.axis_size(axis)
    return lax.ppermute(shard, axis, [(i, (i + by) % size) for i in range(size)])


def attention_grads(grad_out, queries, keys, values, docs):
    length = queries.shape[0]
    kv_heads = keys.shape[1] // HD
    group_size = queries.shape[1] // keys.shape[1]
    query_heads = queries.reshape(length, kv_heads, group_size, HD)
    key_heads = keys.reshape(length, kv_heads, HD)
    value_heads = values.reshape(length, kv_heads, HD)
    grad_heads = grad_out.reshape(length, kv_heads, group_size, HD)
    position = jnp.arange(length, dtype=jnp.int32)
    allowed = (position[:, None] >= position[None, :]) & (docs[:, None] == docs[None, :])
    scores = (
        jnp.einsum("qcgd,kcd->cgqk", query_heads, key_heads, preferred_element_type=jnp.float32)
        * SCALE
    )
    scores = jnp.where(allowed, scores, NEGATIVE)
    row_max = jnp.max(scores, axis=-1, keepdims=True)
    expsum = jnp.exp(scores - row_max)
    chance = expsum / jnp.sum(expsum, axis=-1, keepdims=True)
    chance_low = chance.astype(jnp.bfloat16)
    attended = jnp.einsum(
        "cgqk,kcd->cgqd", chance_low, value_heads, preferred_element_type=jnp.float32
    )
    row_dot = jnp.sum(
        jnp.transpose(grad_heads, (1, 2, 0, 3)).astype(jnp.float32) * attended, axis=-1
    )
    grad_chance = jnp.einsum(
        "qcgd,kcd->cgqk", grad_heads, value_heads, preferred_element_type=jnp.float32
    )
    grad_scores = (chance * (grad_chance - row_dot[..., None])).astype(jnp.bfloat16)
    grad_query = (
        jnp.einsum("cgqk,kcd->qcgd", grad_scores, key_heads, preferred_element_type=jnp.float32)
        * SCALE
    ).astype(jnp.bfloat16)
    grad_key = (
        jnp.einsum("cgqk,qcgd->kcd", grad_scores, query_heads, preferred_element_type=jnp.float32)
        * SCALE
    ).astype(jnp.bfloat16)
    grad_value = jnp.einsum(
        "cgqk,qcgd->kcd", chance_low, grad_heads, preferred_element_type=jnp.float32
    ).astype(jnp.bfloat16)
    return (
        grad_query.reshape(length, -1),
        grad_key.reshape(length, -1),
        grad_value.reshape(length, -1),
    )


def norm_back(cotangent, inputs, gain_row, summed):
    inputs_wide = inputs.astype(jnp.float32)
    inverse = lax.rsqrt(jnp.mean(inputs_wide * inputs_wide, axis=-1, keepdims=True) + EPS)
    scaled = summed * gain_row.astype(jnp.float32)
    inner_mean = jnp.mean(scaled * inputs_wide, axis=-1, keepdims=True)
    updated = (
        cotangent.astype(jnp.float32)
        + inverse * scaled
        - inputs_wide * inverse * inverse * inverse * inner_mean
    )
    return updated.astype(jnp.bfloat16)


def on_device(cot_in, saved_inputs, queries, keys, values, docs, plan, w_value, w_out, norm_gain):
    current = cot_in
    query_list = []
    key_list = []
    for step_index in range(TICKS):
        chosen = plan[step_index, 0]
        value_weight = lax.dynamic_index_in_dim(w_value[:, 0], chosen, 0, keepdims=False)
        out_weight = lax.dynamic_index_in_dim(w_out[:, 0], chosen, 0, keepdims=False)
        gain_row = lax.dynamic_index_in_dim(norm_gain[:, 0], chosen, 0, keepdims=False)
        grad_out = lax.dot_general(
            lax.all_gather(current, "tensor", axis=0, tiled=True),
            out_weight,
            (((1,), (1,)), ((), ())),
            preferred_element_type=jnp.float32,
        ).astype(jnp.bfloat16)
        grad_query, grad_key, grad_value = attention_grads(
            grad_out, queries[step_index], keys[step_index], values[step_index], docs[step_index, 0]
        )
        query_list.append(grad_query)
        key_list.append(grad_key)
        summed = lax.psum_scatter(
            lax.dot_general(
                grad_value,
                value_weight,
                (((1,), (1,)), ((), ())),
                preferred_element_type=jnp.float32,
            ).astype(jnp.bfloat16),
            "tensor",
            scatter_dimension=0,
            tiled=True,
        ).astype(jnp.float32)
        updated = norm_back(current, saved_inputs[step_index], gain_row, summed)
        current = passed_along(updated, "section", -1)
    return (current, jnp.stack(query_list), jnp.stack(key_list))


def solution(mesh):
    return jax.shard_map(
        on_device,
        mesh=mesh,
        in_specs=(
            P(("section", "tensor"), None),
            P(None, ("section", "tensor"), None),
            P(None, "section", "tensor"),
            P(None, "section", "tensor"),
            P(None, "section", "tensor"),
            P(None, "section", None),
            P(None, "section"),
            P(None, "section", None, "tensor"),
            P(None, "section", "tensor", None),
            P(None, "section", None),
        ),
        out_specs=(
            P(("section", "tensor"), None),
            P(None, "section", "tensor"),
            P(None, "section", "tensor"),
        ),
        check_vma=False,
    )
```

profile of v0, /device:TPU:30, one launch (start us, length us, event | category | flops | bytes accessed | tf_op | source)
XLA Modules:
  0.0 349.7 jit_solution(2738741408513327389)
XLA Ops:
  8.0 1.8 fusion.138
  9.8 1.4 fusion.140
  13.1 1.3 fusion.139
  14.5 1.1 fusion.141
  15.8 35.5 %all-gather.4.cloned.1.call-done = bf16[256,2304]{1,0:T(8,128)(2,1)} async-done(((bf16[16,2304]{1,0:T(8,128)(2,1)}), bf16[256,2304]{1,0:T(8,128)(2,1)}) %all-gather.4.cloned.1.call-update) | async-done | bytes 1179664 | tf_op jit(solution)/shard_map/all_gather | solution.py:90
  51.3 2.4 fusion.33
  53.8 3.0 convolution_convert_fusion.2
  61.4 52.1 %reduce-scatter.4.cloned.1.call-done = bf16[16,2304]{1,0:T(8,128)(2,1)} async-done(((bf16[256,2304]{1,0:T(8,128)(2,1)}), bf16[16,2304]{1,0:T(8,128)(2,1)}) %reduce-scatter.4.cloned.1.call-update) | async-done | bytes 73744 | tf_op jit(solution)/shard_map/reduce_scatter | solution.py:100
  113.4 1.6 fusion.101
  115.1 1.0 fusion.92
  116.8 7.0 %collective-permute-done = bf16[16,2304]{1,0:T(8,128)(2,1)S(1)} collective-permute-done((bf16[16,2304]{1,0:T(8,128)(2,1)S(1)}, bf16[16,2304]{1,0:T(8,128)(2,1)S(1)}, u32[]{:S(2)}, u32[]{:S(2)}) %collective-permute-start) | collective-permute-done | bytes 73760 | tf_op jit(solution)/shard_map/ppermute | solution.py:17
  125.4 1.2 fusion.142
  127.8 0.8 fusion.85
  128.6 32.8 %all-gather.6.cloned.1.call-done = bf16[256,2304]{1,0:T(8,128)(2,1)} async-done(((bf16[16,2304]{1,0:T(8,128)(2,1)}), bf16[256,2304]{1,0:T(8,128)(2,1)}) %all-gather.6.cloned.1.call-update) | async-done | bytes 1179664 | tf_op jit(solution)/shard_map/all_gather | solution.py:90
  161.4 2.4 fusion.36
  163.8 3.0 convolution_convert_fusion.1
  166.9 1.2 add_rsqrt_fusion.1
  168.1 55.1 %reduce-scatter.6.cloned.1.call-done = bf16[16,2304]{1,0:T(8,128)(2,1)} async-done(((bf16[256,2304]{1,0:T(8,128)(2,1)}), bf16[16,2304]{1,0:T(8,128)(2,1)}) %reduce-scatter.6.cloned.1.call-update) | async-done | bytes 73744 | tf_op jit(solution)/shard_map/reduce_scatter | solution.py:100
  223.3 1.1 fusion.100
  224.3 1.1 fusion.99
  225.4 0.9 collective-permute-start.1
  226.4 6.9 %collective-permute-done.1 = bf16[16,2304]{1,0:T(8,128)(2,1)} collective-permute-done((bf16[16,2304]{1,0:T(8,128)(2,1)S(1)}, bf16[16,2304]{1,0:T(8,128)(2,1)}, u32[]{:S(2)}, u32[]{:S(2)}) %collective-permute-start.1) | collective-permute-done | bytes 73760 | tf_op jit(solution)/shard_map/ppermute | solution.py:17
  233.4 1.7 copy.105
  235.0 0.8 fusion.81
  235.9 1.2 fusion.143
  238.5 0.8 fusion.84
  239.2 31.1 %all-gather.8.cloned.1.call-done = bf16[256,2304]{1,0:T(8,128)(2,1)} async-done(((bf16[16,2304]{1,0:T(8,128)(2,1)}), bf16[256,2304]{1,0:T(8,128)(2,1)}) %all-gather.8.cloned.1.call-update) | async-done | bytes 1179664 | tf_op jit(solution)/shard_map/all_gather | solution.py:90
  270.3 2.4 fusion.39
  272.7 3.0 convolution_convert_fusion
  275.8 1.3 fusion.44
  277.1 1.1 fusion.24
  278.9 1.1 fusion.30
  280.0 0.8 copy.64
  280.8 1.8 fusion.57
  282.6 1.1 add_rsqrt_fusion
  283.7 1.1 fusion.43
  284.8 1.2 fusion.25
  286.7 1.1 fusion.31
  288.0 1.8 fusion.58
  289.8 1.2 fusion.42
  291.0 1.2 fusion.26
  292.2 1.1 fusion.32
  293.5 0.8 pad_maximum_fusion
  294.5 37.9 %reduce-scatter.8.cloned.1.call-done = bf16[16,2304]{1,0:T(8,128)(2,1)} async-done(((bf16[256,2304]{1,0:T(8,128)(2,1)}), bf16[16,2304]{1,0:T(8,128)(2,1)}) %reduce-scatter.8.cloned.1.call-update) | async-done | bytes 73744 | tf_op jit(solution)/shard_map/reduce_scatter | solution.py:100
  332.4 1.0 fusion.107
  333.5 1.0 fusion.106
  334.5 0.8 collective-permute-start.2
  336.0 6.3 %collective-permute-done.2 = bf16[16,2304]{1,0:T(8,128)(2,1)S(1)} collective-permute-done((bf16[16,2304]{1,0:T(8,128)(2,1)S(1)}, bf16[16,2304]{1,0:T(8,128)(2,1)S(1)}, u32[]{:S(2)}, u32[]{:S(2)}) %collective-permute-start.2) | collective-permute-done | bytes 73760 | tf_op jit(solution)/shard_map/ppermute | solution.py:17
  (86 shorter events, 10.1 us)
Async XLA Ops:
  7.2 44.1 %copy-start = (bf16[2,1,256,2304]{3,2,1,0:T(8,128)(2,1)S(1)}, bf16[2,1,256,2304]{3,2,1,0:T(8,128)(2,1)}, u32[]{:S(2)}) copy-start(bf16[2,1,256,2304]{3,2,1,0:T(8,128)(2,1)} %param.18) | copy-start | bytes 7077892
  7.2 44.1 %all-gather.4.cloned.1.call-start = ((), (), s32[]{:S(2)}) async-start(), calls=%async_computation.3 | async-start | bytes 1253376 | tf_op jit(solution)/shard_map/all_gather | solution.py:90
  7.9 105.5 %reduce-scatter.4.cloned.1.call-start = ((), (), s32[]{:S(2)}) async-start(), calls=%async_computation.4 | async-start | bytes 1253376 | tf_op jit(solution)/shard_map/reduce_scatter | solution.py:100
  15.7 38.0 %copy-start.24 = (f32[2,256]{1,0:T(2,128)}, f32[2,256]{1,0:T(2,128)S(1)}, u32[]{:S(2)}) copy-start(f32[2,256]{1,0:T(2,128)S(1)} %fusion.67) | copy-start | bytes 6148
  15.8 37.9 %copy-start.7 = (bf16[1,2,256,256]{2,3,1,0:T(8,128)(2,1)}, bf16[1,2,256,256]{2,3,1,0:T(8,128)(2,1)S(1)}, u32[]{:S(2)}) copy-start(bf16[1,2,256,256]{2,3,1,0:T(8,128)(2,1)S(1)} %fusion.86) | copy-start | bytes 786436
  53.7 6.9 %copy-start.19 = (bf16[2,1,2304]{2,0,1:T(2,128)(2,1)S(1)}, bf16[2,1,2304]{2,0,1:T(2,128)(2,1)}, u32[]{:S(2)}) copy-start(bf16[2,1,2304]{2,0,1:T(2,128)(2,1)} %param.19) | copy-start | bytes 27652
  53.8 59.7 %copy-start.3 = (bf16[3,16,2304]{2,1,0:T(8,128)(2,1)S(1)}, bf16[3,16,2304]{2,1,0:T(8,128)(2,1)}, u32[]{:S(2)}) copy-start(bf16[3,16,2304]{2,1,0:T(8,128)(2,1)} %param.11) | copy-start | bytes 663556
  56.8 58.3 %copy-start.15 = (bf16[16,2304]{1,0:T(8,128)(2,1)S(1)}, bf16[16,2304]{1,0:T(8,128)(2,1)}, u32[]{:S(2)}) copy-start(bf16[16,2304]{1,0:T(8,128)(2,1)} %param.10) | copy-start | bytes 221188
  56.8 67.8 %copy-start.12 = (bf16[1,256,256]{2,1,0:T(8,128)(2,1)S(1)}, bf16[1,256,256]{2,1,0:T(8,128)(2,1)}, u32[]{:S(2)}) copy-start(bf16[1,256,256]{2,1,0:T(8,128)(2,1)} %get-tuple-element.11) | copy-start | bytes 393220
  56.8 104.5 %all-gather.6.cloned.1.call-start = ((), (), s32[]{:S(2)}) async-start(), calls=%async_computation.5 | async-start | bytes 1253376 | tf_op jit(solution)/shard_map/all_gather | solution.py:90
  116.1 7.8 %collective-permute-start = (bf16[16,2304]{1,0:T(8,128)(2,1)S(1)}, bf16[16,2304]{1,0:T(8,128)(2,1)S(1)}, u32[]{:S(2)}, u32[]{:S(2)}) collective-permute-start(bf16[16,2304]{1,0:T(8,128)(2,1)S(1)} %fusion.92), channel_id=1, source_target_pairs={{0,240},{16,0},{32,16},{48,32},{64,48},{80,64},{96,80},{112,96},{1... | collective-permute-start | bytes 221192 | tf_op jit(solution)/shard_map/ppermute | solution.py:17
  123.8 0.6 copy-start.16
  124.5 98.8 %reduce-scatter.6.cloned.1.call-start = ((), (), s32[]{:S(2)}) async-start(), calls=%async_computation.6 | async-start | bytes 1253376 | tf_op jit(solution)/shard_map/reduce_scatter | solution.py:100
  126.6 0.6 copy-start.20
  127.2 0.6 copy-start.25
  166.8 103.5 %all-gather.8.cloned.1.call-start = ((), (), s32[]{:S(2)}) async-start(), calls=%async_computation.7 | async-start | bytes 1253376 | tf_op jit(solution)/shard_map/all_gather | solution.py:90
  225.4 7.9 %collective-permute-start.1 = (bf16[16,2304]{1,0:T(8,128)(2,1)S(1)}, bf16[16,2304]{1,0:T(8,128)(2,1)}, u32[]{:S(2)}, u32[]{:S(2)}) collective-permute-start(bf16[16,2304]{1,0:T(8,128)(2,1)S(1)} %fusion.99), channel_id=1, source_target_pairs={{0,240},{16,0},{32,16},{48,32},{64,48},{80,64},{96,80},{112,96},{1... | collective-permute-start | bytes 221192 | tf_op jit(solution)/shard_map/ppermute | solution.py:17
  233.3 99.1 %reduce-scatter.8.cloned.1.call-start = ((), (), s32[]{:S(2)}) async-start(), calls=%async_computation.8 | async-start | bytes 1253376 | tf_op jit(solution)/shard_map/reduce_scatter | solution.py:100
  237.1 0.8 copy-start.1
  237.1 0.8 copy-start.22
  237.9 0.6 copy-start.26
  278.2 0.7 copy-start.10
  278.9 4.8 %copy-start.8 = (bf16[1,2,256,256]{2,3,1,0:T(8,128)(2,1)S(1)}, bf16[1,2,256,256]{2,3,1,0:T(8,128)(2,1)}, u32[]{:S(2)}) copy-start(bf16[1,2,256,256]{2,3,1,0:T(8,128)(2,1)} %fusion.85) | copy-start | bytes 786436
  278.9 4.8 %copy-start.14 = (bf16[256,256]{0,1:T(8,128)(2,1)S(1)}, bf16[256,256]{0,1:T(8,128)(2,1)}, u32[]{:S(2)}) copy-start(bf16[256,256]{0,1:T(8,128)(2,1)} %fusion.36) | copy-start | bytes 393220
  278.9 5.9 %copy-start.21 = (f32[2,256]{1,0:T(2,128)S(1)}, f32[2,256]{1,0:T(2,128)}, u32[]{:S(2)}) copy-start(f32[2,256]{1,0:T(2,128)} %copy-done.20) | copy-start | bytes 6148
  284.8 3.1 copy-start.5
  286.0 0.7 copy-start.11
  286.7 3.1 copy-start.9
  286.7 4.3 %copy-start.2 = (f32[1,2,256,256]{2,3,1,0:T(8,128)S(1)}, f32[1,2,256,256]{2,3,1,0:T(8,128)}, u32[]{:S(2)}) copy-start(f32[1,2,256,256]{2,3,1,0:T(8,128)} %copy-done.1) | copy-start | bytes 1572868
  286.7 4.3 %copy-start.23 = (f32[2,256]{1,0:T(2,128)S(1)}, f32[2,256]{1,0:T(2,128)}, u32[]{:S(2)}) copy-start(f32[2,256]{1,0:T(2,128)} %copy-done.22) | copy-start | bytes 6148
  291.0 2.4 copy-start.13
  292.2 2.1 copy-start.6
  292.2 40.3 %copy-start.4 = (bf16[3,16,2304]{2,1,0:T(8,128)(2,1)S(1)}, bf16[3,16,2304]{2,1,0:T(8,128)(2,1)}, u32[]{:S(2)}) copy-start(bf16[3,16,2304]{2,1,0:T(8,128)(2,1)} %param.11) | copy-start | bytes 663556
  292.2 41.3 %copy-start.27 = (f32[16]{0:T(128)S(1)}, f32[16]{0:T(128)}, u32[]{:S(2)}) copy-start(f32[16]{0:T(128)} %add_rsqrt_fusion) | copy-start | bytes 196
  293.5 41.8 %copy-start.17 = (bf16[1,256,128]{2,1,0:T(8,128)(2,1)S(1)}, bf16[1,256,128]{2,1,0:T(8,128)(2,1)}, u32[]{:S(2)}) copy-start(bf16[1,256,128]{2,1,0:T(8,128)(2,1)} %fusion.57) | copy-start | bytes 196612
  293.5 41.8 %copy-start.18 = (bf16[1,256,128]{2,1,0:T(8,128)(2,1)S(1)}, bf16[1,256,128]{2,1,0:T(8,128)(2,1)}, u32[]{:S(2)}) copy-start(bf16[1,256,128]{2,1,0:T(8,128)(2,1)} %fusion.58) | copy-start | bytes 196612
  334.5 7.8 %collective-permute-start.2 = (bf16[16,2304]{1,0:T(8,128)(2,1)S(1)}, bf16[16,2304]{1,0:T(8,128)(2,1)S(1)}, u32[]{:S(2)}, u32[]{:S(2)}) collective-permute-start(bf16[16,2304]{1,0:T(8,128)(2,1)S(1)} %fusion.106), channel_id=1, source_target_pairs={{0,240},{16,0},{32,16},{48,32},{64,48},{80,64},{96,80},{112,96},{1... | collective-permute-start | bytes 221192 | tf_op jit(solution)/shard_map/ppermute | solution.py:17
Sparse Core Ops, SparseCore 0:
  9.8 41.4 all-gather.3
  56.9 56.4 reduce-scatter.3
  124.6 36.6 all-gather.5
  167.0 56.2 reduce-scatter.5
  233.4 36.8 all-gather.7
  275.9 56.4 reduce-scatter.7
where the time goes:
time: 351 us; the launch traced here: 350 us
  waiting for transfers between devices  265 us (75%)
  matrix products  34 us (10%)
  between operations  20.2 us (6%)
  other arithmetic  14.4 us (4%)
  local copies, waits for them, and re-layouts  13 us (4%)
    reduce_scatter x3, waiting for transfers between devices, on_device(): lax.psum_scatter(lax.dot_general(grad_value, value_weight, (((1,), (1,)),...  145 us
    all_gather x3, waiting for transfers between devices, on_device(): lax.all_gather(current, 'tensor', axis=0, tiled=True)  99.4 us
    ppermute x3, waiting for transfers between devices, passed_along(): lax.ppermute(shard, axis, [(i, (i + by) % size) for i in range(size)])  20.3 us
    dot_general x3, matrix products, on_device(): lax.dot_general(grad_value, value_weight, (((1,), (1,)), ((), ())), prefe...  9.12 us
    unnamed x60, local copies, waits for them, and re-layouts  7.59 us
    dot_general x3, matrix products, on_device(): lax.dot_general(lax.all_gather(current, 'tensor', axis=0, tiled=True), ou...  7.26 us
  transfers between devices with their start and end apart: 9, of which 9 were waited for; matrix products, arithmetic and copies ran while one was open for 9% of the time, Pallas kernels for 0%

commit v1 on v0

v1 whole, which is shorter than its diff:
```python
import jax
import jax.numpy as jnp
from jax import lax
from jax.sharding import PartitionSpec as P

HD = 128
TICKS = 3
SCALE = 144.0 ** (-0.5)
EPS = 1e-06
NEGATIVE = -1e30


def dot_t(a, b):
    return lax.dot_general(a, b, (((1,), (1,)), ((), ())), preferred_element_type=jnp.float32)


def probabilities(queries, keys, docs):
    length = queries.shape[0]
    group = queries.shape[1] // HD
    heads = queries.reshape(length, group, HD)
    position = jnp.arange(length, dtype=jnp.int32)
    allowed = (position[:, None] >= position[None, :]) & (docs[:, None] == docs[None, :])
    scores = jnp.einsum("qgd,kd->gqk", heads, keys, preferred_element_type=jnp.float32) * SCALE
    scores = jnp.where(allowed, scores, NEGATIVE)
    row_max = jnp.max(scores, axis=-1, keepdims=True)
    expsum = jnp.exp(scores - row_max)
    return expsum / jnp.sum(expsum, axis=-1, keepdims=True)


def score_grads(chance, chance_low, grad_out, queries, keys, values):
    length = queries.shape[0]
    group = queries.shape[1] // HD
    query_heads = queries.reshape(length, group, HD)
    grad_heads = grad_out.reshape(length, group, HD)
    attended = jnp.einsum("gqk,kd->gqd", chance_low, values, preferred_element_type=jnp.float32)
    row_dot = jnp.sum(jnp.transpose(grad_heads, (1, 0, 2)).astype(jnp.float32) * attended, axis=-1)
    grad_chance = jnp.einsum("qgd,kd->gqk", grad_heads, values, preferred_element_type=jnp.float32)
    grad_scores = (chance * (grad_chance - row_dot[..., None])).astype(jnp.bfloat16)
    grad_query = (
        jnp.einsum("gqk,kd->qgd", grad_scores, keys, preferred_element_type=jnp.float32) * SCALE
    ).astype(jnp.bfloat16)
    grad_key = (
        jnp.einsum("gqk,qgd->kd", grad_scores, query_heads, preferred_element_type=jnp.float32)
        * SCALE
    ).astype(jnp.bfloat16)
    return grad_query.reshape(length, -1), grad_key


def on_device(cot_in, saved_inputs, queries, keys, values, docs, plan, w_value, w_out, norm_gain):
    phases = lax.axis_size("section")
    members = lax.axis_size("tensor")
    chips = members // 2
    rows, width = cot_in.shape
    half = width // 2
    length = rows * members
    rank = lax.axis_index("tensor")
    core = rank % 2
    same_core = [[2 * z + c for z in range(chips)] for c in range(2)]
    swap_pairs = [(t, t ^ 1) for t in range(members)]
    cross_pairs = [
        (s * members + t, ((s - 1) % phases) * members + (t ^ 1))
        for s in range(phases)
        for t in range(members)
    ]

    def swap(block):
        return lax.ppermute(block, "tensor", swap_pairs)

    def back(block):
        return lax.ppermute(block, "section", [(s, (s - 1) % phases) for s in range(phases)])

    def cross(block):
        return lax.ppermute(block, ("section", "tensor"), cross_pairs)

    def halves(block, axis):
        low, high = jnp.split(block, 2, axis=axis)
        return jnp.where(core == 0, low, high), jnp.where(core == 0, high, low)

    def in_order(own, other, axis):
        return jnp.where(
            core == 0,
            jnp.concatenate([own, other], axis=axis),
            jnp.concatenate([other, own], axis=axis),
        )

    def gather(block):
        spread = jnp.broadcast_to(block[None], (chips,) + block.shape)
        found = lax.all_to_all(spread, "tensor", 0, 0, axis_index_groups=same_core)
        return found.reshape(length, half)

    value_own, value_away = halves(w_value[:, 0], 1)
    value_pair = swap(value_away)
    cot_own, cot_other = halves(cot_in, 1)
    block = in_order(cot_own, swap(cot_other), 0)
    query_list = []
    key_list = []
    for tick in range(TICKS):
        chosen = plan[tick, 0]
        out_own, out_other = halves(
            lax.dynamic_index_in_dim(w_out[:, 0], chosen, 0, keepdims=False), 1
        )
        gain_own, gain_other = halves(
            lax.dynamic_index_in_dim(norm_gain[:, 0], chosen, 0, keepdims=False).astype(jnp.float32), 0
        )
        wv_own = lax.dynamic_index_in_dim(value_own, chosen, 0, keepdims=False)
        wv_pair = lax.dynamic_index_in_dim(value_pair, chosen, 0, keepdims=False)
        input_own, input_other = halves(saved_inputs[tick].astype(jnp.float32), 1)
        square = jnp.sum(input_own * input_own, -1, keepdims=True) + jnp.sum(
            input_other * input_other, -1, keepdims=True
        )
        inverse = lax.rsqrt(square / width + EPS)
        chance = probabilities(queries[tick], keys[tick], docs[tick, 0])
        chance_low = chance.astype(jnp.bfloat16)

        whole_own = gather(block)
        whole_other = swap(whole_own)
        grad_out = (dot_t(whole_own, out_own) + dot_t(whole_other, out_other)).astype(jnp.bfloat16)
        grad_heads = grad_out.reshape(length, -1, HD)
        grad_value = jnp.einsum(
            "gqk,qgd->kd", chance_low, grad_heads, preferred_element_type=jnp.float32
        ).astype(jnp.bfloat16)
        pair_value = swap(grad_value)
        partial = (dot_t(grad_value, wv_own) + dot_t(pair_value, wv_pair)).astype(jnp.bfloat16)
        terms = lax.all_to_all(
            partial.reshape(chips, 2 * rows, half), "tensor", 0, 0, axis_index_groups=same_core
        )
        summed = jnp.sum(terms.astype(jnp.float32), axis=0)
        sum_own, sum_away = halves(summed, 0)
        sum_other = swap(sum_away)
        grad_query, grad_key = score_grads(
            chance, chance_low, grad_out, queries[tick], keys[tick], values[tick]
        )
        query_list.append(grad_query)
        key_list.append(grad_key)

        scaled_own = sum_own * gain_own
        scaled_other = sum_other * gain_other
        inner = (
            jnp.sum(scaled_own * input_own, -1, keepdims=True)
            + jnp.sum(scaled_other * input_other, -1, keepdims=True)
        ) / width
        cubed = inverse * inverse * inverse * inner
        new_own = (
            cot_own.astype(jnp.float32) + inverse * scaled_own - input_own * cubed
        ).astype(jnp.bfloat16)
        new_other = (
            cot_other.astype(jnp.float32) + inverse * scaled_other - input_other * cubed
        ).astype(jnp.bfloat16)
        cot_own = back(new_own)
        cot_other = back(new_other)
        if tick < TICKS - 1:
            block = in_order(cot_own, cross(new_other), 0)
    return (in_order(cot_own, cot_other, 1), jnp.stack(query_list), jnp.stack(key_list))


def solution(mesh):
    return jax.shard_map(
        on_device,
        mesh=mesh,
        in_specs=(
            P(("section", "tensor"), None),
            P(None, ("section", "tensor"), None),
            P(None, "section", "tensor"),
            P(None, "section", "tensor"),
            P(None, "section", "tensor"),
            P(None, "section", None),
            P(None, "section"),
            P(None, "section", None, "tensor"),
            P(None, "section", "tensor", None),
            P(None, "section", None),
        ),
        out_specs=(
            P(("section", "tensor"), None),
            P(None, "section", "tensor"),
            P(None, "section", "tensor"),
        ),
        check_vma=False,
    )
```

time: 351 us -> 214 us (0.61)
  waiting for transfers between devices: 265 us -> 129 us
  starting transfers between devices: 2.64 us -> 31.1 us
  between operations: 20.2 us -> 7.19 us
  matrix products: 34 us -> 23.1 us
    reduce_scatter x3 -> x0, waiting for transfers between devices: 145 us -> none  [on_device(): lax.psum_scatter(lax.dot_general(grad_value, value_weight, (((1,), (1,)),...]
    all_to_all x0 -> x6, waiting for transfers between devices: none -> 99.9 us  [the longest x3 55.5 us: on_device(): lax.all_to_all(partial.reshape(chips, 2 * rows, half), 'tensor', 0, 0, ax...]
    all_gather x3 -> x0, waiting for transfers between devices: 99.4 us -> none  [on_device(): lax.all_gather(current, 'tensor', axis=0, tiled=True)]
    all_to_all x0 -> x6, starting transfers between devices: none -> 26.7 us  [the longest x3 15.8 us: gather(): found = lax.all_to_all(spread, 'tensor', 0, 0, axis_index_groups=same_core)]
    dot_general x21 -> x27, matrix products: 34 us -> 18 us  [the longest x12 10 us: dot_t(): lax.dot_general(a, b, (((1,), (1,)), ((), ())), preferred_element_type=jn...]
    ppermute x3 -> x19, waiting for transfers between devices: 20.3 us -> 29.6 us  [the longest x6 24.8 us: back(): lax.ppermute(block, 'section', [(s, (s - 1) % phases) for s in range(phas...]
    unnamed x60 -> x73, local copies, waits for them, and re-layouts: 7.59 us -> 2.12 us
    sub x0 -> x3, matrix products: none -> 5.11 us  [probabilities(): expsum = jnp.exp(scores - row_max)]
  transfers between devices with their start and end apart: 9 -> 25, of which waited for: 9 -> 18; matrix products, arithmetic and copies ran while one was open for 9% -> 16% of each run, Pallas kernels for 0% -> 0%
where the time goes in v1:
time: 214 us; the launch traced here: 212 us
  waiting for transfers between devices  129 us (60%)
  starting transfers between devices  31.1 us (15%)
  matrix products  23.1 us (11%)
  other arithmetic  10.9 us (5%)
  local copies, waits for them, and re-layouts  9.99 us (5%)
  between operations  7.19 us (3%)
    all_to_all x3, waiting for transfers between devices, on_device(): lax.all_to_all(partial.reshape(chips, 2 * rows, half), 'tensor', 0, 0, ax...  55.5 us
    all_to_all x3, waiting for transfers between devices, gather(): found = lax.all_to_all(spread, 'tensor', 0, 0, axis_index_groups=same_core)  44.4 us
    ppermute x6, waiting for transfers between devices, back(): lax.ppermute(block, 'section', [(s, (s - 1) % phases) for s in range(phas...  24.8 us
    all_to_all x3, starting transfers between devices, gather(): found = lax.all_to_all(spread, 'tensor', 0, 0, axis_index_groups=same_core)  15.8 us
    all_to_all x3, starting transfers between devices, on_device(): lax.all_to_all(partial.reshape(chips, 2 * rows, half), 'tensor', 0, 0, ax...  10.9 us
    dot_general x12, matrix products, dot_t(): lax.dot_general(a, b, (((1,), (1,)), ((), ())), preferred_element_type=jn...  10 us
    sub x3, matrix products, probabilities(): expsum = jnp.exp(scores - row_max)  5.11 us
  transfers between devices with their start and end apart: 25, of which 18 were waited for; matrix products, arithmetic and copies ran while one was open for 16% of the time, Pallas kernels for 0%

profile of v1, /device:TPU:30, one launch (start us, length us, event | category | flops | bytes accessed | tf_op | source)
XLA Modules:
  0.0 211.8 jit_solution(12210954319454479509)
XLA Ops:
  0.6 0.8 broadcast_select_fusion.3
  1.6 2.1 %broadcast_select_fusion = (bf16[2,1152,128]{2,1,0:T(8,128)(2,1)}, bf16[2,1152,128]{2,1,0:T(8,128)(2,1)S(1)}) fusion(pred[]{:T(512)S(6)} %eq.28, bf16[2,2304,128]{2,1,0:T(8,128)(2,1)} %bitcast.265), kind=kLoop, calls=%fused_computation.87 | loop fusion | flops 589824 | bytes 2359297 | tf_op jit(solution)/shard_map/jit(_where)/select_n | solution.py:77
  8.7 0.9 broadcast_in_dim.24
  9.6 8.6 %all-to-all-start = ((bf16[8,32,1152]{2,1,0:T(8,128)(2,1)}), bf16[8,32,1152]{2,1,0:T(8,128)(2,1)}, u32[]{:S(2)}, u32[]{:S(2)}) async-start(bf16[8,32,1152]{2,1,0:T(8,128)(2,1)} %broadcast_in_dim.24), calls=%async_computation | async-start | bytes 1179648 | tf_op jit(solution)/shard_map/all_to_all | solution.py:88
  18.2 1.8 fusion.156
  20.0 1.7 copy.103
  23.5 0.7 fusion.92
  24.3 1.9 dynamic-slice_bitcast_fusion
  26.1 11.2 %all-to-all-done = bf16[8,32,1152]{2,1,0:T(8,128)(2,1)} async-done(((bf16[8,32,1152]{2,1,0:T(8,128)(2,1)}), bf16[8,32,1152]{2,1,0:T(8,128)(2,1)}, u32[]{:S(2)}, u32[]{:S(2)}) %all-to-all-start) | async-done | bytes 589856 | tf_op jit(solution)/shard_map/all_to_all | solution.py:88
  37.4 1.3 fusion.165
  38.7 1.6 fusion.55
  40.3 1.5 fusion.30
  43.5 1.2 fusion.3
  44.7 3.5 %all-to-all-start.1 = ((bf16[8,32,1152]{2,1,0:T(8,128)(2,1)}), bf16[8,32,1152]{2,1,0:T(8,128)(2,1)S(1)}, u32[]{:S(2)}, u32[]{:S(2)}) async-start(bf16[8,32,1152]{2,1,0:T(8,128)(2,1)} %bitcast.15), calls=%async_computation.1 | async-start | bytes 1179648 | tf_op jit(solution)/shard_map/all_to_all | solution.py:124
  48.9 0.7 bitcast_convert_fusion
  49.6 18.2 %all-to-all-done.1 = bf16[8,32,1152]{2,1,0:T(8,128)(2,1)S(1)} async-done(((bf16[8,32,1152]{2,1,0:T(8,128)(2,1)}), bf16[8,32,1152]{2,1,0:T(8,128)(2,1)S(1)}, u32[]{:S(2)}, u32[]{:S(2)}) %all-to-all-start.1) | async-done | bytes 589856 | tf_op jit(solution)/shard_map/all_to_all | solution.py:124
  68.2 1.2 collective-permute-done.4
  69.7 0.9 collective-permute-start.5
  70.6 6.6 %collective-permute-done.5 = bf16[16,1152]{1,0:T(8,128)(2,1)S(1)} collective-permute-done((bf16[16,1152]{1,0:T(8,128)(2,1)S(1)}, bf16[16,1152]{1,0:T(8,128)(2,1)S(1)}, u32[]{:S(2)}, u32[]{:S(2)}) %collective-permute-start.5) | collective-permute-done | bytes 36896 | tf_op jit(solution)/shard_map/ppermute | solution.py:70
  77.7 0.9 broadcast_in_dim.26
  78.5 3.5 %all-to-all-start.2 = ((bf16[8,32,1152]{2,1,0:T(8,128)(2,1)}), bf16[8,32,1152]{2,1,0:T(8,128)(2,1)S(1)}, u32[]{:S(2)}, u32[]{:S(2)}) async-start(bf16[8,32,1152]{2,1,0:T(8,128)(2,1)} %broadcast_in_dim.26), calls=%async_computation.2 | async-start | bytes 1179648 | tf_op jit(solution)/shard_map/all_to_all | solution.py:88
  82.3 19.2 %all-to-all-done.2 = bf16[8,32,1152]{2,1,0:T(8,128)(2,1)S(1)} async-done(((bf16[8,32,1152]{2,1,0:T(8,128)(2,1)}), bf16[8,32,1152]{2,1,0:T(8,128)(2,1)S(1)}, u32[]{:S(2)}, u32[]{:S(2)}) %all-to-all-start.2) | async-done | bytes 589856 | tf_op jit(solution)/shard_map/all_to_all | solution.py:88
  101.5 1.9 fusion.162
  103.5 1.1 fusion.94
  105.0 1.4 fusion.31
  108.1 1.2 fusion.4
  109.3 3.7 %all-to-all-start.3 = ((bf16[8,32,1152]{2,1,0:T(8,128)(2,1)}), bf16[8,32,1152]{2,1,0:T(8,128)(2,1)S(1)}, u32[]{:S(2)}, u32[]{:S(2)}) async-start(bf16[8,32,1152]{2,1,0:T(8,128)(2,1)} %bitcast.30), calls=%async_computation.3 | async-start | bytes 1179648 | tf_op jit(solution)/shard_map/all_to_all | solution.py:124
  113.2 19.4 %all-to-all-done.3 = bf16[8,32,1152]{2,1,0:T(8,128)(2,1)S(1)} async-done(((bf16[8,32,1152]{2,1,0:T(8,128)(2,1)}), bf16[8,32,1152]{2,1,0:T(8,128)(2,1)S(1)}, u32[]{:S(2)}, u32[]{:S(2)}) %all-to-all-start.3) | async-done | bytes 589856 | tf_op jit(solution)/shard_map/all_to_all | solution.py:124
  133.2 0.9 collective-permute-done.9
  134.3 6.2 %collective-permute-done.11 = bf16[16,1152]{1,0:T(8,128)(2,1)S(1)} collective-permute-done((bf16[16,1152]{1,0:T(8,128)(2,1)S(1)}, bf16[16,1152]{1,0:T(8,128)(2,1)S(1)}, u32[]{:S(2)}, u32[]{:S(2)}) %collective-permute-start.11) | collective-permute-done | bytes 36896 | tf_op jit(solution)/shard_map/ppermute | solution.py:70
  140.7 1.9 fusion.159
  142.7 5.2 %collective-permute-done.10 = bf16[16,1152]{1,0:T(8,128)(2,1)S(1)} collective-permute-done((bf16[16,1152]{1,0:T(8,128)(2,1)S(1)}, bf16[16,1152]{1,0:T(8,128)(2,1)S(1)}, u32[]{:S(2)}, u32[]{:S(2)}) %collective-permute-start.10) | collective-permute-done | bytes 36896 | tf_op jit(solution)/shard_map/ppermute | solution.py:70
  148.0 0.9 broadcast_in_dim.28
  148.9 3.7 %all-to-all-start.4 = ((bf16[8,32,1152]{2,1,0:T(8,128)(2,1)}), bf16[8,32,1152]{2,1,0:T(8,128)(2,1)S(1)}, u32[]{:S(2)}, u32[]{:S(2)}) async-start(bf16[8,32,1152]{2,1,0:T(8,128)(2,1)} %broadcast_in_dim.28), calls=%async_computation.4 | async-start | bytes 1179648 | tf_op jit(solution)/shard_map/all_to_all | solution.py:88
  152.6 1.1 fusion.95
  153.7 1.1 fusion.33
  154.8 1.1 fusion.26
  155.9 1.1 fusion.27
  157.0 0.8 copy.64
  158.0 14.0 %all-to-all-done.4 = bf16[8,32,1152]{2,1,0:T(8,128)(2,1)S(1)} async-done(((bf16[8,32,1152]{2,1,0:T(8,128)(2,1)}), bf16[8,32,1152]{2,1,0:T(8,128)(2,1)S(1)}, u32[]{:S(2)}, u32[]{:S(2)}) %all-to-all-start.4) | async-done | bytes 589856 | tf_op jit(solution)/shard_map/all_to_all | solution.py:88
  172.1 1.2 fusion.34
  173.3 1.2 fusion.25
  177.1 1.1 fusion.5
  178.3 3.7 %all-to-all-start.5 = ((bf16[8,32,1152]{2,1,0:T(8,128)(2,1)}), bf16[8,32,1152]{2,1,0:T(8,128)(2,1)S(1)}, u32[]{:S(2)}, u32[]{:S(2)}) async-start(bf16[8,32,1152]{2,1,0:T(8,128)(2,1)} %bitcast.45), calls=%async_computation.5 | async-start | bytes 1179648 | tf_op jit(solution)/shard_map/all_to_all | solution.py:124
  183.7 17.9 %all-to-all-done.5 = bf16[8,32,1152]{2,1,0:T(8,128)(2,1)S(1)} async-done(((bf16[8,32,1152]{2,1,0:T(8,128)(2,1)}), bf16[8,32,1152]{2,1,0:T(8,128)(2,1)S(1)}, u32[]{:S(2)}, u32[]{:S(2)}) %all-to-all-start.5) | async-done | bytes 589856 | tf_op jit(solution)/shard_map/all_to_all | solution.py:124
  201.8 0.8 pad_maximum_fusion
  203.5 0.7 pad_maximum_fusion.1
  204.2 6.5 %collective-permute-done.16 = bf16[16,1152]{1,0:T(8,128)(2,1)S(1)} collective-permute-done((bf16[16,1152]{1,0:T(8,128)(2,1)S(1)}, bf16[16,1152]{1,0:T(8,128)(2,1)S(1)}, u32[]{:S(2)}, u32[]{:S(2)}) %collective-permute-start.16) | collective-permute-done | bytes 36896 | tf_op jit(solution)/shard_map/ppermute | solution.py:70
  (149 shorter events, 15.0 us)
Async XLA Ops:
  1.5 7.2 %copy-start.16 = (bf16[16,1152]{1,0:T(8,128)(2,1)}, bf16[16,1152]{1,0:T(8,128)(2,1)S(1)}, u32[]{:S(2)}) copy-start(bf16[16,1152]{1,0:T(8,128)(2,1)S(1)} %get-tuple-element.53) | copy-start | bytes 110596
  1.5 7.2 %collective-permute-start = (bf16[16,1152]{1,0:T(8,128)(2,1)S(1)}, bf16[16,1152]{1,0:T(8,128)(2,1)S(1)}, u32[]{:S(2)}, u32[]{:S(2)}) collective-permute-start(bf16[16,1152]{1,0:T(8,128)(2,1)S(1)} %get-tuple-element.54), channel_id=1, source_target_pairs={{0,1},{1,0},{2,3},{3,2},{4,5},{5,4},{6,7},{7,6},{8,9},{9,8},{10,11... | collective-permute-start | bytes 110600 | tf_op jit(solution)/shard_map/ppermute | solution.py:67
  3.7 39.2 %collective-permute-start.3 = (bf16[2,1152,128]{2,1,0:T(8,128)(2,1)}, bf16[2,1152,128]{2,1,0:T(8,128)(2,1)S(1)}, u32[]{:S(2)}, u32[]{:S(2)}) collective-permute-start(bf16[2,1152,128]{2,1,0:T(8,128)(2,1)} %get-tuple-element.36), channel_id=1, source_target_pairs={{0,1},{1,0},{2,3},{3,2},{4,5},{5,4},{6,7},{7,6},{8,9},{9,8},{10,11... | collective-permute-start | bytes 1769480 | tf_op jit(solution)/shard_map/ppermute | solution.py:67
  8.7 15.6 %copy-start = (bf16[2,1,256,2304]{3,2,1,0:T(8,128)(2,1)S(1)}, bf16[2,1,256,2304]{3,2,1,0:T(8,128)(2,1)}, u32[]{:S(2)}) copy-start(bf16[2,1,256,2304]{3,2,1,0:T(8,128)(2,1)} %param.18) | copy-start | bytes 7077892
  9.6 13.9 %copy-start.31 = (s32[3,1,256]{2,1,0:T(1,128)S(1)}, s32[3,1,256]{2,1,0:T(1,128)}, u32[]{:S(2)}) copy-start(s32[3,1,256]{2,1,0:T(1,128)} %param.15) | copy-start | bytes 9220
  9.6 27.8 %all-to-all-start = ((bf16[8,32,1152]{2,1,0:T(8,128)(2,1)}), bf16[8,32,1152]{2,1,0:T(8,128)(2,1)}, u32[]{:S(2)}, u32[]{:S(2)}) async-start(bf16[8,32,1152]{2,1,0:T(8,128)(2,1)} %broadcast_in_dim.24), calls=%async_computation | async-start | bytes 1179648 | tf_op jit(solution)/shard_map/all_to_all | solution.py:88
  26.1 12.6 %copy-start.3 = (bf16[256,2304]{1,0:T(8,128)(2,1)S(1)}, bf16[256,2304]{1,0:T(8,128)(2,1)}, u32[]{:S(2)}) copy-start(bf16[256,2304]{1,0:T(8,128)(2,1)} %get-tuple-element.34) | copy-start | bytes 3538948
  37.4 3.0 %collective-permute-start.1 = (bf16[256,1152]{1,0:T(8,128)(2,1)}, bf16[256,1152]{1,0:T(8,128)(2,1)}, u32[]{:S(2)}, u32[]{:S(2)}) collective-permute-start(bf16[256,1152]{1,0:T(8,128)(2,1)} %bitcast.7), channel_id=1, source_target_pairs={{0,1},{1,0},{2,3},{3,2},{4,5},{5,4},{6,7},{7,6},{8,9},{9,8},{10,11... | collective-permute-start | bytes 1769480 | tf_op jit(solution)/shard_map/ppermute | solution.py:67
  42.0 1.5 collective-permute-start.2
  42.9 5.3 %copy-start.25 = (bf16[2,1,2304]{2,0,1:T(2,128)(2,1)S(1)}, bf16[2,1,2304]{2,0,1:T(2,128)(2,1)}, u32[]{:S(2)}) copy-start(bf16[2,1,2304]{2,0,1:T(2,128)(2,1)} %param.19) | copy-start | bytes 27652
  42.9 5.9 %copy-start.18 = (bf16[3,16,2304]{2,1,0:T(8,128)(2,1)S(1)}, bf16[3,16,2304]{2,1,0:T(8,128)(2,1)}, u32[]{:S(2)}) copy-start(bf16[3,16,2304]{2,1,0:T(8,128)(2,1)} %param.11) | copy-start | bytes 663556
  44.7 23.2 %all-to-all-start.1 = ((bf16[8,32,1152]{2,1,0:T(8,128)(2,1)}), bf16[8,32,1152]{2,1,0:T(8,128)(2,1)S(1)}, u32[]{:S(2)}, u32[]{:S(2)}) async-start(bf16[8,32,1152]{2,1,0:T(8,128)(2,1)} %bitcast.15), calls=%async_computation.1 | async-start | bytes 1179648 | tf_op jit(solution)/shard_map/all_to_all | solution.py:124
  48.2 21.3 %copy-start.17 = (bf16[16,1152]{1,0:T(8,128)(2,1)S(1)}, bf16[16,1152]{1,0:T(8,128)(2,1)}, u32[]{:S(2)}) copy-start(bf16[16,1152]{1,0:T(8,128)(2,1)} %copy-done.16) | copy-start | bytes 110596
  48.2 21.3 %copy-start.21 = (bf16[16,1152]{1,0:T(8,128)(2,1)S(1)}, bf16[16,1152]{1,0:T(8,128)(2,1)}, u32[]{:S(2)}) copy-start(bf16[16,1152]{1,0:T(8,128)(2,1)} %copy-done.20) | copy-start | bytes 110596
  68.0 1.4 collective-permute-start.4
  69.5 12.6 %copy-start.14 = (bf16[1,256,256]{2,1,0:T(8,128)(2,1)S(1)}, bf16[1,256,256]{2,1,0:T(8,128)(2,1)}, u32[]{:S(2)}) copy-start(bf16[1,256,256]{2,1,0:T(8,128)(2,1)} %get-tuple-element.39) | copy-start | bytes 393220
  69.7 7.5 %collective-permute-start.5 = (bf16[16,1152]{1,0:T(8,128)(2,1)S(1)}, bf16[16,1152]{1,0:T(8,128)(2,1)S(1)}, u32[]{:S(2)}, u32[]{:S(2)}) collective-permute-start(bf16[16,1152]{1,0:T(8,128)(2,1)S(1)} %get-tuple-element.65), channel_id=1, source_target_pairs={{0,240},{16,0},{32,16},{48,32},{64,48},{80,64},{96,80},{112,96},{1... | collective-permute-start | bytes 110600 | tf_op jit(solution)/shard_map/ppermute | solution.py:70
  70.6 7.1 %collective-permute-start.6 = (bf16[16,1152]{1,0:T(8,128)(2,1)S(1)}, bf16[16,1152]{1,0:T(8,128)(2,1)S(1)}, u32[]{:S(2)}, u32[]{:S(2)}) collective-permute-start(bf16[16,1152]{1,0:T(8,128)(2,1)S(1)} %get-tuple-element.66), channel_id=1, source_target_pairs={{0,241},{1,240},{2,243},{3,242},{4,245},{5,244},{6,247},{7,246},{8... | collective-permute-start | bytes 110600 | tf_op jit(solution)/shard_map/ppermute | solution.py:73
  78.5 23.0 %all-to-all-start.2 = ((bf16[8,32,1152]{2,1,0:T(8,128)(2,1)}), bf16[8,32,1152]{2,1,0:T(8,128)(2,1)S(1)}, u32[]{:S(2)}, u32[]{:S(2)}) async-start(bf16[8,32,1152]{2,1,0:T(8,128)(2,1)} %broadcast_in_dim.26), calls=%async_computation.2 | async-start | bytes 1179648 | tf_op jit(solution)/shard_map/all_to_all | solution.py:88
  82.1 22.5 %copy-start.2 = (bf16[256,2304]{1,0:T(8,128)(2,1)S(1)}, bf16[256,2304]{1,0:T(8,128)(2,1)}, u32[]{:S(2)}) copy-start(bf16[256,2304]{1,0:T(8,128)(2,1)} %get-tuple-element.35) | copy-start | bytes 3538948
  82.2 21.2 %copy-start.7 = (bf16[1,256,256]{1,2,0:T(8,128)(2,1)}, bf16[1,256,256]{1,2,0:T(8,128)(2,1)S(1)}, u32[]{:S(2)}) copy-start(bf16[1,256,256]{1,2,0:T(8,128)(2,1)S(1)} %copy.104) | copy-start | bytes 393220
  101.5 3.5 %collective-permute-start.7 = (bf16[256,1152]{1,0:T(8,128)(2,1)S(1)}, bf16[256,1152]{1,0:T(8,128)(2,1)}, u32[]{:S(2)}, u32[]{:S(2)}) collective-permute-start(bf16[256,1152]{1,0:T(8,128)(2,1)S(1)} %bitcast.268), channel_id=1, source_target_pairs={{0,1},{1,0},{2,3},{3,2},{4,5},{5,4},{6,7},{7,6},{8,9},{9,8},{10,11... | collective-permute-start | bytes 1769480 | tf_op jit(solution)/shard_map/ppermute | solution.py:67
  106.7 1.5 collective-permute-start.8
  107.5 5.4 %copy-start.13 = (bf16[1,256,256]{2,1,0:T(8,128)(2,1)S(1)}, bf16[1,256,256]{2,1,0:T(8,128)(2,1)}, u32[]{:S(2)}) copy-start(bf16[1,256,256]{2,1,0:T(8,128)(2,1)} %get-tuple-element.40) | copy-start | bytes 393220
  109.3 23.6 %copy-start.29 = (f32[1,1,2304]{2,0,1:T(1,128)S(1)}, f32[1,1,2304]{2,0,1:T(1,128)}, u32[]{:S(2)}) copy-start(f32[1,1,2304]{2,0,1:T(1,128)} %get-tuple-element.57) | copy-start | bytes 27652
  109.3 24.8 %copy-start.5 = (f32[16,2304]{1,0:T(8,128)S(1)}, f32[16,2304]{1,0:T(8,128)}, u32[]{:S(2)}) copy-start(f32[16,2304]{1,0:T(8,128)} %get-tuple-element.43) | copy-start | bytes 442372
  109.3 23.3 %all-to-all-start.3 = ((bf16[8,32,1152]{2,1,0:T(8,128)(2,1)}), bf16[8,32,1152]{2,1,0:T(8,128)(2,1)S(1)}, u32[]{:S(2)}, u32[]{:S(2)}) async-start(bf16[8,32,1152]{2,1,0:T(8,128)(2,1)} %bitcast.30), calls=%async_computation.3 | async-start | bytes 1179648 | tf_op jit(solution)/shard_map/all_to_all | solution.py:124
  132.7 1.4 collective-permute-start.9
  132.9 7.5 %collective-permute-start.11 = (bf16[16,1152]{1,0:T(8,128)(2,1)S(1)}, bf16[16,1152]{1,0:T(8,128)(2,1)S(1)}, u32[]{:S(2)}, u32[]{:S(2)}) collective-permute-start(bf16[16,1152]{1,0:T(8,128)(2,1)S(1)} %get-tuple-element.66), channel_id=1, source_target_pairs={{0,240},{16,0},{32,16},{48,32},{64,48},{80,64},{96,80},{112,96},{1... | collective-permute-start | bytes 110600 | tf_op jit(solution)/shard_map/ppermute | solution.py:70
  140.6 7.4 %copy-start.26 = (bf16[16,1152]{1,0:T(8,128)(2,1)}, bf16[16,1152]{1,0:T(8,128)(2,1)S(1)}, u32[]{:S(2)}) copy-start(bf16[16,1152]{1,0:T(8,128)(2,1)S(1)} %get-tuple-element.64) | copy-start | bytes 110596
  140.6 7.4 %collective-permute-start.10 = (bf16[16,1152]{1,0:T(8,128)(2,1)S(1)}, bf16[16,1152]{1,0:T(8,128)(2,1)S(1)}, u32[]{:S(2)}, u32[]{:S(2)}) collective-permute-start(bf16[16,1152]{1,0:T(8,128)(2,1)S(1)} %get-tuple-element.63), channel_id=1, source_target_pairs={{0,240},{16,0},{32,16},{48,32},{64,48},{80,64},{96,80},{112,96},{1... | collective-permute-start | bytes 110600 | tf_op jit(solution)/shard_map/ppermute | solution.py:70
  140.7 7.3 %collective-permute-start.12 = (bf16[16,1152]{1,0:T(8,128)(2,1)S(1)}, bf16[16,1152]{1,0:T(8,128)(2,1)S(1)}, u32[]{:S(2)}, u32[]{:S(2)}) collective-permute-start(bf16[16,1152]{1,0:T(8,128)(2,1)S(1)} %get-tuple-element.64), channel_id=1, source_target_pairs={{0,241},{1,240},{2,243},{3,242},{4,245},{5,244},{6,247},{7,246},{8... | collective-permute-start | bytes 110600 | tf_op jit(solution)/shard_map/ppermute | solution.py:73
  142.7 9.9 %copy-start.28 = (f32[1,1,2304]{2,0,1:T(1,128)S(1)}, f32[1,1,2304]{2,0,1:T(1,128)}, u32[]{:S(2)}) copy-start(f32[1,1,2304]{2,0,1:T(1,128)} %get-tuple-element.55) | copy-start | bytes 27652
  147.9 5.7 %copy-start.23 = (bf16[256,256]{0,1:T(8,128)(2,1)S(1)}, bf16[256,256]{0,1:T(8,128)(2,1)}, u32[]{:S(2)}) copy-start(bf16[256,256]{0,1:T(8,128)(2,1)} %copy-done.22) | copy-start | bytes 393220
  148.9 5.9 %copy-start.10 = (f32[2,256,256]{1,2,0:T(8,128)S(1)}, f32[2,256,256]{1,2,0:T(8,128)}, u32[]{:S(2)}) copy-start(f32[2,256,256]{1,2,0:T(8,128)} %copy-done.9) | copy-start | bytes 1572868
  148.9 5.9 %copy-start.33 = (f32[2,256]{1,0:T(2,128)S(1)}, f32[2,256]{1,0:T(2,128)}, u32[]{:S(2)}) copy-start(f32[2,256]{1,0:T(2,128)} %copy-done.32) | copy-start | bytes 6148
  148.9 23.2 %all-to-all-start.4 = ((bf16[8,32,1152]{2,1,0:T(8,128)(2,1)}), bf16[8,32,1152]{2,1,0:T(8,128)(2,1)S(1)}, u32[]{:S(2)}, u32[]{:S(2)}) async-start(bf16[8,32,1152]{2,1,0:T(8,128)(2,1)} %broadcast_in_dim.28), calls=%async_computation.4 | async-start | bytes 1179648 | tf_op jit(solution)/shard_map/all_to_all | solution.py:88
  155.9 17.4 %copy-start.11 = (f32[2,256,256]{1,2,0:T(8,128)S(1)}, f32[2,256,256]{1,2,0:T(8,128)}, u32[]{:S(2)}) copy-start(f32[2,256,256]{1,2,0:T(8,128)} %get-tuple-element.73) | copy-start | bytes 1572868
  172.0 3.0 %collective-permute-start.13 = (bf16[256,1152]{1,0:T(8,128)(2,1)S(1)}, bf16[256,1152]{1,0:T(8,128)(2,1)S(1)}, u32[]{:S(2)}, u32[]{:S(2)}) collective-permute-start(bf16[256,1152]{1,0:T(8,128)(2,1)S(1)} %bitcast.266), channel_id=1, source_target_pairs={{0,1},{1,0},{2,3},{3,2},{4,5},{5,4},{6,7},{7,6},{8,9},{9,8},{10,11... | collective-permute-start | bytes 1769480 | tf_op jit(solution)/shard_map/ppermute | solution.py:67
  175.7 1.5 collective-permute-start.14
  176.5 5.4 %copy-start.19 = (bf16[3,256,128]{2,1,0:T(8,128)(2,1)S(1)}, bf16[3,256,128]{2,1,0:T(8,128)(2,1)}, u32[]{:S(2)}) copy-start(bf16[3,256,128]{2,1,0:T(8,128)(2,1)} %param.13) | copy-start | bytes 589828
  178.3 23.3 %all-to-all-start.5 = ((bf16[8,32,1152]{2,1,0:T(8,128)(2,1)}), bf16[8,32,1152]{2,1,0:T(8,128)(2,1)S(1)}, u32[]{:S(2)}, u32[]{:S(2)}) async-start(bf16[8,32,1152]{2,1,0:T(8,128)(2,1)} %bitcast.45), calls=%async_computation.5 | async-start | bytes 1179648 | tf_op jit(solution)/shard_map/all_to_all | solution.py:124
  182.5 20.7 %collective-permute-start.17 = (bf16[16,1152]{1,0:T(8,128)(2,1)S(1)}, bf16[16,1152]{1,0:T(8,128)(2,1)S(1)}, u32[]{:S(2)}, u32[]{:S(2)}) collective-permute-start(bf16[16,1152]{1,0:T(8,128)(2,1)S(1)} %copy-done.27), channel_id=1, source_target_pairs={{0,240},{16,0},{32,16},{48,32},{64,48},{80,64},{96,80},{112,96},{1... | collective-permute-start | bytes 110600 | tf_op jit(solution)/shard_map/ppermute | solution.py:70
  183.1 18.7 %copy-start.15 = (bf16[1,256,256]{2,1,0:T(8,128)(2,1)S(1)}, bf16[1,256,256]{2,1,0:T(8,128)(2,1)}, u32[]{:S(2)}) copy-start(bf16[1,256,256]{2,1,0:T(8,128)(2,1)} %copy.64) | copy-start | bytes 393220
  183.4 19.7 %copy-start.4 = (f32[16,2304]{1,0:T(8,128)S(1)}, f32[16,2304]{1,0:T(8,128)}, u32[]{:S(2)}) copy-start(f32[16,2304]{1,0:T(8,128)} %get-tuple-element.41) | copy-start | bytes 442372
  201.7 1.4 collective-permute-start.15
  203.4 7.4 %collective-permute-start.16 = (bf16[16,1152]{1,0:T(8,128)(2,1)S(1)}, bf16[16,1152]{1,0:T(8,128)(2,1)S(1)}, u32[]{:S(2)}, u32[]{:S(2)}) collective-permute-start(bf16[16,1152]{1,0:T(8,128)(2,1)S(1)} %get-tuple-element.61), channel_id=1, source_target_pairs={{0,240},{16,0},{32,16},{48,32},{64,48},{80,64},{96,80},{112,96},{1... | collective-permute-start | bytes 110600 | tf_op jit(solution)/shard_map/ppermute | solution.py:70
  203.5 7.7 %collective-permute-start.18 = (bf16[16,1152]{1,0:T(8,128)(2,1)S(1)}, bf16[16,1152]{1,0:T(8,128)(2,1)S(1)}, u32[]{:S(2)}, u32[]{:S(2)}) collective-permute-start(bf16[16,1152]{1,0:T(8,128)(2,1)S(1)} %get-tuple-element.62), channel_id=1, source_target_pairs={{0,240},{16,0},{32,16},{48,32},{64,48},{80,64},{96,80},{112,96},{1... | collective-permute-start | bytes 110600 | tf_op jit(solution)/shard_map/ppermute | solution.py:70
  (12 other events, 33.7 us)

commit v2 on v1

v2 whole, which is shorter than its diff:
```python
import jax
import jax.numpy as jnp
from jax import lax
from jax.sharding import PartitionSpec as P

HD = 128
TICKS = 3
SCALE = 144.0 ** (-0.5)
EPS = 1e-06
NEGATIVE = -1e30


def dot_t(a, b):
    return lax.dot_general(a, b, (((1,), (1,)), ((), ())), preferred_element_type=jnp.float32)


def probabilities(queries, keys, docs):
    length = queries.shape[0]
    group = queries.shape[1] // HD
    heads = queries.reshape(length, group, HD)
    position = jnp.arange(length, dtype=jnp.int32)
    allowed = (position[:, None] >= position[None, :]) & (docs[:, None] == docs[None, :])
    scores = jnp.einsum("qgd,kd->gqk", heads, keys, preferred_element_type=jnp.float32) * SCALE
    scores = jnp.where(allowed, scores, NEGATIVE)
    row_max = jnp.max(scores, axis=-1, keepdims=True)
    expsum = jnp.exp(scores - row_max)
    return expsum / jnp.sum(expsum, axis=-1, keepdims=True)


def score_grads(chance, chance_low, grad_out, queries, keys, values):
    length = queries.shape[0]
    group = queries.shape[1] // HD
    query_heads = queries.reshape(length, group, HD)
    grad_heads = grad_out.reshape(length, group, HD)
    attended = jnp.einsum("gqk,kd->gqd", chance_low, values, preferred_element_type=jnp.float32)
    row_dot = jnp.sum(jnp.transpose(grad_heads, (1, 0, 2)).astype(jnp.float32) * attended, axis=-1)
    grad_chance = jnp.einsum("qgd,kd->gqk", grad_heads, values, preferred_element_type=jnp.float32)
    grad_scores = (chance * (grad_chance - row_dot[..., None])).astype(jnp.bfloat16)
    grad_query = (
        jnp.einsum("gqk,kd->qgd", grad_scores, keys, preferred_element_type=jnp.float32) * SCALE
    ).astype(jnp.bfloat16)
    grad_key = (
        jnp.einsum("gqk,qgd->kd", grad_scores, query_heads, preferred_element_type=jnp.float32)
        * SCALE
    ).astype(jnp.bfloat16)
    return grad_query.reshape(length, -1), grad_key


def on_device(cot_in, saved_inputs, queries, keys, values, docs, plan, w_value, w_out, norm_gain):
    phases = lax.axis_size("section")
    members = lax.axis_size("tensor")
    rows, width = cot_in.shape
    half = width // 2
    length = rows * members
    core = lax.axis_index("tensor") % 2
    swap_pairs = [(t, t ^ 1) for t in range(members)]
    back_pairs = [(s, (s - 1) % phases) for s in range(phases)]

    def swap(block):
        return lax.ppermute(block, "tensor", swap_pairs)

    def halves(block, axis):
        low, high = jnp.split(block, 2, axis=axis)
        return jnp.where(core == 0, low, high), jnp.where(core == 0, high, low)

    def gather(block):
        both = jnp.stack(jnp.split(block, 2, axis=1))
        spread = jnp.broadcast_to(both[None], (members // 2,) + both.shape)
        found = lax.all_to_all(spread.reshape(members, rows, half), "tensor", 0, 0)
        return found.reshape(length, half)

    def scatter(partial):
        terms = lax.all_to_all(partial.reshape(members, rows, half), "tensor", 0, 0)
        terms = terms.reshape(members // 2, 2, rows, half).astype(jnp.float32)
        low, high = jnp.sum(terms[:, 0], axis=0), jnp.sum(terms[:, 1], axis=0)
        return jnp.concatenate([low, high], axis=1)

    current = cot_in
    value_own, value_away = halves(w_value[:, 0], 1)
    value_pair = swap(value_away)
    query_list = []
    key_list = []
    for tick in range(TICKS):
        chosen = plan[tick, 0]
        out_own, out_other = halves(
            lax.dynamic_index_in_dim(w_out[:, 0], chosen, 0, keepdims=False), 1
        )
        gain_row = lax.dynamic_index_in_dim(norm_gain[:, 0], chosen, 0, keepdims=False)
        wv_own = lax.dynamic_index_in_dim(value_own, chosen, 0, keepdims=False)
        wv_pair = lax.dynamic_index_in_dim(value_pair, chosen, 0, keepdims=False)
        inputs = saved_inputs[tick].astype(jnp.float32)
        inverse = lax.rsqrt(jnp.mean(inputs * inputs, -1, keepdims=True) + EPS)
        chance = probabilities(queries[tick], keys[tick], docs[tick, 0])
        chance_low = chance.astype(jnp.bfloat16)

        whole_own = gather(current)
        whole_other = swap(whole_own)
        grad_out = (dot_t(whole_own, out_own) + dot_t(whole_other, out_other)).astype(jnp.bfloat16)
        grad_heads = grad_out.reshape(length, -1, HD)
        grad_value = jnp.einsum(
            "gqk,qgd->kd", chance_low, grad_heads, preferred_element_type=jnp.float32
        ).astype(jnp.bfloat16)
        pair_value = swap(grad_value)
        partial = (dot_t(grad_value, wv_own) + dot_t(pair_value, wv_pair)).astype(jnp.bfloat16)
        summed = scatter(partial)
        grad_query, grad_key = score_grads(
            chance, chance_low, grad_out, queries[tick], keys[tick], values[tick]
        )
        query_list.append(grad_query)
        key_list.append(grad_key)

        scaled = summed * gain_row.astype(jnp.float32)
        inner = jnp.mean(scaled * inputs, -1, keepdims=True)
        updated = (
            current.astype(jnp.float32)
            + inverse * scaled
            - inputs * (inverse * inverse * inverse * inner)
        ).astype(jnp.bfloat16)
        current = lax.ppermute(updated, "section", back_pairs)
    return (current, jnp.stack(query_list), jnp.stack(key_list))


def solution(mesh):
    return jax.shard_map(
        on_device,
        mesh=mesh,
        in_specs=(
            P(("section", "tensor"), None),
            P(None, ("section", "tensor"), None),
            P(None, "section", "tensor"),
            P(None, "section", "tensor"),
            P(None, "section", "tensor"),
            P(None, "section", None),
            P(None, "section"),
            P(None, "section", None, "tensor"),
            P(None, "section", "tensor", None),
            P(None, "section", None),
        ),
        out_specs=(
            P(("section", "tensor"), None),
            P(None, "section", "tensor"),
            P(None, "section", "tensor"),
        ),
        check_vma=False,
    )
```

time: 214 us -> 195 us (0.911)
  waiting for transfers between devices: 129 us -> 84.7 us
  blocking collectives: 0 us -> 21.6 us
  local copies, waits for them, and re-layouts: 9.99 us -> 14.1 us
    all_to_all x6 -> x5, waiting for transfers between devices: 99.9 us -> 60.6 us  [the longest x2 31.4 us: scatter(): terms = lax.all_to_all(partial.reshape(members, rows, half), 'tensor', 0, 0)]
    all_to_all x0 -> x1, blocking collectives: none -> 21.6 us  [scatter(): terms = lax.all_to_all(partial.reshape(members, rows, half), 'tensor', 0, 0)]
    ppermute x8 -> x3, waiting for transfers between devices: 25.3 us -> 21.5 us  [on_device(): current = lax.ppermute(updated, 'section', back_pairs)]
    ppermute x11 -> x7, starting transfers between devices: 2.8 us -> 6.05 us  [swap(): return lax.ppermute(block, 'tensor', swap_pairs)]
    unnamed x73 -> x82, local copies, waits for them, and re-layouts: 2.12 us -> 4.9 us
    all_to_all x6 -> x5, starting transfers between devices: 26.7 us -> 25.1 us  [the longest x3 17.3 us: gather(): found = lax.all_to_all(spread.reshape(members, rows, half), 'tensor', 0, 0)]
  transfers between devices with their start and end apart: 25 -> 15, of which waited for: 18 -> 11; matrix products, arithmetic and copies ran while one was open for 16% -> 17% of each run, Pallas kernels for 0% -> 0%
where the time goes in v2:
time: 195 us; the launch traced here: 193 us
  waiting for transfers between devices  84.7 us (43%)
  starting transfers between devices  32.3 us (17%)
  matrix products  23.5 us (12%)
  blocking collectives  21.6 us (11%)
  local copies, waits for them, and re-layouts  14.1 us (7%)
  other arithmetic  8.83 us (5%)
  between operations  7.39 us (4%)
    all_to_all x2, waiting for transfers between devices, scatter(): terms = lax.all_to_all(partial.reshape(members, rows, half), 'tensor', 0, 0)  31.4 us
    all_to_all x3, waiting for transfers between devices, gather(): found = lax.all_to_all(spread.reshape(members, rows, half), 'tensor', 0, 0)  29.1 us
    all_to_all x1, blocking collectives, scatter(): terms = lax.all_to_all(partial.reshape(members, rows, half), 'tensor', 0, 0)  21.6 us
    ppermute x3, waiting for transfers between devices, on_device(): current = lax.ppermute(updated, 'section', back_pairs)  21.5 us
    all_to_all x3, starting transfers between devices, gather(): found = lax.all_to_all(spread.reshape(members, rows, half), 'tensor', 0, 0)  17.3 us
    dot_general x12, matrix products, dot_t(): lax.dot_general(a, b, (((1,), (1,)), ((), ())), preferred_element_type=jn...  11.4 us
    all_to_all x2, starting transfers between devices, scatter(): terms = lax.all_to_all(partial.reshape(members, rows, half), 'tensor', 0, 0)  7.82 us
    ppermute x7, starting transfers between devices, swap(): return lax.ppermute(block, 'tensor', swap_pairs)  6.05 us
  transfers between devices with their start and end apart: 15, of which 11 were waited for; matrix products, arithmetic and copies ran while one was open for 17% of the time, Pallas kernels for 0%

profile of v2, /device:TPU:30, one launch (start us, length us, event | category | flops | bytes accessed | tf_op | source)
XLA Modules:
  0.0 192.5 jit_solution(3479409749463895287)
XLA Ops:
  0.6 0.8 slice_bitcast_fusion.5
  1.4 0.9 broadcast_in_dim.24
  2.3 8.6 %all-to-all-start = ((bf16[16,16,1152]{2,1,0:T(8,128)(2,1)}), bf16[16,16,1152]{2,1,0:T(8,128)(2,1)}, u32[]{:S(2)}, u32[]{:S(2)}) async-start(bf16[16,16,1152]{2,1,0:T(8,128)(2,1)} %bitcast.8), calls=%async_computation | async-start | bytes 1179648 | tf_op jit(solution)/shard_map/all_to_all | solution.py:69
  11.0 2.3 %broadcast_select_fusion = (bf16[2,1152,128]{2,1,0:T(8,128)(2,1)}, bf16[2,1152,128]{2,1,0:T(8,128)(2,1)S(1)}) fusion(pred[]{:T(512)S(6)} %eq.61, bf16[2,2304,128]{2,1,0:T(8,128)(2,1)} %bitcast.296), kind=kLoop, calls=%fused_computation.90 | loop fusion | flops 589824 | bytes 2359297 | tf_op jit(solution)/shard_map/jit(_where)/select_n | solution.py:64
  18.2 1.8 fusion.162
  20.0 1.7 copy.103
  25.0 1.9 dynamic-slice_bitcast_fusion
  26.8 1.4 all-to-all-done
  28.2 1.9 collective-permute-start
  30.1 1.2 fusion.165
  31.4 1.6 fusion.55
  33.0 1.4 fusion.30
  35.1 0.9 collective-permute-done.1
  36.0 1.2 fusion.3
  37.2 4.1 %all-to-all-start.1 = ((bf16[16,16,1152]{2,1,0:T(8,128)(2,1)}), bf16[16,16,1152]{2,1,0:T(8,128)(2,1)S(1)}, u32[]{:S(2)}, u32[]{:S(2)}) async-start(bf16[16,16,1152]{2,1,0:T(8,128)(2,1)} %bitcast.17), calls=%async_computation.1 | async-start | bytes 1179648 | tf_op jit(solution)/shard_map/all_to_all | solution.py:73
  41.4 17.1 %all-to-all-done.1 = bf16[16,16,1152]{2,1,0:T(8,128)(2,1)S(1)} async-done(((bf16[16,16,1152]{2,1,0:T(8,128)(2,1)}), bf16[16,16,1152]{2,1,0:T(8,128)(2,1)S(1)}, u32[]{:S(2)}, u32[]{:S(2)}) %all-to-all-start.1) | async-done | bytes 589856 | tf_op jit(solution)/shard_map/all_to_all | solution.py:73
  59.6 0.9 collective-permute-start.3
  60.5 6.8 %collective-permute-done.3 = bf16[16,2304]{1,0:T(8,128)(2,1)S(1)} collective-permute-done((bf16[16,2304]{1,0:T(8,128)(2,1)S(1)}, bf16[16,2304]{1,0:T(8,128)(2,1)S(1)}, u32[]{:S(2)}, u32[]{:S(2)}) %collective-permute-start.3) | collective-permute-done | bytes 73760 | tf_op jit(solution)/shard_map/ppermute | solution.py:119
  67.4 0.9 broadcast_in_dim.26
  68.2 4.5 %all-to-all-start.2 = ((bf16[16,16,1152]{2,1,0:T(8,128)(2,1)}), bf16[16,16,1152]{2,1,0:T(8,128)(2,1)}, u32[]{:S(2)}, u32[]{:S(2)}) async-start(bf16[16,16,1152]{2,1,0:T(8,128)(2,1)} %bitcast.29), calls=%async_computation.2 | async-start | bytes 1179648 | tf_op jit(solution)/shard_map/all_to_all | solution.py:69
  73.0 17.0 %all-to-all-done.2 = bf16[16,16,1152]{2,1,0:T(8,128)(2,1)} async-done(((bf16[16,16,1152]{2,1,0:T(8,128)(2,1)}), bf16[16,16,1152]{2,1,0:T(8,128)(2,1)}, u32[]{:S(2)}, u32[]{:S(2)}) %all-to-all-start.2) | async-done | bytes 589856 | tf_op jit(solution)/shard_map/all_to_all | solution.py:69
  90.0 1.9 collective-permute-start.4
  91.8 2.0 %fusion.168 = (f32[2,256]{1,0:T(2,128)S(1)}, f32[2,256,256]{1,2,0:T(8,128)}) fusion(bf16[256,2,128]{0,2,1:T(8,128)(2,1)S(1)} %bitcast.299, pred[256,256]{0,1:T(8,128)(4,1)S(1)} %fusion.91, bf16[3,256,128]{2,1,0:T(8,128)(2,1)} %param.13), kind=kOutput, calls=%fused_computation.228 | convolution fusion | flops 34078976 | bytes 788480 | tf_op jit(solution)/shard_map/sub | solution.py:26
  93.8 1.1 fusion.94
  94.9 1.5 fusion.52
  96.4 1.5 fusion.31
  98.5 0.9 collective-permute-done.5
  99.7 21.6 %all_to_all.30 = bf16[16,16,1152]{2,1,0:T(8,128)(2,1)S(1)} all-to-all(bf16[16,16,1152]{2,1,0:T(8,128)(2,1)S(1)} %bitcast.295), channel_id=1, replica_groups=mesh['section'=16,'tensor'=16] {'tensor'}, dimensions={0} | all-to-all | bytes 1179648 | tf_op jit(solution)/shard_map/all_to_all | solution.py:73
  122.8 7.7 %collective-permute-done.6 = bf16[16,2304]{1,0:T(8,128)(2,1)S(1)} collective-permute-done((bf16[16,2304]{1,0:T(8,128)(2,1)S(1)}, bf16[16,2304]{1,0:T(8,128)(2,1)S(1)}, u32[]{:S(2)}, u32[]{:S(2)}) %collective-permute-start.6) | collective-permute-done | bytes 73760 | tf_op jit(solution)/shard_map/ppermute | solution.py:119
  130.5 0.9 broadcast_in_dim.28
  131.3 4.2 %all-to-all-start.4 = ((bf16[16,16,1152]{2,1,0:T(8,128)(2,1)}), bf16[16,16,1152]{2,1,0:T(8,128)(2,1)}, u32[]{:S(2)}, u32[]{:S(2)}) async-start(bf16[16,16,1152]{2,1,0:T(8,128)(2,1)} %bitcast.49), calls=%async_computation.4 | async-start | bytes 1179648 | tf_op jit(solution)/shard_map/all_to_all | solution.py:69
  135.6 1.1 fusion.171
  136.7 1.1 fusion.95
  137.9 1.2 fusion.33
  139.1 1.1 fusion.26
  140.4 0.8 copy.64
  141.2 0.9 fusion.45
  142.0 10.8 %all-to-all-done.4 = bf16[16,16,1152]{2,1,0:T(8,128)(2,1)} async-done(((bf16[16,16,1152]{2,1,0:T(8,128)(2,1)}), bf16[16,16,1152]{2,1,0:T(8,128)(2,1)}, u32[]{:S(2)}, u32[]{:S(2)}) %all-to-all-start.4) | async-done | bytes 589856 | tf_op jit(solution)/shard_map/all_to_all | solution.py:69
  152.8 1.8 collective-permute-start.7
  154.6 1.1 fusion.34
  155.7 1.4 fusion.25
  157.2 1.4 fusion.49
  160.1 0.9 collective-permute-done.8
  161.0 1.1 fusion.5
  162.1 3.7 %all-to-all-start.5 = ((bf16[16,16,1152]{2,1,0:T(8,128)(2,1)}), bf16[16,16,1152]{2,1,0:T(8,128)(2,1)S(1)}, u32[]{:S(2)}, u32[]{:S(2)}) async-start(bf16[16,16,1152]{2,1,0:T(8,128)(2,1)} %bitcast.57), calls=%async_computation.5 | async-start | bytes 1179648 | tf_op jit(solution)/shard_map/all_to_all | solution.py:73
  167.7 0.8 pad_maximum_fusion
  168.7 14.3 %all-to-all-done.5 = bf16[16,16,1152]{2,1,0:T(8,128)(2,1)S(1)} async-done(((bf16[16,16,1152]{2,1,0:T(8,128)(2,1)}), bf16[16,16,1152]{2,1,0:T(8,128)(2,1)S(1)}, u32[]{:S(2)}, u32[]{:S(2)}) %all-to-all-start.5) | async-done | bytes 589856 | tf_op jit(solution)/shard_map/all_to_all | solution.py:73
  184.9 6.9 %collective-permute-done.9 = bf16[16,2304]{1,0:T(8,128)(2,1)S(1)} collective-permute-done((bf16[16,2304]{1,0:T(8,128)(2,1)S(1)}, bf16[16,2304]{1,0:T(8,128)(2,1)S(1)}, u32[]{:S(2)}, u32[]{:S(2)}) %collective-permute-start.9) | collective-permute-done | bytes 73760 | tf_op jit(solution)/shard_map/ppermute | solution.py:119
  (136 shorter events, 12.9 us)
Async XLA Ops:
  2.3 25.9 %all-to-all-start = ((bf16[16,16,1152]{2,1,0:T(8,128)(2,1)}), bf16[16,16,1152]{2,1,0:T(8,128)(2,1)}, u32[]{:S(2)}, u32[]{:S(2)}) async-start(bf16[16,16,1152]{2,1,0:T(8,128)(2,1)} %bitcast.8), calls=%async_computation | async-start | bytes 1179648 | tf_op jit(solution)/shard_map/all_to_all | solution.py:69
  10.9 2.7 %copy-start.35 = (s32[3,1]{0,1:T(1,128)S(1)}, s32[3,1]{0,1:T(1,128)}, u32[]{:S(2)}) copy-start(s32[3,1]{0,1:T(1,128)} %param.16) | copy-start | bytes 40
  10.9 12.7 %copy-start.36 = (s32[3,1,256]{2,1,0:T(1,128)S(1)}, s32[3,1,256]{2,1,0:T(1,128)}, u32[]{:S(2)}) copy-start(s32[3,1,256]{2,1,0:T(1,128)} %param.15) | copy-start | bytes 9220
  11.0 14.0 %copy-start = (bf16[2,1,256,2304]{3,2,1,0:T(8,128)(2,1)S(1)}, bf16[2,1,256,2304]{3,2,1,0:T(8,128)(2,1)}, u32[]{:S(2)}) copy-start(bf16[2,1,256,2304]{3,2,1,0:T(8,128)(2,1)} %param.18) | copy-start | bytes 7077892
  13.3 21.9 %collective-permute-start.2 = (bf16[2,1152,128]{2,1,0:T(8,128)(2,1)}, bf16[2,1152,128]{2,1,0:T(8,128)(2,1)S(1)}, u32[]{:S(2)}, u32[]{:S(2)}) collective-permute-start(bf16[2,1152,128]{2,1,0:T(8,128)(2,1)} %get-tuple-element.19), channel_id=1, source_target_pairs={{0,1},{1,0},{2,3},{3,2},{4,5},{5,4},{6,7},{7,6},{8,9},{9,8},{10,11... | collective-permute-start | bytes 1769480 | tf_op jit(solution)/shard_map/ppermute | solution.py:60
  26.8 4.6 %copy-start.4 = (bf16[256,2304]{1,0:T(8,128)(2,1)S(1)}, bf16[256,2304]{1,0:T(8,128)(2,1)}, u32[]{:S(2)}) copy-start(bf16[256,2304]{1,0:T(8,128)(2,1)} %get-tuple-element.17) | copy-start | bytes 3538948
  28.2 4.8 %collective-permute-start = (bf16[256,1152]{1,0:T(8,128)(2,1)}, bf16[256,1152]{1,0:T(8,128)(2,1)}, u32[]{:S(2)}, u32[]{:S(2)}) collective-permute-start(bf16[256,1152]{1,0:T(8,128)(2,1)} %bitcast.9), channel_id=1, source_target_pairs={{0,1},{1,0},{2,3},{3,2},{4,5},{5,4},{6,7},{7,6},{8,9},{9,8},{10,11... | collective-permute-start | bytes 1769480 | tf_op jit(solution)/shard_map/ppermute | solution.py:60
  31.3 1.7 copy-start.12
  34.4 2.7 %copy-start.26 = (bf16[256,256]{0,1:T(8,128)(2,1)}, bf16[256,256]{0,1:T(8,128)(2,1)S(1)}, u32[]{:S(2)}) copy-start(bf16[256,256]{0,1:T(8,128)(2,1)S(1)} %fusion.30) | copy-start | bytes 393220
  34.7 1.3 collective-permute-start.1
  35.1 6.2 %copy-start.33 = (bf16[2,1,2304]{2,0,1:T(2,128)(2,1)S(1)}, bf16[2,1,2304]{2,0,1:T(2,128)(2,1)}, u32[]{:S(2)}) copy-start(bf16[2,1,2304]{2,0,1:T(2,128)(2,1)} %param.19) | copy-start | bytes 27652
  37.2 21.3 %all-to-all-start.1 = ((bf16[16,16,1152]{2,1,0:T(8,128)(2,1)}), bf16[16,16,1152]{2,1,0:T(8,128)(2,1)S(1)}, u32[]{:S(2)}, u32[]{:S(2)}) async-start(bf16[16,16,1152]{2,1,0:T(8,128)(2,1)} %bitcast.17), calls=%async_computation.1 | async-start | bytes 1179648 | tf_op jit(solution)/shard_map/all_to_all | solution.py:73
  41.4 17.3 %copy-start.1 = (bf16[3,16,2304]{2,1,0:T(8,128)(2,1)S(1)}, bf16[3,16,2304]{2,1,0:T(8,128)(2,1)}, u32[]{:S(2)}) copy-start(bf16[3,16,2304]{2,1,0:T(8,128)(2,1)} %param.11) | copy-start | bytes 663556
  59.5 13.2 %copy-start.16 = (bf16[1,256,256]{2,1,0:T(8,128)(2,1)S(1)}, bf16[1,256,256]{2,1,0:T(8,128)(2,1)}, u32[]{:S(2)}) copy-start(bf16[1,256,256]{2,1,0:T(8,128)(2,1)} %get-tuple-element.22) | copy-start | bytes 393220
  59.6 13.3 %copy-start.34 = (s32[1,1,256]{2,1,0:T(1,128)S(1)}, s32[1,1,256]{2,1,0:T(1,128)}, u32[]{:S(2)}) copy-start(s32[1,1,256]{2,1,0:T(1,128)} %get-tuple-element.32) | copy-start | bytes 3076
  59.6 7.8 %collective-permute-start.3 = (bf16[16,2304]{1,0:T(8,128)(2,1)S(1)}, bf16[16,2304]{1,0:T(8,128)(2,1)S(1)}, u32[]{:S(2)}, u32[]{:S(2)}) collective-permute-start(bf16[16,2304]{1,0:T(8,128)(2,1)S(1)} %fusion.99), channel_id=1, source_target_pairs={{0,240},{16,0},{32,16},{48,32},{64,48},{80,64},{96,80},{112,96},{1... | collective-permute-start | bytes 221192 | tf_op jit(solution)/shard_map/ppermute | solution.py:119
  67.4 5.5 %copy-start.21 = (bf16[16,2304]{1,0:T(8,128)(2,1)}, bf16[16,2304]{1,0:T(8,128)(2,1)S(1)}, u32[]{:S(2)}) copy-start(bf16[16,2304]{1,0:T(8,128)(2,1)S(1)} %collective-permute-done.3) | copy-start | bytes 221188
  68.2 21.7 %all-to-all-start.2 = ((bf16[16,16,1152]{2,1,0:T(8,128)(2,1)}), bf16[16,16,1152]{2,1,0:T(8,128)(2,1)}, u32[]{:S(2)}, u32[]{:S(2)}) async-start(bf16[16,16,1152]{2,1,0:T(8,128)(2,1)} %bitcast.29), calls=%async_computation.2 | async-start | bytes 1179648 | tf_op jit(solution)/shard_map/all_to_all | solution.py:69
  72.7 22.2 %copy-start.3 = (bf16[256,2304]{1,0:T(8,128)(2,1)S(1)}, bf16[256,2304]{1,0:T(8,128)(2,1)}, u32[]{:S(2)}) copy-start(bf16[256,2304]{1,0:T(8,128)(2,1)} %get-tuple-element.18) | copy-start | bytes 3538948
  72.8 20.9 %copy-start.8 = (bf16[1,256,256]{1,2,0:T(8,128)(2,1)}, bf16[1,256,256]{1,2,0:T(8,128)(2,1)S(1)}, u32[]{:S(2)}) copy-start(bf16[1,256,256]{1,2,0:T(8,128)(2,1)S(1)} %copy.104) | copy-start | bytes 393220
  90.0 6.4 %collective-permute-start.4 = (bf16[256,1152]{1,0:T(8,128)(2,1)}, bf16[256,1152]{1,0:T(8,128)(2,1)}, u32[]{:S(2)}, u32[]{:S(2)}) collective-permute-start(bf16[256,1152]{1,0:T(8,128)(2,1)} %bitcast.30), channel_id=1, source_target_pairs={{0,1},{1,0},{2,3},{3,2},{4,5},{5,4},{6,7},{7,6},{8,9},{9,8},{10,11... | collective-permute-start | bytes 1769480 | tf_op jit(solution)/shard_map/ppermute | solution.py:60
  97.8 1.9 copy-start.29
  98.1 1.3 collective-permute-start.5
  121.5 1.2 copy-start.15
  122.4 8.0 %collective-permute-start.6 = (bf16[16,2304]{1,0:T(8,128)(2,1)S(1)}, bf16[16,2304]{1,0:T(8,128)(2,1)S(1)}, u32[]{:S(2)}, u32[]{:S(2)}) collective-permute-start(bf16[16,2304]{1,0:T(8,128)(2,1)S(1)} %fusion.103), channel_id=1, source_target_pairs={{0,240},{16,0},{32,16},{48,32},{64,48},{80,64},{96,80},{112,96},{1... | collective-permute-start | bytes 221192 | tf_op jit(solution)/shard_map/ppermute | solution.py:119
  122.6 13.0 %copy-start.24 = (bf16[3,256,128]{2,1,0:T(8,128)(2,1)S(1)}, bf16[3,256,128]{2,1,0:T(8,128)(2,1)}, u32[]{:S(2)}) copy-start(bf16[3,256,128]{2,1,0:T(8,128)(2,1)} %param.13) | copy-start | bytes 589828
  122.8 14.0 %copy-start.10 = (bf16[1,256,256]{1,2,0:T(8,128)(2,1)}, bf16[1,256,256]{1,2,0:T(8,128)(2,1)S(1)}, u32[]{:S(2)}) copy-start(bf16[1,256,256]{1,2,0:T(8,128)(2,1)S(1)} %copy.105) | copy-start | bytes 393220
  130.4 6.3 %copy-start.19 = (bf16[16,2304]{1,0:T(8,128)(2,1)}, bf16[16,2304]{1,0:T(8,128)(2,1)S(1)}, u32[]{:S(2)}) copy-start(bf16[16,2304]{1,0:T(8,128)(2,1)S(1)} %collective-permute-done.6) | copy-start | bytes 221188
  131.3 21.4 %all-to-all-start.4 = ((bf16[16,16,1152]{2,1,0:T(8,128)(2,1)}), bf16[16,16,1152]{2,1,0:T(8,128)(2,1)}, u32[]{:S(2)}, u32[]{:S(2)}) async-start(bf16[16,16,1152]{2,1,0:T(8,128)(2,1)} %bitcast.49), calls=%async_computation.4 | async-start | bytes 1179648 | tf_op jit(solution)/shard_map/all_to_all | solution.py:69
  135.6 2.3 %copy-start.27 = (bf16[256,256]{0,1:T(8,128)(2,1)S(1)}, bf16[256,256]{0,1:T(8,128)(2,1)}, u32[]{:S(2)}) copy-start(bf16[256,256]{0,1:T(8,128)(2,1)} %copy-done.26) | copy-start | bytes 393220
  135.6 3.4 %copy-start.13 = (f32[2,256,256]{1,2,0:T(8,128)S(1)}, f32[2,256,256]{1,2,0:T(8,128)}, u32[]{:S(2)}) copy-start(f32[2,256,256]{1,2,0:T(8,128)} %copy-done.12) | copy-start | bytes 1572868
  136.7 2.3 %copy-start.28 = (bf16[256,256]{0,1:T(8,128)(2,1)S(1)}, bf16[256,256]{0,1:T(8,128)(2,1)}, u32[]{:S(2)}) copy-start(bf16[256,256]{0,1:T(8,128)(2,1)} %copy-done.26) | copy-start | bytes 393220
  137.9 21.2 %copy-start.5 = (bf16[2,256,256]{1,2,0:T(8,128)(2,1)}, bf16[2,256,256]{1,2,0:T(8,128)(2,1)S(1)}, u32[]{:S(2)}) copy-start(bf16[2,256,256]{1,2,0:T(8,128)(2,1)S(1)} %fusion.95) | copy-start | bytes 786436
  139.1 2.1 %copy-start.7 = (bf16[1,256,256]{1,2,0:T(8,128)(2,1)S(1)}, bf16[1,256,256]{1,2,0:T(8,128)(2,1)}, u32[]{:S(2)}) copy-start(bf16[1,256,256]{1,2,0:T(8,128)(2,1)} %copy.103) | copy-start | bytes 393220
  139.1 15.5 %copy-start.30 = (bf16[256,256]{0,1:T(8,128)(2,1)S(1)}, bf16[256,256]{0,1:T(8,128)(2,1)}, u32[]{:S(2)}) copy-start(bf16[256,256]{0,1:T(8,128)(2,1)} %copy-done.29) | copy-start | bytes 393220
  152.8 5.9 %collective-permute-start.7 = (bf16[256,1152]{1,0:T(8,128)(2,1)}, bf16[256,1152]{1,0:T(8,128)(2,1)S(1)}, u32[]{:S(2)}, u32[]{:S(2)}) collective-permute-start(bf16[256,1152]{1,0:T(8,128)(2,1)} %bitcast.50), channel_id=1, source_target_pairs={{0,1},{1,0},{2,3},{3,2},{4,5},{5,4},{6,7},{7,6},{8,9},{9,8},{10,11... | collective-permute-start | bytes 1769480 | tf_op jit(solution)/shard_map/ppermute | solution.py:60
  155.7 1.5 copy-start.2
  159.7 1.3 collective-permute-start.8
  160.0 5.8 %copy-start.25 = (bf16[3,256,128]{2,1,0:T(8,128)(2,1)S(1)}, bf16[3,256,128]{2,1,0:T(8,128)(2,1)}, u32[]{:S(2)}) copy-start(bf16[3,256,128]{2,1,0:T(8,128)(2,1)} %param.13) | copy-start | bytes 589828
  162.1 4.1 %copy-start.9 = (bf16[1,256,256]{1,2,0:T(8,128)(2,1)S(1)}, bf16[1,256,256]{1,2,0:T(8,128)(2,1)}, u32[]{:S(2)}) copy-start(bf16[1,256,256]{1,2,0:T(8,128)(2,1)} %copy-done.8) | copy-start | bytes 393220
  162.1 4.4 %copy-start.6 = (bf16[2,256,256]{1,2,0:T(8,128)(2,1)S(1)}, bf16[2,256,256]{1,2,0:T(8,128)(2,1)}, u32[]{:S(2)}) copy-start(bf16[2,256,256]{1,2,0:T(8,128)(2,1)} %copy-done.5) | copy-start | bytes 786436
  162.1 4.4 %copy-start.32 = (bf16[256,256]{0,1:T(8,128)(2,1)S(1)}, bf16[256,256]{0,1:T(8,128)(2,1)}, u32[]{:S(2)}) copy-start(bf16[256,256]{0,1:T(8,128)(2,1)} %copy-done.31) | copy-start | bytes 393220
  162.1 4.4 %copy-start.38 = (bf16[3,256,128]{2,1,0:T(8,128)(2,1)S(1)}, bf16[3,256,128]{2,1,0:T(8,128)(2,1)}, u32[]{:S(2)}) copy-start(bf16[3,256,128]{2,1,0:T(8,128)(2,1)} %param.14) | copy-start | bytes 589828
  162.1 4.6 %copy-start.14 = (f32[2,256,256]{1,2,0:T(8,128)S(1)}, f32[2,256,256]{1,2,0:T(8,128)}, u32[]{:S(2)}) copy-start(f32[2,256,256]{1,2,0:T(8,128)} %get-tuple-element.47) | copy-start | bytes 1572868
  162.1 20.9 %all-to-all-start.5 = ((bf16[16,16,1152]{2,1,0:T(8,128)(2,1)}), bf16[16,16,1152]{2,1,0:T(8,128)(2,1)S(1)}, u32[]{:S(2)}, u32[]{:S(2)}) async-start(bf16[16,16,1152]{2,1,0:T(8,128)(2,1)} %bitcast.57), calls=%async_computation.5 | async-start | bytes 1179648 | tf_op jit(solution)/shard_map/all_to_all | solution.py:73
  167.0 1.5 copy-start.11
  183.1 1.1 copy-start.23
  184.1 7.8 %collective-permute-start.9 = (bf16[16,2304]{1,0:T(8,128)(2,1)S(1)}, bf16[16,2304]{1,0:T(8,128)(2,1)S(1)}, u32[]{:S(2)}, u32[]{:S(2)}) collective-permute-start(bf16[16,2304]{1,0:T(8,128)(2,1)S(1)} %fusion.107), channel_id=1, source_target_pairs={{0,240},{16,0},{32,16},{48,32},{64,48},{80,64},{96,80},{112,96},{1... | collective-permute-start | bytes 221192 | tf_op jit(solution)/shard_map/ppermute | solution.py:119
  (6 other events, 4.8 us)

commit v3 on v2

v3 whole, which is shorter than its diff:
```python
import functools

import jax
import jax.numpy as jnp
from jax import lax
from jax.experimental import pallas as pl
from jax.experimental.pallas import tpu as pltpu
from jax.sharding import PartitionSpec as P

HD = 128
TICKS = 3
SCALE = 144.0 ** (-0.5)
EPS = 1e-06
NEGATIVE = -1e30
BIG = 56
VMEM = pl.BlockSpec(memory_space=pltpu.VMEM)


def dot_t(a, b):
    return lax.dot_general(a, b, (((1,), (1,)), ((), ())), preferred_element_type=jnp.float32)


def dot_n(a, b):
    return lax.dot_general(a, b, (((1,), (0,)), ((), ())), preferred_element_type=jnp.float32)


def token_order(place, rank, rows, chips, direction):
    length = 2 * rows * chips
    half, size, far = length // 2, 2 * rows, chips // 2
    chip, own = rank // 2, rank % 2
    core = jnp.where(place < half, own, 1 - own)
    inner = jnp.where(place < half, place, place - half)
    part = inner // size
    within = inner - part * size
    near = (chip + direction * (1 - 2 * core) * (far - 1 - part) + chips) % chips
    near_token = near * size + within
    edge = jnp.where(within < rows, (chip + far) % chips, chip)
    edge_token = edge * size + rows * core + jnp.where(within < rows, within, within - rows)
    return jnp.where(part < far - 1, near_token, edge_token)


def softmax_kernel(rows, chips, tick, q_ref, k_ref, docs_ref, gate_ref, chance_ref, low_t_ref):
    length = q_ref.shape[1]
    rank = lax.axis_index("tensor")
    down = lax.broadcasted_iota(jnp.int32, (length, length), 0)
    across = lax.broadcasted_iota(jnp.int32, (length, length), 1)
    line = docs_ref[tick]
    column = jnp.sum(jnp.where(down == across, line, 0), axis=1, keepdims=True)
    allowed = (down >= across) & (column == line)
    key_hot = (token_order(down, rank, rows, chips, 1) == across).astype(jnp.bfloat16)
    query_hot = (token_order(across, rank, rows, chips, -1) == down).astype(jnp.bfloat16)
    for head in range(q_ref.shape[2] // HD):
        scores = dot_t(q_ref[tick, :, head * HD : (head + 1) * HD], k_ref[tick]) * SCALE
        scores = jnp.where(allowed, scores, NEGATIVE)
        expsum = jnp.exp(scores - jnp.max(scores, axis=-1, keepdims=True))
        chance = expsum / jnp.sum(expsum, axis=-1, keepdims=True)
        chance_ref[head] = chance
        turned = dot_t(key_hot, chance.astype(jnp.bfloat16)).astype(jnp.bfloat16)
        low_t_ref[head] = dot_n(turned, query_hot).astype(jnp.bfloat16)


def grads_kernel(rows, chips, tick, chance_ref, go_ref, q_ref, k_ref, v_ref, gq_ref, gk_ref):
    length = q_ref.shape[1]
    rank = lax.axis_index("tensor")
    down = lax.broadcasted_iota(jnp.int32, (length, length), 0)
    across = lax.broadcasted_iota(jnp.int32, (length, length), 1)
    query_hot = (token_order(across, rank, rows, chips, -1) == down).astype(jnp.bfloat16)
    grad_out = dot_n(query_hot, go_ref[...]).astype(jnp.bfloat16)
    total = jnp.zeros(gk_ref.shape, jnp.float32)
    for head in range(q_ref.shape[2] // HD):
        columns = slice(head * HD, (head + 1) * HD)
        chance = chance_ref[head]
        grad = grad_out[:, columns]
        attended = dot_n(chance.astype(jnp.bfloat16), v_ref[tick])
        row_dot = jnp.sum(grad.astype(jnp.float32) * attended, axis=-1, keepdims=True)
        grad_chance = dot_t(grad, v_ref[tick])
        grad_scores = (chance * (grad_chance - row_dot)).astype(jnp.bfloat16)
        gq_ref[:, columns] = (dot_n(grad_scores, k_ref[tick]) * SCALE).astype(jnp.bfloat16)
        total = total + lax.dot_general(
            grad_scores,
            q_ref[tick, :, columns],
            (((0,), (0,)), ((), ())),
            preferred_element_type=jnp.float32,
        )
    gk_ref[...] = (total * SCALE).astype(jnp.bfloat16)


def order_kernel(a_ref, b_ref, pair_ref):
    rows = a_ref.shape[0]
    first = lax.axis_index("tensor") % 2 == 0
    pair_ref[:rows] = jnp.where(first, a_ref[...], b_ref[...])
    pair_ref[rows:] = jnp.where(first, b_ref[...], a_ref[...])


def out_kernel(*refs):
    *parts, here_ref, own_ref, pair_ref, keep_ref, send_ref, mine_ref = refs
    at = 0
    for part in parts:
        mine_ref[at : at + part.shape[0]] = part[...]
        at += part.shape[0]
    rows = here_ref.shape[0] // 2
    first = lax.axis_index("tensor") % 2 == 0
    mine_ref[at:] = jnp.where(first, here_ref[:rows], here_ref[rows:])
    keep_ref[...] = dot_t(mine_ref[...], own_ref[...]).astype(jnp.bfloat16)
    send_ref[...] = dot_t(mine_ref[...], pair_ref[...]).astype(jnp.bfloat16)


def value_kernel(keep_ref, recv_ref, low_t_ref, go_ref, own_ref, away_ref):
    half = keep_ref.shape[0]
    go_ref[:half] = keep_ref[...]
    go_ref[half:] = recv_ref[...]
    total = jnp.zeros((2 * half, HD), jnp.float32)
    for head in range(low_t_ref.shape[0]):
        total = total + dot_n(low_t_ref[head], go_ref[:, head * HD : (head + 1) * HD])
    total = total.astype(jnp.bfloat16)
    own_ref[...] = total[:half]
    away_ref[...] = total[half:]


def partial_kernel(gv_ref, gv_pair_ref, own_ref, pair_ref, *outs):
    total = dot_t(gv_ref[...], own_ref[...]) + dot_t(gv_pair_ref[...], pair_ref[...])
    total = total.astype(jnp.bfloat16)
    at = 0
    for out in outs:
        out[...] = total[at : at + out.shape[0]]
        at += out.shape[0]


def sum_kernel(*refs):
    *near, away_ref, here_ref, total_ref = refs
    rows = away_ref.shape[0]
    total = near[0][...].astype(jnp.float32)
    for ref in near[1:]:
        total = total + ref[...].astype(jnp.float32)
    edge = away_ref[...].astype(jnp.float32) + here_ref[...].astype(jnp.float32)
    first = lax.axis_index("tensor") % 2 == 0
    total_ref[:rows] = total[:rows] + jnp.where(first, edge, 0.0)
    total_ref[rows:] = total[rows:] + jnp.where(first, 0.0, edge)


def norm_kernel(tick, a_ref, b_ref, x_own_ref, x_other_ref, gain_ref, current_ref, new_ref, mine_ref):
    rows = x_own_ref.shape[1]
    first = lax.axis_index("tensor") % 2 == 0
    gain = gain_ref[...].astype(jnp.float32)
    low = jnp.where(first, x_own_ref[tick], x_other_ref[tick])
    high = jnp.where(first, x_other_ref[tick], x_own_ref[tick])
    found = []
    for at, piece in ((0, low), (rows, high)):
        inputs = piece.astype(jnp.float32)
        inverse = lax.rsqrt(jnp.mean(inputs * inputs, -1, keepdims=True) + EPS)
        scaled = (a_ref[at : at + rows] + b_ref[at : at + rows]) * gain
        inner = jnp.mean(scaled * inputs, -1, keepdims=True)
        updated = (
            current_ref[at : at + rows].astype(jnp.float32)
            + inverse * scaled
            - inputs * (inverse * inverse * inverse * inner)
        ).astype(jnp.bfloat16)
        new_ref[at : at + rows] = updated
        found.append(updated)
    mine_ref[...] = jnp.where(first, found[0], found[1])


def choose_kernel(tick, plan_ref, *refs):
    chosen = plan_ref[tick, 0]
    count = (len(refs) - 2) // 2
    sources, outs, sems = refs[:count], refs[count + 1 : -1], refs[-1]
    copies = [
        pltpu.make_async_copy(source.at[chosen, 0] if source.ndim == 4 else source.at[chosen], out, sems.at[i])
        for i, (source, out) in enumerate(zip(sources, outs))
    ]
    for copy in copies:
        copy.start()
    for copy in copies:
        copy.wait()


def on_core(kernel, shapes, operands, scratch=(), limit=24, gate=None):
    specs = [VMEM] * len(operands)
    if gate is not None:
        specs.append(pl.BlockSpec(memory_space=pl.ANY))
        operands = (*operands, gate)
    return pl.pallas_call(
        kernel,
        out_shape=shapes,
        in_specs=specs,
        out_specs=[VMEM] * len(shapes),
        scratch_shapes=list(scratch),
        cost_estimate=pl.CostEstimate(flops=1000, bytes_accessed=1000, transcendentals=0),
        compiler_params=pltpu.CompilerParams(vmem_limit_bytes=limit * 1024 * 1024),
    )(*operands)


def choose(tick, plan, weights, gate):
    anywhere = pl.BlockSpec(memory_space=pl.ANY)
    shapes = [jax.ShapeDtypeStruct(item.shape[-2:], item.dtype) for item in weights]
    return pl.pallas_call(
        functools.partial(choose_kernel, tick),
        out_shape=shapes,
        in_specs=[pl.BlockSpec(memory_space=pltpu.SMEM)] + [anywhere] * (len(weights) + 1),
        out_specs=[VMEM] * len(shapes),
        scratch_shapes=[pltpu.SemaphoreType.DMA((len(weights),))],
        cost_estimate=pl.CostEstimate(flops=1000, bytes_accessed=1000, transcendentals=0),
        compiler_params=pltpu.CompilerParams(vmem_limit_bytes=24 * 1024 * 1024),
    )(plan, *weights, gate)


def bf16(*shape):
    return jax.ShapeDtypeStruct(shape, jnp.bfloat16)


def f32(*shape):
    return jax.ShapeDtypeStruct(shape, jnp.float32)


def on_device(cot_in, saved_inputs, queries, keys, values, docs, plan, w_value, w_out, norm_gain):
    phases = lax.axis_size("section")
    members = lax.axis_size("tensor")
    chips = members // 2
    far = chips // 2
    rows, width = cot_in.shape
    length = rows * members
    half = length // 2
    heads = queries.shape[2] // HD
    hold = lax.optimization_barrier

    def swap(block):
        return lax.ppermute(block, "tensor", [(t, t ^ 1) for t in range(members)])

    def along(block, by):
        return lax.ppermute(block, "section", [(s, (s + by) % phases) for s in range(phases)])

    def hop(block, steps, back):
        pairs = []
        for s in range(phases):
            for z in range(chips):
                for c in range(2):
                    there = (z + (steps if c == 0 else -steps)) % chips
                    target = (s - back) % phases
                    pairs.append((s * members + 2 * z + c, target * members + 2 * there + c))
        return lax.ppermute(block, ("section", "tensor"), pairs)

    def attention_ready(tick, gate):
        return on_core(
            functools.partial(softmax_kernel, rows, chips, tick),
            [f32(heads, length, length), bf16(heads, length, length)],
            (queries, keys, docs),
            limit=BIG,
            gate=gate,
        )

    def grads(chance, grad_out, tick):
        return on_core(
            functools.partial(grads_kernel, rows, chips, tick),
            [bf16(*queries.shape[1:]), bf16(*keys.shape[1:])],
            (chance, grad_out, queries, keys, values),
            limit=BIG,
        )

    def gather(pair, mine, back, done):
        near = [hop(pair, k, back) for k in range(far - 1, 0, -1)]
        away = hop(mine, far, back)
        here = hop(pair, 0, back) if back else pair
        return hold((near + [away, here], done))

    def scatter(blocks, done):
        steps = list(range(far - 1, 0, -1)) + [far]
        moved = [hop(block, k, 0) for block, k in zip(blocks[:-1], steps)]
        moved, done = hold((moved + [blocks[-1]], done))
        total = on_core(sum_kernel, [f32(2 * rows, width)], moved)[0]
        return total, swap(total), done

    current = on_core(order_kernel, [bf16(2 * rows, width)], (cot_in, swap(cot_in)))[0]
    current, *later = hold((current, w_out, w_value, saved_inputs))
    away_out, away_value, inputs_away = (swap(item) for item in later)
    weights = [w_out, w_value, away_out, away_value, norm_gain]
    mine = cot_in
    query_list = []
    key_list = []
    for tick in range(TICKS):
        last = tick == TICKS - 1
        if tick == 0:
            done = attention_ready(0, current), choose(0, plan, weights, current), inputs_away
        elif tick == 1:
            done = attention_ready(2, current)
        else:
            done = ()
        parts, done = gather(current, mine, 1 if tick else 0, done)
        if tick == 0:
            ready, chosen, inputs_away = done
        elif tick == 1:
            ready_last = done
        current = parts[-1]
        chance, low_t = ready
        keep, send = on_core(
            out_kernel,
            [bf16(half, heads * HD)] * 2,
            parts + [chosen[0], chosen[2]],
            [pltpu.VMEM((half, width), jnp.bfloat16)],
        )
        grad_out, value_keep, value_send = on_core(
            value_kernel,
            [bf16(length, heads * HD), bf16(half, HD), bf16(half, HD)],
            (keep, swap(send), low_t),
        )
        blocks = on_core(
            partial_kernel,
            [bf16(2 * rows, width)] * (far - 1) + [bf16(rows, width)] * 2,
            (value_keep, swap(value_send), chosen[1], chosen[3]),
        )
        found = grads(chance, grad_out, tick)
        if last:
            done = jnp.stack(query_list + [found[0]]), jnp.stack(key_list + [found[1]])
        else:
            done = found, choose(tick + 1, plan, weights, blocks[-1])
            if tick == 0:
                done += (attention_ready(1, blocks[-1]),)
        total, total_pair, done = scatter(blocks, done)
        gain = chosen[4]
        if last:
            query, key = done
        else:
            found, chosen = done[:2]
            query_list.append(found[0])
            key_list.append(found[1])
            ready = done[2] if tick == 0 else ready_last
        current, mine = on_core(
            functools.partial(norm_kernel, tick),
            [bf16(2 * rows, width), bf16(rows, width)],
            (total, total_pair, saved_inputs, inputs_away, gain, current),
        )
    return along(mine, -1), query, key


def solution(mesh):
    return jax.shard_map(
        on_device,
        mesh=mesh,
        in_specs=(
            P(("section", "tensor"), None),
            P(None, ("section", "tensor"), None),
            P(None, "section", "tensor"),
            P(None, "section", "tensor"),
            P(None, "section", "tensor"),
            P(None, "section", None),
            P(None, "section"),
            P(None, "section", None, "tensor"),
            P(None, "section", "tensor", None),
            P(None, "section", None),
        ),
        out_specs=(
            P(("section", "tensor"), None),
            P(None, "section", "tensor"),
            P(None, "section", "tensor"),
        ),
        check_vma=False,
    )
```

time: 195 us -> 176 us (0.903)
  Pallas kernels: 0 us -> 38.7 us
  starting transfers between devices: 32.3 us -> 57.6 us
  matrix products: 23.5 us -> 0 us
  waiting for transfers between devices: 84.7 us -> 62.9 us
  blocking collectives: 21.6 us -> 0 us
  other arithmetic: 8.83 us -> 1.49 us
  between operations: 7.39 us -> 1.02 us
    all_to_all x5 -> x0, waiting for transfers between devices: 60.6 us -> none  [the longest x2 31.4 us: scatter(): terms = lax.all_to_all(partial.reshape(members, rows, half), 'tensor', 0, 0)]
    ppermute x10 -> x40, starting transfers between devices: 7.13 us -> 57.6 us  [the longest x26 55.6 us: hop(): return lax.ppermute(block, ('section', 'tensor'), pairs)]
    ppermute x10 -> x40, waiting for transfers between devices: 24.2 us -> 62.9 us  [the longest x26 42.3 us: hop(): return lax.ppermute(block, ('section', 'tensor'), pairs)]
    pallas_call x0 -> x25, Pallas kernels: none -> 38.7 us  [the longest x22 34.6 us: on_core(): pl.pallas_call(kernel, out_shape=shapes, in_specs=specs, out_specs=[VMEM]...]
    all_to_all x5 -> x0, starting transfers between devices: 25.1 us -> none  [the longest x3 17.3 us: gather(): found = lax.all_to_all(spread.reshape(members, rows, half), 'tensor', 0, 0)]
    all_to_all x1 -> x0, blocking collectives: 21.6 us -> none  [scatter(): terms = lax.all_to_all(partial.reshape(members, rows, half), 'tensor', 0, 0)]
    dot_general x27 -> x0, matrix products: 19.3 us -> none  [the longest x12 11.4 us: dot_t(): lax.dot_general(a, b, (((1,), (1,)), ((), ())), preferred_element_type=jn...]
    unnamed x82 -> x65, local copies, waits for them, and re-layouts: 4.9 us -> 13.3 us
  transfers between devices with their start and end apart: 15 -> 40, of which waited for: 11 -> 17; matrix products, arithmetic and copies ran while one was open for 17% -> 2% of each run, Pallas kernels for 0% -> 12%
where the time goes in v3:
time: 176 us; the launch traced here: 175 us
  waiting for transfers between devices  62.9 us (36%)
  starting transfers between devices  57.6 us (33%)
  Pallas kernels  38.7 us (22%)
  local copies, waits for them, and re-layouts  13.3 us (8%)
    ppermute x26, starting transfers between devices, hop(): return lax.ppermute(block, ('section', 'tensor'), pairs)  55.6 us
    ppermute x26, waiting for transfers between devices, hop(): return lax.ppermute(block, ('section', 'tensor'), pairs)  42.3 us
    pallas_call x22, Pallas kernels, on_core(): pl.pallas_call(kernel, out_shape=shapes, in_specs=specs, out_specs=[VMEM]...  34.6 us
    unnamed x65, local copies, waits for them, and re-layouts  13.3 us
    ppermute x13, waiting for transfers between devices, swap(): return lax.ppermute(block, 'tensor', [(t, t ^ 1) for t in range(members)])  12.9 us
    ppermute x1, waiting for transfers between devices, along(): lax.ppermute(block, 'section', [(s, (s + by) % phases) for s in range(pha...  7.67 us
    pallas_call x3, Pallas kernels, choose(): pl.pallas_call(functools.partial(choose_kernel, tick), out_shape=shapes,...  4.07 us
  transfers between devices with their start and end apart: 40, of which 17 were waited for; matrix products, arithmetic and copies ran while one was open for 2% of the time, Pallas kernels for 12%

profile of v3, /device:TPU:30, one launch (start us, length us, event | category | flops | bytes accessed | tf_op | source)
XLA Modules:
  0.0 175.0 jit_solution(457062546153918876)
XLA Ops:
  0.7 1.5 collective-permute-done.b_ref
  2.2 1.6 shard_map.121.gate_ref.refs_5_.refs_4_.current_ref
  4.4 1.9 %collective-permute-start.3 = (bf16[32,2304]{1,0:T(8,128)(2,1)}, bf16[32,2304]{1,0:T(8,128)(2,1)}, u32[]{:S(2)}, u32[]{:S(2)}) collective-permute-start(bf16[32,2304]{1,0:T(8,128)(2,1)} %shard_map.121.gate_ref.refs_5_.refs_4_.current_ref), channel_id=1, source_target_pairs={{0,2},{1,15},{2,4},{3,1},{4,6},{5,3},{6,8},{7,5},{8,10},{9,7},{10,... | collective-permute-start | bytes 442376 | tf_op jit(solution)/shard_map/ppermute | solution.py:240
  6.3 3.3 %collective-permute-start.2 = (bf16[32,2304]{1,0:T(8,128)(2,1)}, bf16[32,2304]{1,0:T(8,128)(2,1)}, u32[]{:S(2)}, u32[]{:S(2)}) collective-permute-start(bf16[32,2304]{1,0:T(8,128)(2,1)} %shard_map.121.gate_ref.refs_5_.refs_4_.current_ref), channel_id=1, source_target_pairs={{0,4},{1,13},{2,6},{3,15},{4,8},{5,1},{6,10},{7,3},{8,12},{9,5},{1... | collective-permute-start | bytes 442376 | tf_op jit(solution)/shard_map/ppermute | solution.py:240
  10.5 4.6 %collective-permute-start.1 = (bf16[32,2304]{1,0:T(8,128)(2,1)}, bf16[32,2304]{1,0:T(8,128)(2,1)}, u32[]{:S(2)}, u32[]{:S(2)}) collective-permute-start(bf16[32,2304]{1,0:T(8,128)(2,1)} %shard_map.121.gate_ref.refs_5_.refs_4_.current_ref), channel_id=1, source_target_pairs={{0,6},{1,11},{2,8},{3,13},{4,10},{5,15},{6,12},{7,1},{8,14},{9,3},... | collective-permute-start | bytes 442376 | tf_op jit(solution)/shard_map/ppermute | solution.py:240
  15.1 4.5 %collective-permute-start.4 = (bf16[16,2304]{1,0:T(8,128)(2,1)}, bf16[16,2304]{1,0:T(8,128)(2,1)}, u32[]{:S(2)}, u32[]{:S(2)}) collective-permute-start(bf16[16,2304]{1,0:T(8,128)(2,1)} %a_ref.1), channel_id=1, source_target_pairs={{0,8},{1,9},{2,10},{3,11},{4,12},{5,13},{6,14},{7,15},{8,0},{9,1},... | collective-permute-start | bytes 221192 | tf_op jit(solution)/shard_map/ppermute | solution.py:240
  21.1 3.0 %shard_map.122 = (f32[2,256,256]{2,1,0:T(8,128)}, bf16[2,256,256]{2,1,0:T(8,128)(2,1)}) custom-call(bf16[3,256,256]{2,1,0:T(8,128)(2,1)} %q_ref.11, bf16[3,256,128]{2,1,0:T(8,128)(2,1)} %k_ref.11, s32[3,1,256]{2,1,0:T(1,128)} %docs_ref.5, bf16[32,2304]{1,0:T(8,128)(2,1)} %shard_map.121.gate_ref.refs_5_.refs_4_.current_ref), custom_call_target="tpu_custom_call" | custom-call | flops 1000 | bytes 1000 | tf_op jit(solution)/shard_map/pallas_call | solution.py:182
  24.1 1.7 copy-done
  25.8 1.3 copy-done.2
  27.0 1.4 shard_map.123
  28.5 2.1 %shard_map.124 = (bf16[128,256]{1,0:T(8,128)(2,1)S(1)}, bf16[128,256]{1,0:T(8,128)(2,1)S(1)}) custom-call(bf16[32,2304]{1,0:T(8,128)(2,1)} %collective-permute-done.1.refs_0_, bf16[32,2304]{1,0:T(8,128)(2,1)} %collective-permute-done.2.refs_1_, bf16[32,2304]{1,0:T(8,128)(2,1)} %collective-permute-done.3.refs_2_, ...), custom_call_target="tpu_custom_call" | custom-call | flops 1000 | bytes 1000 | tf_op jit(solution)/shard_map/pallas_call | solution.py:182
  30.7 1.2 collective-permute-done.8.recv_ref
  35.8 3.4 %collective-permute-start.11 = (bf16[32,2304]{1,0:T(8,128)(2,1)}, bf16[32,2304]{1,0:T(8,128)(2,1)S(1)}, u32[]{:S(2)}, u32[]{:S(2)}) collective-permute-start(bf16[32,2304]{1,0:T(8,128)(2,1)} %get-tuple-element.153), channel_id=1, source_target_pairs={{0,4},{1,13},{2,6},{3,15},{4,8},{5,1},{6,10},{7,3},{8,12},{9,5},{1... | collective-permute-start | bytes 442376 | tf_op jit(solution)/shard_map/ppermute | solution.py:240
  39.2 1.5 collective-permute-start.12
  41.8 2.8 %shard_map.127 = (bf16[256,256]{1,0:T(8,128)(2,1)}, bf16[256,128]{1,0:T(8,128)(2,1)}) custom-call(f32[2,256,256]{2,1,0:T(8,128)} %get-tuple-element.157.chance_ref, bf16[256,256]{1,0:T(8,128)(2,1)} %copy-done.22, bf16[3,256,256]{2,1,0:T(8,128)(2,1)} %q_ref.11, bf16[3,256,128]{2,1,0:T(8,128)(2,1)} %k_ref.11, bf16[3,256,128]{2,1,0:T(8,128)(2,1)} %v_ref.5), custom_call_target="tpu_custom_call" | custom-call | flops 1000 | bytes 1000 | tf_op jit(solution)/shard_map/pallas_call | solution.py:182
  44.6 3.0 %shard_map.129 = (f32[2,256,256]{2,1,0:T(8,128)}, bf16[2,256,256]{2,1,0:T(8,128)(2,1)}) custom-call(bf16[3,256,256]{2,1,0:T(8,128)(2,1)} %q_ref.11, bf16[3,256,128]{2,1,0:T(8,128)(2,1)} %k_ref.11, s32[3,1,256]{2,1,0:T(1,128)} %docs_ref.5, bf16[16,2304]{1,0:T(8,128)(2,1)} %copy-done.9), custom_call_target="tpu_custom_call" | custom-call | flops 1000 | bytes 1000 | tf_op jit(solution)/shard_map/pallas_call | solution.py:182
  48.5 1.4 shard_map.128
  50.9 2.9 %collective-permute-done.13.refs_3_ = bf16[16,2304]{1,0:T(8,128)(2,1)S(1)} collective-permute-done((bf16[16,2304]{1,0:T(8,128)(2,1)}, bf16[16,2304]{1,0:T(8,128)(2,1)S(1)}, u32[]{:S(2)}, u32[]{:S(2)}) %collective-permute-start.13) | collective-permute-done | bytes 73760 | tf_op jit(solution)/shard_map/ppermute | solution.py:240
  58.1 1.6 collective-permute-done.14.b_ref
  59.6 1.9 %shard_map.131 = (bf16[32,2304]{1,0:T(8,128)(2,1)}, bf16[16,2304]{1,0:T(8,128)(2,1)}) custom-call(f32[32,2304]{1,0:T(8,128)S(1)} %shard_map.130.a_ref, f32[32,2304]{1,0:T(8,128)S(1)} %collective-permute-done.14.b_ref, bf16[3,16,2304]{2,1,0:T(8,128)(2,1)S(1)} %copy-done.4, bf16[3,16,2304]{2,1,0:T(8,128)(2,1)} %collective-permute-done.7.x_other_ref, ...), custom_call_target="tpu_custom_call" | custom-call | flops 1000 | bytes 1000 | tf_op jit(solution)/shard_map/pallas_call | solution.py:182
  62.4 1.6 collective-permute-start.16
  64.0 6.1 %collective-permute-start.15 = (bf16[32,2304]{1,0:T(8,128)(2,1)}, bf16[32,2304]{1,0:T(8,128)(2,1)}, u32[]{:S(2)}, u32[]{:S(2)}) collective-permute-start(bf16[32,2304]{1,0:T(8,128)(2,1)} %get-tuple-element.175.gate_ref), channel_id=1, source_target_pairs={{0,246},{1,251},{2,248},{3,253},{4,250},{5,255},{6,252},{7,241},{8... | collective-permute-start | bytes 442376 | tf_op jit(solution)/shard_map/ppermute | solution.py:240
  70.1 1.8 %collective-permute-start.18 = (bf16[16,2304]{1,0:T(8,128)(2,1)}, bf16[16,2304]{1,0:T(8,128)(2,1)S(1)}, u32[]{:S(2)}, u32[]{:S(2)}) collective-permute-start(bf16[16,2304]{1,0:T(8,128)(2,1)} %get-tuple-element.176), channel_id=1, source_target_pairs={{0,248},{1,249},{2,250},{3,251},{4,252},{5,253},{6,254},{7,255},{8... | collective-permute-start | bytes 221192 | tf_op jit(solution)/shard_map/ppermute | solution.py:240
  72.0 3.0 %shard_map.132 = (f32[2,256,256]{2,1,0:T(8,128)}, bf16[2,256,256]{2,1,0:T(8,128)(2,1)}) custom-call(bf16[3,256,256]{2,1,0:T(8,128)(2,1)} %q_ref.11, bf16[3,256,128]{2,1,0:T(8,128)(2,1)} %k_ref.11, s32[3,1,256]{2,1,0:T(1,128)} %docs_ref.5, bf16[32,2304]{1,0:T(8,128)(2,1)} %get-tuple-element.175.gate_ref), custom_call_target="tpu_custom_call" | custom-call | flops 1000 | bytes 1000 | tf_op jit(solution)/shard_map/pallas_call | solution.py:182
  75.0 11.0 %collective-permute-done.18.refs_3_ = bf16[16,2304]{1,0:T(8,128)(2,1)S(1)} collective-permute-done((bf16[16,2304]{1,0:T(8,128)(2,1)}, bf16[16,2304]{1,0:T(8,128)(2,1)S(1)}, u32[]{:S(2)}, u32[]{:S(2)}) %collective-permute-start.18) | collective-permute-done | bytes 73760 | tf_op jit(solution)/shard_map/ppermute | solution.py:240
  86.1 1.3 copy-done.6
  87.3 1.3 copy-done.8
  88.6 1.9 %shard_map.133 = (bf16[128,256]{1,0:T(8,128)(2,1)S(1)}, bf16[128,256]{1,0:T(8,128)(2,1)S(1)}) custom-call(bf16[32,2304]{1,0:T(8,128)(2,1)} %collective-permute-done.15.refs_0_, bf16[32,2304]{1,0:T(8,128)(2,1)} %collective-permute-done.16.refs_1_, bf16[32,2304]{1,0:T(8,128)(2,1)S(1)} %collective-permute-done.17.refs_2_, ...), custom_call_target="tpu_custom_call" | custom-call | flops 1000 | bytes 1000 | tf_op jit(solution)/shard_map/pallas_call | solution.py:182
  90.7 1.2 collective-permute-done.20.recv_ref
  94.7 1.7 collective-permute-start.22
  96.4 1.6 collective-permute-start.24
  98.0 3.7 %collective-permute-start.25 = (bf16[16,2304]{1,0:T(8,128)(2,1)}, bf16[16,2304]{1,0:T(8,128)(2,1)}, u32[]{:S(2)}, u32[]{:S(2)}) collective-permute-start(bf16[16,2304]{1,0:T(8,128)(2,1)} %get-tuple-element.196), channel_id=1, source_target_pairs={{0,8},{1,9},{2,10},{3,11},{4,12},{5,13},{6,14},{7,15},{8,0},{9,1},... | collective-permute-start | bytes 221192 | tf_op jit(solution)/shard_map/ppermute | solution.py:240
  101.7 2.8 %shard_map.136 = (bf16[256,256]{1,0:T(8,128)(2,1)}, bf16[256,128]{1,0:T(8,128)(2,1)}) custom-call(f32[2,256,256]{2,1,0:T(8,128)} %get-tuple-element.198.chance_ref, bf16[256,256]{1,0:T(8,128)(2,1)} %copy-done.23, bf16[3,256,256]{2,1,0:T(8,128)(2,1)} %q_ref.11, bf16[3,256,128]{2,1,0:T(8,128)(2,1)} %k_ref.11, bf16[3,256,128]{2,1,0:T(8,128)(2,1)} %v_ref.5), custom_call_target="tpu_custom_call" | custom-call | flops 1000 | bytes 1000 | tf_op jit(solution)/shard_map/pallas_call | solution.py:182
  104.5 1.4 shard_map.137
  105.9 5.8 %collective-permute-done.25.refs_3_ = bf16[16,2304]{1,0:T(8,128)(2,1)} collective-permute-done((bf16[16,2304]{1,0:T(8,128)(2,1)}, bf16[16,2304]{1,0:T(8,128)(2,1)}, u32[]{:S(2)}, u32[]{:S(2)}) %collective-permute-start.25) | collective-permute-done | bytes 73760 | tf_op jit(solution)/shard_map/ppermute | solution.py:240
  112.9 1.6 collective-permute-done.26.b_ref
  115.8 1.9 %collective-permute-start.28 = (bf16[32,2304]{1,0:T(8,128)(2,1)S(1)}, bf16[32,2304]{1,0:T(8,128)(2,1)S(1)}, u32[]{:S(2)}, u32[]{:S(2)}) collective-permute-start(bf16[32,2304]{1,0:T(8,128)(2,1)S(1)} %get-tuple-element.213), channel_id=1, source_target_pairs={{0,244},{1,253},{2,246},{3,255},{4,248},{5,241},{6,250},{7,243},{8... | collective-permute-start | bytes 442376 | tf_op jit(solution)/shard_map/ppermute | solution.py:240
  117.7 6.4 %collective-permute-start.27 = (bf16[32,2304]{1,0:T(8,128)(2,1)S(1)}, bf16[32,2304]{1,0:T(8,128)(2,1)S(1)}, u32[]{:S(2)}, u32[]{:S(2)}) collective-permute-start(bf16[32,2304]{1,0:T(8,128)(2,1)S(1)} %get-tuple-element.213), channel_id=1, source_target_pairs={{0,246},{1,251},{2,248},{3,253},{4,250},{5,255},{6,252},{7,241},{8... | collective-permute-start | bytes 442376 | tf_op jit(solution)/shard_map/ppermute | solution.py:240
  124.1 1.7 collective-permute-start.30
  125.8 13.2 %collective-permute-done.30.refs_3_ = bf16[16,2304]{1,0:T(8,128)(2,1)S(1)} collective-permute-done((bf16[16,2304]{1,0:T(8,128)(2,1)S(1)}, bf16[16,2304]{1,0:T(8,128)(2,1)S(1)}, u32[]{:S(2)}, u32[]{:S(2)}) %collective-permute-start.30) | collective-permute-done | bytes 73760 | tf_op jit(solution)/shard_map/ppermute | solution.py:240
  141.1 1.2 collective-permute-done.32.recv_ref
  143.4 2.8 %shard_map.143 = (bf16[256,256]{1,0:T(8,128)(2,1)}, bf16[256,128]{1,0:T(8,128)(2,1)}) custom-call(f32[2,256,256]{2,1,0:T(8,128)} %get-tuple-element.236.chance_ref, bf16[256,256]{1,0:T(8,128)(2,1)} %copy-done.24, bf16[3,256,256]{2,1,0:T(8,128)(2,1)} %q_ref.11, bf16[3,256,128]{2,1,0:T(8,128)(2,1)} %k_ref.11, bf16[3,256,128]{2,1,0:T(8,128)(2,1)} %v_ref.5), custom_call_target="tpu_custom_call" | custom-call | flops 1000 | bytes 1000 | tf_op jit(solution)/shard_map/pallas_call | solution.py:182
  147.6 2.7 %collective-permute-start.36 = (bf16[32,2304]{1,0:T(8,128)(2,1)S(1)}, bf16[32,2304]{1,0:T(8,128)(2,1)S(1)}, u32[]{:S(2)}, u32[]{:S(2)}) collective-permute-start(bf16[32,2304]{1,0:T(8,128)(2,1)S(1)} %get-tuple-element.231), channel_id=1, source_target_pairs={{0,2},{1,15},{2,4},{3,1},{4,6},{5,3},{6,8},{7,5},{8,10},{9,7},{10,... | collective-permute-start | bytes 442376 | tf_op jit(solution)/shard_map/ppermute | solution.py:240
  151.1 3.0 %collective-permute-start.37 = (bf16[16,2304]{1,0:T(8,128)(2,1)S(1)}, bf16[16,2304]{1,0:T(8,128)(2,1)S(1)}, u32[]{:S(2)}, u32[]{:S(2)}) collective-permute-start(bf16[16,2304]{1,0:T(8,128)(2,1)S(1)} %get-tuple-element.232), channel_id=1, source_target_pairs={{0,8},{1,9},{2,10},{3,11},{4,12},{5,13},{6,14},{7,15},{8,0},{9,1},... | collective-permute-start | bytes 221192 | tf_op jit(solution)/shard_map/ppermute | solution.py:240
  154.8 8.2 %collective-permute-done.37.refs_3_ = bf16[16,2304]{1,0:T(8,128)(2,1)S(1)} collective-permute-done((bf16[16,2304]{1,0:T(8,128)(2,1)S(1)}, bf16[16,2304]{1,0:T(8,128)(2,1)S(1)}, u32[]{:S(2)}, u32[]{:S(2)}) %collective-permute-start.37) | collective-permute-done | bytes 73760 | tf_op jit(solution)/shard_map/ppermute | solution.py:240
  163.3 1.6 collective-permute-done.38.b_ref
  164.9 1.8 %shard_map.145 = (bf16[32,2304]{1,0:T(8,128)(2,1)}, bf16[16,2304]{1,0:T(8,128)(2,1)S(1)}) custom-call(f32[32,2304]{1,0:T(8,128)S(1)} %shard_map.144.a_ref, f32[32,2304]{1,0:T(8,128)S(1)} %collective-permute-done.38.b_ref, bf16[3,16,2304]{2,1,0:T(8,128)(2,1)S(1)} %copy-done.4, bf16[3,16,2304]{2,1,0:T(8,128)(2,1)} %collective-permute-done.7.x_other_ref, ...), custom_call_target="tpu_custom_call" | custom-call | flops 1000 | bytes 1000 | tf_op jit(solution)/shard_map/pallas_call | solution.py:182
  166.6 7.7 %collective-permute-done.39 = bf16[16,2304]{1,0:T(8,128)(2,1)S(1)} collective-permute-done((bf16[16,2304]{1,0:T(8,128)(2,1)S(1)}, bf16[16,2304]{1,0:T(8,128)(2,1)S(1)}, u32[]{:S(2)}, u32[]{:S(2)}) %collective-permute-start.39) | collective-permute-done | bytes 73760 | tf_op jit(solution)/shard_map/ppermute | solution.py:230
  (124 shorter events, 27.4 us)
Async XLA Ops:
  0.6 1.6 collective-permute-start
  3.8 11.4 %collective-permute-start.5 = (bf16[2,1,256,2304]{3,2,1,0:T(8,128)(2,1)}, bf16[2,1,256,2304]{3,2,1,0:T(8,128)(2,1)S(1)}, u32[]{:S(2)}, u32[]{:S(2)}) collective-permute-start(bf16[2,1,256,2304]{3,2,1,0:T(8,128)(2,1)} %refs_0_.5), channel_id=1, source_target_pairs={{0,1},{1,0},{2,3},{3,2},{4,5},{5,4},{6,7},{7,6},{8,9},{9,8},{10,11... | collective-permute-start | bytes 7077896 | tf_op jit(solution)/shard_map/ppermute | solution.py:227
  3.9 6.6 %collective-permute-start.6 = (bf16[2,1,2304,128]{3,2,1,0:T(8,128)(2,1)}, bf16[2,1,2304,128]{3,2,1,0:T(8,128)(2,1)S(1)}, u32[]{:S(2)}, u32[]{:S(2)}) collective-permute-start(bf16[2,1,2304,128]{3,2,1,0:T(8,128)(2,1)} %refs_1_.5), channel_id=1, source_target_pairs={{0,1},{1,0},{2,3},{3,2},{4,5},{5,4},{6,7},{7,6},{8,9},{9,8},{10,11... | collective-permute-start | bytes 3538952 | tf_op jit(solution)/shard_map/ppermute | solution.py:227
  4.3 24.2 %collective-permute-start.7 = (bf16[3,16,2304]{2,1,0:T(8,128)(2,1)}, bf16[3,16,2304]{2,1,0:T(8,128)(2,1)}, u32[]{:S(2)}, u32[]{:S(2)}) collective-permute-start(bf16[3,16,2304]{2,1,0:T(8,128)(2,1)} %x_own_ref.5), channel_id=1, source_target_pairs={{0,1},{1,0},{2,3},{3,2},{4,5},{5,4},{6,7},{7,6},{8,9},{9,8},{10,11... | collective-permute-start | bytes 663560 | tf_op jit(solution)/shard_map/ppermute | solution.py:227
  4.4 24.0 %collective-permute-start.3 = (bf16[32,2304]{1,0:T(8,128)(2,1)}, bf16[32,2304]{1,0:T(8,128)(2,1)}, u32[]{:S(2)}, u32[]{:S(2)}) collective-permute-start(bf16[32,2304]{1,0:T(8,128)(2,1)} %shard_map.121.gate_ref.refs_5_.refs_4_.current_ref), channel_id=1, source_target_pairs={{0,2},{1,15},{2,4},{3,1},{4,6},{5,3},{6,8},{7,5},{8,10},{9,7},{10,... | collective-permute-start | bytes 442376 | tf_op jit(solution)/shard_map/ppermute | solution.py:240
  6.3 22.1 %collective-permute-start.2 = (bf16[32,2304]{1,0:T(8,128)(2,1)}, bf16[32,2304]{1,0:T(8,128)(2,1)}, u32[]{:S(2)}, u32[]{:S(2)}) collective-permute-start(bf16[32,2304]{1,0:T(8,128)(2,1)} %shard_map.121.gate_ref.refs_5_.refs_4_.current_ref), channel_id=1, source_target_pairs={{0,4},{1,13},{2,6},{3,15},{4,8},{5,1},{6,10},{7,3},{8,12},{9,5},{1... | collective-permute-start | bytes 442376 | tf_op jit(solution)/shard_map/ppermute | solution.py:240
  10.5 17.9 %collective-permute-start.1 = (bf16[32,2304]{1,0:T(8,128)(2,1)}, bf16[32,2304]{1,0:T(8,128)(2,1)}, u32[]{:S(2)}, u32[]{:S(2)}) collective-permute-start(bf16[32,2304]{1,0:T(8,128)(2,1)} %shard_map.121.gate_ref.refs_5_.refs_4_.current_ref), channel_id=1, source_target_pairs={{0,6},{1,11},{2,8},{3,13},{4,10},{5,15},{6,12},{7,1},{8,14},{9,3},... | collective-permute-start | bytes 442376 | tf_op jit(solution)/shard_map/ppermute | solution.py:240
  15.1 13.3 %collective-permute-start.4 = (bf16[16,2304]{1,0:T(8,128)(2,1)}, bf16[16,2304]{1,0:T(8,128)(2,1)}, u32[]{:S(2)}, u32[]{:S(2)}) collective-permute-start(bf16[16,2304]{1,0:T(8,128)(2,1)} %a_ref.1), channel_id=1, source_target_pairs={{0,8},{1,9},{2,10},{3,11},{4,12},{5,13},{6,14},{7,15},{8,0},{9,1},... | collective-permute-start | bytes 221192 | tf_op jit(solution)/shard_map/ppermute | solution.py:240
  30.6 1.3 collective-permute-start.8
  31.9 15.7 %copy-start.3 = (bf16[2,1,2304,128]{3,2,1,0:T(8,128)(2,1)S(1)}, bf16[2,1,2304,128]{3,2,1,0:T(8,128)(2,1)}, u32[]{:S(2)}) copy-start(bf16[2,1,2304,128]{3,2,1,0:T(8,128)(2,1)} %refs_1_.5) | copy-start | bytes 3538948
  32.2 1.3 collective-permute-start.9
  33.4 14.2 %copy-start.1 = (bf16[2,1,256,2304]{3,2,1,0:T(8,128)(2,1)S(1)}, bf16[2,1,256,2304]{3,2,1,0:T(8,128)(2,1)}, u32[]{:S(2)}) copy-start(bf16[2,1,256,2304]{3,2,1,0:T(8,128)(2,1)} %refs_0_.5) | copy-start | bytes 7077892
  34.7 9.9 %copy-start.9 = (bf16[16,2304]{1,0:T(8,128)(2,1)}, bf16[16,2304]{1,0:T(8,128)(2,1)S(1)}, u32[]{:S(2)}) copy-start(bf16[16,2304]{1,0:T(8,128)(2,1)S(1)} %get-tuple-element.172.refs_5_.gate_ref.refs_4_) | copy-start | bytes 221188
  34.7 19.1 %collective-permute-start.10 = (bf16[32,2304]{1,0:T(8,128)(2,1)}, bf16[32,2304]{1,0:T(8,128)(2,1)S(1)}, u32[]{:S(2)}, u32[]{:S(2)}) collective-permute-start(bf16[32,2304]{1,0:T(8,128)(2,1)} %get-tuple-element.152), channel_id=1, source_target_pairs={{0,6},{1,11},{2,8},{3,13},{4,10},{5,15},{6,12},{7,1},{8,14},{9,3},... | collective-permute-start | bytes 442376 | tf_op jit(solution)/shard_map/ppermute | solution.py:240
  35.8 18.6 %collective-permute-start.11 = (bf16[32,2304]{1,0:T(8,128)(2,1)}, bf16[32,2304]{1,0:T(8,128)(2,1)S(1)}, u32[]{:S(2)}, u32[]{:S(2)}) collective-permute-start(bf16[32,2304]{1,0:T(8,128)(2,1)} %get-tuple-element.153), channel_id=1, source_target_pairs={{0,4},{1,13},{2,6},{3,15},{4,8},{5,1},{6,10},{7,3},{8,12},{9,5},{1... | collective-permute-start | bytes 442376 | tf_op jit(solution)/shard_map/ppermute | solution.py:240
  39.2 15.9 %collective-permute-start.12 = (bf16[32,2304]{1,0:T(8,128)(2,1)}, bf16[32,2304]{1,0:T(8,128)(2,1)}, u32[]{:S(2)}, u32[]{:S(2)}) collective-permute-start(bf16[32,2304]{1,0:T(8,128)(2,1)} %get-tuple-element.154), channel_id=1, source_target_pairs={{0,2},{1,15},{2,4},{3,1},{4,6},{5,3},{6,8},{7,5},{8,10},{9,7},{10,... | collective-permute-start | bytes 442376 | tf_op jit(solution)/shard_map/ppermute | solution.py:240
  40.7 13.1 %collective-permute-start.13 = (bf16[16,2304]{1,0:T(8,128)(2,1)}, bf16[16,2304]{1,0:T(8,128)(2,1)S(1)}, u32[]{:S(2)}, u32[]{:S(2)}) collective-permute-start(bf16[16,2304]{1,0:T(8,128)(2,1)} %get-tuple-element.155), channel_id=1, source_target_pairs={{0,8},{1,9},{2,10},{3,11},{4,12},{5,13},{6,14},{7,15},{8,0},{9,1},... | collective-permute-start | bytes 221192 | tf_op jit(solution)/shard_map/ppermute | solution.py:240
  48.5 11.1 %copy-start.4 = (bf16[3,16,2304]{2,1,0:T(8,128)(2,1)S(1)}, bf16[3,16,2304]{2,1,0:T(8,128)(2,1)}, u32[]{:S(2)}) copy-start(bf16[3,16,2304]{2,1,0:T(8,128)(2,1)} %x_own_ref.5) | copy-start | bytes 663556
  50.9 10.6 %copy-start.5 = (bf16[256,2304]{1,0:T(8,128)(2,1)}, bf16[256,2304]{1,0:T(8,128)(2,1)S(1)}, u32[]{:S(2)}) copy-start(bf16[256,2304]{1,0:T(8,128)(2,1)S(1)} %get-tuple-element.184.refs_5_) | copy-start | bytes 3538948
  50.9 10.6 %copy-start.13 = (bf16[2304,128]{1,0:T(8,128)(2,1)}, bf16[2304,128]{1,0:T(8,128)(2,1)S(1)}, u32[]{:S(2)}) copy-start(bf16[2304,128]{1,0:T(8,128)(2,1)S(1)} %get-tuple-element.192.pair_ref) | copy-start | bytes 1769476
  58.0 1.7 collective-permute-start.14
  61.5 24.5 %collective-permute-start.19 = (bf16[32,2304]{1,0:T(8,128)(2,1)}, bf16[32,2304]{1,0:T(8,128)(2,1)S(1)}, u32[]{:S(2)}, u32[]{:S(2)}) collective-permute-start(bf16[32,2304]{1,0:T(8,128)(2,1)} %get-tuple-element.175.gate_ref), channel_id=1, source_target_pairs={{0,240},{1,241},{2,242},{3,243},{4,244},{5,245},{6,246},{7,247},{8... | collective-permute-start | bytes 442376 | tf_op jit(solution)/shard_map/ppermute | solution.py:240
  62.4 23.6 %collective-permute-start.17 = (bf16[32,2304]{1,0:T(8,128)(2,1)}, bf16[32,2304]{1,0:T(8,128)(2,1)S(1)}, u32[]{:S(2)}, u32[]{:S(2)}) collective-permute-start(bf16[32,2304]{1,0:T(8,128)(2,1)} %get-tuple-element.175.gate_ref), channel_id=1, source_target_pairs={{0,242},{1,255},{2,244},{3,241},{4,246},{5,243},{6,248},{7,245},{8... | collective-permute-start | bytes 442376 | tf_op jit(solution)/shard_map/ppermute | solution.py:240
  62.4 23.6 %collective-permute-start.16 = (bf16[32,2304]{1,0:T(8,128)(2,1)}, bf16[32,2304]{1,0:T(8,128)(2,1)}, u32[]{:S(2)}, u32[]{:S(2)}) collective-permute-start(bf16[32,2304]{1,0:T(8,128)(2,1)} %get-tuple-element.175.gate_ref), channel_id=1, source_target_pairs={{0,244},{1,253},{2,246},{3,255},{4,248},{5,241},{6,250},{7,243},{8... | collective-permute-start | bytes 442376 | tf_op jit(solution)/shard_map/ppermute | solution.py:240
  64.0 22.1 %collective-permute-start.15 = (bf16[32,2304]{1,0:T(8,128)(2,1)}, bf16[32,2304]{1,0:T(8,128)(2,1)}, u32[]{:S(2)}, u32[]{:S(2)}) collective-permute-start(bf16[32,2304]{1,0:T(8,128)(2,1)} %get-tuple-element.175.gate_ref), channel_id=1, source_target_pairs={{0,246},{1,251},{2,248},{3,253},{4,250},{5,255},{6,252},{7,241},{8... | collective-permute-start | bytes 442376 | tf_op jit(solution)/shard_map/ppermute | solution.py:240
  70.1 15.9 %collective-permute-start.18 = (bf16[16,2304]{1,0:T(8,128)(2,1)}, bf16[16,2304]{1,0:T(8,128)(2,1)S(1)}, u32[]{:S(2)}, u32[]{:S(2)}) collective-permute-start(bf16[16,2304]{1,0:T(8,128)(2,1)} %get-tuple-element.176), channel_id=1, source_target_pairs={{0,248},{1,249},{2,250},{3,251},{4,252},{5,253},{6,254},{7,255},{8... | collective-permute-start | bytes 221192 | tf_op jit(solution)/shard_map/ppermute | solution.py:240
  90.6 1.3 collective-permute-start.20
  92.1 1.3 collective-permute-start.21
  94.7 17.0 %collective-permute-start.22 = (bf16[32,2304]{1,0:T(8,128)(2,1)}, bf16[32,2304]{1,0:T(8,128)(2,1)S(1)}, u32[]{:S(2)}, u32[]{:S(2)}) collective-permute-start(bf16[32,2304]{1,0:T(8,128)(2,1)} %get-tuple-element.193), channel_id=1, source_target_pairs={{0,6},{1,11},{2,8},{3,13},{4,10},{5,15},{6,12},{7,1},{8,14},{9,3},... | collective-permute-start | bytes 442376 | tf_op jit(solution)/shard_map/ppermute | solution.py:240
  96.3 15.4 %collective-permute-start.23 = (bf16[32,2304]{1,0:T(8,128)(2,1)}, bf16[32,2304]{1,0:T(8,128)(2,1)}, u32[]{:S(2)}, u32[]{:S(2)}) collective-permute-start(bf16[32,2304]{1,0:T(8,128)(2,1)} %get-tuple-element.194), channel_id=1, source_target_pairs={{0,4},{1,13},{2,6},{3,15},{4,8},{5,1},{6,10},{7,3},{8,12},{9,5},{1... | collective-permute-start | bytes 442376 | tf_op jit(solution)/shard_map/ppermute | solution.py:240
  96.4 15.3 %collective-permute-start.24 = (bf16[32,2304]{1,0:T(8,128)(2,1)}, bf16[32,2304]{1,0:T(8,128)(2,1)}, u32[]{:S(2)}, u32[]{:S(2)}) collective-permute-start(bf16[32,2304]{1,0:T(8,128)(2,1)} %get-tuple-element.195), channel_id=1, source_target_pairs={{0,2},{1,15},{2,4},{3,1},{4,6},{5,3},{6,8},{7,5},{8,10},{9,7},{10,... | collective-permute-start | bytes 442376 | tf_op jit(solution)/shard_map/ppermute | solution.py:240
  98.0 13.7 %collective-permute-start.25 = (bf16[16,2304]{1,0:T(8,128)(2,1)}, bf16[16,2304]{1,0:T(8,128)(2,1)}, u32[]{:S(2)}, u32[]{:S(2)}) collective-permute-start(bf16[16,2304]{1,0:T(8,128)(2,1)} %get-tuple-element.196), channel_id=1, source_target_pairs={{0,8},{1,9},{2,10},{3,11},{4,12},{5,13},{6,14},{7,15},{8,0},{9,1},... | collective-permute-start | bytes 221192 | tf_op jit(solution)/shard_map/ppermute | solution.py:240
  105.9 35.1 %copy-start.11 = (bf16[2304,128]{1,0:T(8,128)(2,1)}, bf16[2304,128]{1,0:T(8,128)(2,1)S(1)}, u32[]{:S(2)}) copy-start(bf16[2304,128]{1,0:T(8,128)(2,1)S(1)} %get-tuple-element.228.pair_ref) | copy-start | bytes 1769476
  112.8 1.7 collective-permute-start.26
  115.6 23.4 %collective-permute-start.31 = (bf16[32,2304]{1,0:T(8,128)(2,1)S(1)}, bf16[32,2304]{1,0:T(8,128)(2,1)S(1)}, u32[]{:S(2)}, u32[]{:S(2)}) collective-permute-start(bf16[32,2304]{1,0:T(8,128)(2,1)S(1)} %get-tuple-element.213), channel_id=1, source_target_pairs={{0,240},{1,241},{2,242},{3,243},{4,244},{5,245},{6,246},{7,247},{8... | collective-permute-start | bytes 442376 | tf_op jit(solution)/shard_map/ppermute | solution.py:240
  115.7 23.3 %collective-permute-start.29 = (bf16[32,2304]{1,0:T(8,128)(2,1)S(1)}, bf16[32,2304]{1,0:T(8,128)(2,1)S(1)}, u32[]{:S(2)}, u32[]{:S(2)}) collective-permute-start(bf16[32,2304]{1,0:T(8,128)(2,1)S(1)} %get-tuple-element.213), channel_id=1, source_target_pairs={{0,242},{1,255},{2,244},{3,241},{4,246},{5,243},{6,248},{7,245},{8... | collective-permute-start | bytes 442376 | tf_op jit(solution)/shard_map/ppermute | solution.py:240
  115.8 23.2 %collective-permute-start.28 = (bf16[32,2304]{1,0:T(8,128)(2,1)S(1)}, bf16[32,2304]{1,0:T(8,128)(2,1)S(1)}, u32[]{:S(2)}, u32[]{:S(2)}) collective-permute-start(bf16[32,2304]{1,0:T(8,128)(2,1)S(1)} %get-tuple-element.213), channel_id=1, source_target_pairs={{0,244},{1,253},{2,246},{3,255},{4,248},{5,241},{6,250},{7,243},{8... | collective-permute-start | bytes 442376 | tf_op jit(solution)/shard_map/ppermute | solution.py:240
  117.7 22.3 %collective-permute-start.27 = (bf16[32,2304]{1,0:T(8,128)(2,1)S(1)}, bf16[32,2304]{1,0:T(8,128)(2,1)S(1)}, u32[]{:S(2)}, u32[]{:S(2)}) collective-permute-start(bf16[32,2304]{1,0:T(8,128)(2,1)S(1)} %get-tuple-element.213), channel_id=1, source_target_pairs={{0,246},{1,251},{2,248},{3,253},{4,250},{5,255},{6,252},{7,241},{8... | collective-permute-start | bytes 442376 | tf_op jit(solution)/shard_map/ppermute | solution.py:240
  124.1 18.2 %copy-start.15 = (bf16[2,256,256]{2,1,0:T(8,128)(2,1)S(1)}, bf16[2,256,256]{2,1,0:T(8,128)(2,1)}, u32[]{:S(2)}) copy-start(bf16[2,256,256]{2,1,0:T(8,128)(2,1)} %get-tuple-element.224.low_t_ref) | copy-start | bytes 786436
  124.1 14.9 %collective-permute-start.30 = (bf16[16,2304]{1,0:T(8,128)(2,1)S(1)}, bf16[16,2304]{1,0:T(8,128)(2,1)S(1)}, u32[]{:S(2)}, u32[]{:S(2)}) collective-permute-start(bf16[16,2304]{1,0:T(8,128)(2,1)S(1)} %get-tuple-element.214), channel_id=1, source_target_pairs={{0,248},{1,249},{2,250},{3,251},{4,252},{5,253},{6,254},{7,255},{8... | collective-permute-start | bytes 221192 | tf_op jit(solution)/shard_map/ppermute | solution.py:240
  141.0 1.3 collective-permute-start.32
  143.2 3.0 %collective-permute-start.33 = (bf16[128,128]{1,0:T(8,128)(2,1)S(1)}, bf16[128,128]{1,0:T(8,128)(2,1)S(1)}, u32[]{:S(2)}, u32[]{:S(2)}) collective-permute-start(bf16[128,128]{1,0:T(8,128)(2,1)S(1)} %get-tuple-element.226), channel_id=1, source_target_pairs={{0,1},{1,0},{2,3},{3,2},{4,5},{5,4},{6,7},{7,6},{8,9},{9,8},{10,11... | collective-permute-start | bytes 98312 | tf_op jit(solution)/shard_map/ppermute | solution.py:227
  146.7 16.3 %collective-permute-start.34 = (bf16[32,2304]{1,0:T(8,128)(2,1)S(1)}, bf16[32,2304]{1,0:T(8,128)(2,1)S(1)}, u32[]{:S(2)}, u32[]{:S(2)}) collective-permute-start(bf16[32,2304]{1,0:T(8,128)(2,1)S(1)} %get-tuple-element.229), channel_id=1, source_target_pairs={{0,6},{1,11},{2,8},{3,13},{4,10},{5,15},{6,12},{7,1},{8,14},{9,3},... | collective-permute-start | bytes 442376 | tf_op jit(solution)/shard_map/ppermute | solution.py:240
  147.6 15.5 %collective-permute-start.35 = (bf16[32,2304]{1,0:T(8,128)(2,1)S(1)}, bf16[32,2304]{1,0:T(8,128)(2,1)S(1)}, u32[]{:S(2)}, u32[]{:S(2)}) collective-permute-start(bf16[32,2304]{1,0:T(8,128)(2,1)S(1)} %get-tuple-element.230), channel_id=1, source_target_pairs={{0,4},{1,13},{2,6},{3,15},{4,8},{5,1},{6,10},{7,3},{8,12},{9,5},{1... | collective-permute-start | bytes 442376 | tf_op jit(solution)/shard_map/ppermute | solution.py:240
  147.6 15.5 %collective-permute-start.36 = (bf16[32,2304]{1,0:T(8,128)(2,1)S(1)}, bf16[32,2304]{1,0:T(8,128)(2,1)S(1)}, u32[]{:S(2)}, u32[]{:S(2)}) collective-permute-start(bf16[32,2304]{1,0:T(8,128)(2,1)S(1)} %get-tuple-element.231), channel_id=1, source_target_pairs={{0,2},{1,15},{2,4},{3,1},{4,6},{5,3},{6,8},{7,5},{8,10},{9,7},{10,... | collective-permute-start | bytes 442376 | tf_op jit(solution)/shard_map/ppermute | solution.py:240
  151.1 12.0 %collective-permute-start.37 = (bf16[16,2304]{1,0:T(8,128)(2,1)S(1)}, bf16[16,2304]{1,0:T(8,128)(2,1)S(1)}, u32[]{:S(2)}, u32[]{:S(2)}) collective-permute-start(bf16[16,2304]{1,0:T(8,128)(2,1)S(1)} %get-tuple-element.232), channel_id=1, source_target_pairs={{0,8},{1,9},{2,10},{3,11},{4,12},{5,13},{6,14},{7,15},{8,0},{9,1},... | collective-permute-start | bytes 221192 | tf_op jit(solution)/shard_map/ppermute | solution.py:240
  163.2 1.7 collective-permute-start.38
  166.6 7.7 %collective-permute-start.39 = (bf16[16,2304]{1,0:T(8,128)(2,1)S(1)}, bf16[16,2304]{1,0:T(8,128)(2,1)S(1)}, u32[]{:S(2)}, u32[]{:S(2)}) collective-permute-start(bf16[16,2304]{1,0:T(8,128)(2,1)S(1)} %get-tuple-element.248), channel_id=1, source_target_pairs={{0,240},{16,0},{32,16},{48,32},{64,48},{80,64},{96,80},{112,96},{1... | collective-permute-start | bytes 221192 | tf_op jit(solution)/shard_map/ppermute | solution.py:230
  (23 other events, 75.8 us)

commit v4 on v3

v4 whole, which is shorter than its diff:
```python
import functools

import jax
import jax.numpy as jnp
from jax import lax
from jax.experimental import pallas as pl
from jax.experimental.pallas import tpu as pltpu
from jax.sharding import PartitionSpec as P

HD = 128
TICKS = 3
SCALE = 144.0 ** (-0.5)
EPS = 1e-06
NEGATIVE = -1e30
VMEM = pl.BlockSpec(memory_space=pltpu.VMEM)


def dot_t(a, b):
    return lax.dot_general(a, b, (((1,), (1,)), ((), ())), preferred_element_type=jnp.float32)


def dot_n(a, b):
    return lax.dot_general(a, b, (((1,), (0,)), ((), ())), preferred_element_type=jnp.float32)


def token_order(place, rank, rows, chips, direction):
    length = 2 * rows * chips
    half, size, far = length // 2, 2 * rows, chips // 2
    chip, own = rank // 2, rank % 2
    core = jnp.where(place < half, own, 1 - own)
    inner = jnp.where(place < half, place, place - half)
    part = inner // size
    within = inner - part * size
    near = (chip + direction * (1 - 2 * core) * (far - part) + chips) % chips
    edge = jnp.where(core == 0, (chip + far) % chips, chip)
    return jnp.where(part == 0, edge, near) * size + within


def softmax_kernel(rows, chips, wait, q_ref, k_ref, docs_ref, chance_ref, low_t_ref):
    length = q_ref.shape[0]
    rank = lax.axis_index("tensor")
    down = lax.broadcasted_iota(jnp.int32, (length, length), 0)
    across = lax.broadcasted_iota(jnp.int32, (length, length), 1)
    key_hot = (token_order(down, rank, rows, chips, 1) == across).astype(jnp.bfloat16)
    query_hot = (token_order(across, rank, rows, chips, -1) == down).astype(jnp.bfloat16)
    wait()
    line = docs_ref[...]
    column = jnp.sum(jnp.where(down == across, line, 0), axis=1, keepdims=True)
    allowed = (down >= across) & (column == line)
    for head in range(q_ref.shape[1] // HD):
        scores = dot_t(q_ref[:, head * HD : (head + 1) * HD], k_ref[...]) * SCALE
        scores = jnp.where(allowed, scores, NEGATIVE)
        expsum = jnp.exp(scores - jnp.max(scores, axis=-1, keepdims=True))
        chance = expsum / jnp.sum(expsum, axis=-1, keepdims=True)
        chance_ref[head] = chance
        turned = dot_t(key_hot, chance.astype(jnp.bfloat16)).astype(jnp.bfloat16)
        low_t_ref[head] = dot_n(turned, query_hot).astype(jnp.bfloat16)


def grads_kernel(rows, chips, wait, chance_ref, go_ref, q_ref, k_ref, v_ref, gq_ref, gk_ref):
    length = q_ref.shape[0]
    rank = lax.axis_index("tensor")
    down = lax.broadcasted_iota(jnp.int32, (length, length), 0)
    across = lax.broadcasted_iota(jnp.int32, (length, length), 1)
    query_hot = (token_order(across, rank, rows, chips, -1) == down).astype(jnp.bfloat16)
    wait()
    grad_out = dot_n(query_hot, go_ref[...]).astype(jnp.bfloat16)
    total = jnp.zeros(gk_ref.shape, jnp.float32)
    for head in range(q_ref.shape[1] // HD):
        columns = slice(head * HD, (head + 1) * HD)
        chance = chance_ref[head]
        grad = grad_out[:, columns]
        attended = dot_n(chance.astype(jnp.bfloat16), v_ref[...])
        row_dot = jnp.sum(grad.astype(jnp.float32) * attended, axis=-1, keepdims=True)
        grad_chance = dot_t(grad, v_ref[...])
        grad_scores = (chance * (grad_chance - row_dot)).astype(jnp.bfloat16)
        gq_ref[:, columns] = (dot_n(grad_scores, k_ref[...]) * SCALE).astype(jnp.bfloat16)
        total = total + lax.dot_general(
            grad_scores,
            q_ref[:, columns],
            (((0,), (0,)), ((), ())),
            preferred_element_type=jnp.float32,
        )
    gk_ref[...] = (total * SCALE).astype(jnp.bfloat16)


def order_kernel(a_ref, b_ref, pair_ref):
    rows = a_ref.shape[0]
    first = lax.axis_index("tensor") % 2 == 0
    pair_ref[:rows] = jnp.where(first, a_ref[...], b_ref[...])
    pair_ref[rows:] = jnp.where(first, b_ref[...], a_ref[...])


def out_kernel(*refs):
    edge_ref, *near, own_ref, pair_ref, keep_ref, send_ref, mine_ref = refs
    size = edge_ref.shape[0]
    for i, part in enumerate((edge_ref, *near[::-1])):
        mine_ref[i * size : (i + 1) * size] = part[...]
    send_ref[...] = dot_t(mine_ref[...], pair_ref[...]).astype(jnp.bfloat16)
    keep_ref[...] = dot_t(mine_ref[...], own_ref[...]).astype(jnp.bfloat16)


def value_kernel(keep_ref, recv_ref, low_t_ref, go_ref, own_ref, away_ref):
    half = keep_ref.shape[0]
    go_ref[:half] = keep_ref[...]
    go_ref[half:] = recv_ref[...]
    total = jnp.zeros((2 * half, HD), jnp.float32)
    for head in range(low_t_ref.shape[0]):
        total = total + dot_n(low_t_ref[head], go_ref[:, head * HD : (head + 1) * HD])
    total = total.astype(jnp.bfloat16)
    own_ref[...] = total[:half]
    away_ref[...] = total[half:]


def partial_kernel(gv_ref, gv_pair_ref, own_ref, pair_ref, *outs):
    total = dot_t(gv_ref[...], own_ref[...]) + dot_t(gv_pair_ref[...], pair_ref[...])
    total = total.astype(jnp.bfloat16)
    size = outs[0].shape[0]
    for i, out in enumerate(outs):
        at = (i + 1) % len(outs) * size
        out[...] = total[at : at + size]


def sum_kernel(*refs):
    *parts, total_ref = refs
    total = parts[0][...].astype(jnp.float32)
    for ref in parts[1:]:
        total = total + ref[...].astype(jnp.float32)
    total_ref[...] = total


def lines_kernel(wait, own_ref, other_ref, pair_ref):
    wait()
    order_kernel(own_ref, other_ref, pair_ref)


def norm_kernel(a_ref, b_ref, x_ref, gain_ref, even_ref, odd_ref, new_ref, mine_ref):
    rows = mine_ref.shape[0]
    first = lax.axis_index("tensor") % 2 == 0
    inputs = x_ref[...].astype(jnp.float32)
    inverse = lax.rsqrt(jnp.mean(inputs * inputs, -1, keepdims=True) + EPS)
    scaled = (a_ref[...] + b_ref[...]) * gain_ref[...].astype(jnp.float32)
    inner = jnp.mean(scaled * inputs, -1, keepdims=True)
    current = jnp.where(first, even_ref[...], odd_ref[...]).astype(jnp.float32)
    updated = (
        current + inverse * scaled - inputs * (inverse * inverse * inverse * inner)
    ).astype(jnp.bfloat16)
    new_ref[...] = updated
    mine_ref[...] = jnp.where(first, updated[:rows], updated[rows:])


def staged_kernel(kernel, picks, count, *refs):
    sources = refs[: len(picks)]
    outs = refs[-count - len(picks) - 1 : -len(picks) - 1]
    held, sems = refs[-len(picks) - 1 : -1], refs[-1]
    copies = [
        pltpu.make_async_copy(source if pick is None else source.at[pick], slot, sems.at[i])
        for i, (pick, source, slot) in enumerate(zip(picks, sources, held))
    ]
    for copy in copies:
        copy.start()

    def wait():
        for copy in copies:
            copy.wait()

    kernel(wait, *held, *outs)


def choose_kernel(tick, plan_ref, *refs):
    chosen = plan_ref[tick, 0]
    count = (len(refs) - 2) // 2
    sources, outs, sems = refs[:count], refs[count + 1 : -1], refs[-1]
    copies = []
    for i, (source, out) in enumerate(zip(sources, outs)):
        view = source.at[chosen, 0] if len(source.shape) == 4 else source.at[chosen]
        copies.append(pltpu.make_async_copy(view, out, sems.at[i]))
    for copy in copies:
        copy.start()
    for copy in copies:
        copy.wait()


FAR = pl.BlockSpec(memory_space=pltpu.HBM)
LIGHT = pl.CostEstimate(flops=1000, bytes_accessed=1000, transcendentals=0)
PARAMS = pltpu.CompilerParams(vmem_limit_bytes=24 * 1024 * 1024)


def staged(kernel, shapes, operands, gate):
    arrays, picks = [pair[0] for pair in operands], [pair[1] for pair in operands]
    slots = [
        pltpu.VMEM(array.shape if pick is None else array.shape[1:], array.dtype)
        for array, pick in operands
    ]
    return pl.pallas_call(
        functools.partial(staged_kernel, kernel, picks, len(shapes)),
        out_shape=shapes,
        in_specs=[FAR] * (len(arrays) + 1),
        out_specs=[VMEM] * len(shapes),
        scratch_shapes=slots + [pltpu.SemaphoreType.DMA((len(picks),))],
        cost_estimate=LIGHT,
        compiler_params=PARAMS,
    )(*arrays, gate)


def on_core(kernel, shapes, operands, scratch=()):
    return pl.pallas_call(
        kernel,
        out_shape=shapes,
        in_specs=[VMEM] * len(operands),
        out_specs=[VMEM] * len(shapes),
        scratch_shapes=list(scratch),
        cost_estimate=LIGHT,
        compiler_params=PARAMS,
    )(*operands)


def choose(tick, plan, weights, gate):
    shapes = [jax.ShapeDtypeStruct(item.shape[-2:], item.dtype) for item in weights]
    return pl.pallas_call(
        functools.partial(choose_kernel, tick),
        out_shape=shapes,
        in_specs=[pl.BlockSpec(memory_space=pltpu.SMEM)] + [FAR] * (len(weights) + 1),
        out_specs=[VMEM] * len(shapes),
        scratch_shapes=[pltpu.SemaphoreType.DMA((len(weights),))],
        cost_estimate=LIGHT,
        compiler_params=PARAMS,
    )(plan, *weights, gate)


def bf16(*shape):
    return jax.ShapeDtypeStruct(shape, jnp.bfloat16)


def f32(*shape):
    return jax.ShapeDtypeStruct(shape, jnp.float32)


def on_device(cot_in, saved_inputs, queries, keys, values, docs, plan, w_value, w_out, norm_gain):
    phases = lax.axis_size("section")
    members = lax.axis_size("tensor")
    chips = members // 2
    far = chips // 2
    rows, width = cot_in.shape
    length = rows * members
    half = length // 2
    heads = queries.shape[2] // HD
    hold = lax.optimization_barrier

    def swap(block):
        return lax.ppermute(block, "tensor", [(t, t ^ 1) for t in range(members)])

    def along(block, by):
        return lax.ppermute(block, "section", [(s, (s + by) % phases) for s in range(phases)])

    def hop(block, steps, back):
        pairs = []
        for section in range(phases):
            for z in range(chips):
                up, down = (z + steps) % chips, (z - steps) % chips if steps != far else z
                base = (section - back) % phases * members
                pairs.append((section * members + 2 * z, base + 2 * up))
                pairs.append((section * members + 2 * z + 1, base + 2 * down + 1))
        return lax.ppermute(block, ("section", "tensor"), pairs)

    def attention_ready(tick, gate):
        return staged(
            functools.partial(softmax_kernel, rows, chips),
            [f32(heads, length, length), bf16(heads, length, length)],
            [(item, tick) for item in (queries, keys, docs)],
            gate,
        )

    def grads(chance, grad_out, tick, gate):
        return staged(
            functools.partial(grads_kernel, rows, chips),
            [bf16(*queries.shape[1:]), bf16(*keys.shape[1:])],
            [(chance, None), (grad_out, None)]
            + [(item, tick) for item in (queries, keys, values)],
            gate,
        )

    def gather(pair, back, done):
        moved = [hop(pair, k, back) for k in (far, *range(1, far))]
        return hold((moved, done))

    def scatter(blocks, done):
        steps = list(range(far - 1, 0, -1)) + [far]
        moved = [hop(block, k, 0) for block, k in zip(blocks, steps)]
        return hold((moved, done))

    other = swap(cot_in)
    other, *later = hold((other, w_value, w_out))
    away_value, away_out = (swap(item) for item in later)
    pair = on_core(order_kernel, [bf16(2 * rows, width)], (cot_in, other))[0]
    weights = [w_out, away_out, w_value, away_value, norm_gain]
    query_list = []
    key_list = []
    for tick in range(TICKS):
        last = tick == TICKS - 1
        if tick == 0:
            done = attention_ready(0, pair), choose(0, plan, weights, pair)
        elif tick == 1:
            done = attention_ready(2, pair)
        else:
            done = ()
        parts, done = gather(pair, 1 if tick else 0, done)
        if tick == 0:
            ready, chosen = done
        elif tick == 1:
            ready_last = done
        own_out, pair_out, own_value, pair_value, gain = chosen
        chance, low_t = ready
        keep, send = on_core(
            out_kernel,
            [bf16(half, heads * HD)] * 2,
            [*parts, own_out, pair_out],
            [pltpu.VMEM((half, width), jnp.bfloat16)],
        )
        grad_out, value_keep, value_send = on_core(
            value_kernel,
            [bf16(length, heads * HD), bf16(half, HD), bf16(half, HD)],
            (keep, swap(send), low_t),
        )
        blocks = on_core(
            partial_kernel,
            [bf16(2 * rows, width)] * far,
            (value_keep, swap(value_send), own_value, pair_value),
        )
        gate = blocks[-1]
        found = grads(chance, grad_out, tick, gate)
        if tick:
            even, odd = swap(parts[0]), parts[0]
        else:
            even = odd = pair
            later, _ = hold((saved_inputs, gate))
            inputs_away = swap(later)
        lines = staged(
            lines_kernel,
            [bf16(2 * rows, width)],
            [(saved_inputs, tick), (inputs_away, tick)],
            gate,
        )[0]
        if last:
            done = jnp.stack(query_list + [found[0]]), jnp.stack(key_list + [found[1]])
        elif tick == 0:
            done = found, choose(1, plan, weights, gate), attention_ready(1, gate), inputs_away
        else:
            done = found, choose(2, plan, weights, gate)
        done = done, lines, even
        terms, (done, lines, even) = scatter(blocks, done)
        total = on_core(sum_kernel, [f32(2 * rows, width)], terms)[0]
        if last:
            query, key = done
        else:
            found, chosen = done[:2]
            if tick == 0:
                ready, inputs_away = done[2:]
            else:
                ready = ready_last
            query_list.append(found[0])
            key_list.append(found[1])
        pair, mine = on_core(
            norm_kernel,
            [bf16(2 * rows, width), bf16(rows, width)],
            (total, swap(total), lines, gain, even, odd),
        )
    return along(mine, -1), query, key


def solution(mesh):
    return jax.shard_map(
        on_device,
        mesh=mesh,
        in_specs=(
            P(("section", "tensor"), None),
            P(None, ("section", "tensor"), None),
            P(None, "section", "tensor"),
            P(None, "section", "tensor"),
            P(None, "section", "tensor"),
            P(None, "section", None),
            P(None, "section"),
            P(None, "section", None, "tensor"),
            P(None, "section", "tensor", None),
            P(None, "section", None),
        ),
        out_specs=(
            P(("section", "tensor"), None),
            P(None, "section", "tensor"),
            P(None, "section", "tensor"),
        ),
        check_vma=False,
    )
```

time: 176 us -> 163 us (0.926)
  Pallas kernels: 38.7 us -> 24.3 us
  starting transfers between devices: 57.6 us -> 68 us
  local copies, waits for them, and re-layouts: 13.3 us -> 8.55 us
  waiting for transfers between devices: 62.9 us -> 58.8 us
    pallas_call x22 -> x25, Pallas kernels: 34.6 us -> 20.2 us  [the longest x16 10.3 us: on_core(): pl.pallas_call(kernel, out_shape=shapes, in_specs=[VMEM] * len(operands),...]
    ppermute x26 -> x24, starting transfers between devices: 55.6 us -> 65.1 us  [hop(): return lax.ppermute(block, ('section', 'tensor'), pairs)]
    unnamed x65 -> x29, local copies, waits for them, and re-layouts: 13.3 us -> 8.55 us
    ppermute x26 -> x24, waiting for transfers between devices: 42.3 us -> 38.8 us  [hop(): return lax.ppermute(block, ('section', 'tensor'), pairs)]
    ppermute x13 -> x15, waiting for transfers between devices: 12.9 us -> 12.4 us  [swap(): return lax.ppermute(block, 'tensor', [(t, t ^ 1) for t in range(members)])]
  transfers between devices with their start and end apart: 40 -> 40, of which waited for: 17 -> 23; matrix products, arithmetic and copies ran while one was open for 2% -> 2% of each run, Pallas kernels for 12% -> 10%
where the time goes in v4:
time: 163 us; the launch traced here: 162 us
  starting transfers between devices  68 us (42%)
  waiting for transfers between devices  58.8 us (36%)
  Pallas kernels  24.3 us (15%)
  local copies, waits for them, and re-layouts  8.55 us (5%)
    ppermute x24, starting transfers between devices, hop(): return lax.ppermute(block, ('section', 'tensor'), pairs)  65.1 us
    ppermute x24, waiting for transfers between devices, hop(): return lax.ppermute(block, ('section', 'tensor'), pairs)  38.8 us
    ppermute x15, waiting for transfers between devices, swap(): return lax.ppermute(block, 'tensor', [(t, t ^ 1) for t in range(members)])  12.4 us
    pallas_call x16, Pallas kernels, on_core(): pl.pallas_call(kernel, out_shape=shapes, in_specs=[VMEM] * len(operands),...  10.3 us
    pallas_call x9, Pallas kernels, staged(): pl.pallas_call(functools.partial(staged_kernel, kernel, picks, len(shapes...  9.89 us
    unnamed x29, local copies, waits for them, and re-layouts  8.55 us
    ppermute x1, waiting for transfers between devices, along(): lax.ppermute(block, 'section', [(s, (s + by) % phases) for s in range(pha...  7.67 us
    pallas_call x3, Pallas kernels, choose(): pl.pallas_call(functools.partial(choose_kernel, tick), out_shape=shapes,...  4.07 us
  transfers between devices with their start and end apart: 40, of which 23 were waited for; matrix products, arithmetic and copies ran while one was open for 2% of the time, Pallas kernels for 10%

profile of v4, /device:TPU:30, one launch (start us, length us, event | category | flops | bytes accessed | tf_op | source)
XLA Modules:
  0.0 162.3 jit_solution(7071087916669753003)
XLA Ops:
  0.7 1.5 collective-permute-done.b_ref
  4.3 4.6 %collective-permute-start.4 = (bf16[32,2304]{1,0:T(8,128)(2,1)}, bf16[32,2304]{1,0:T(8,128)(2,1)}, u32[]{:S(2)}, u32[]{:S(2)}) collective-permute-start(bf16[32,2304]{1,0:T(8,128)(2,1)} %shard_map.121.refs_3_.refs_5_.even_ref.odd_ref), channel_id=1, source_target_pairs={{0,6},{1,11},{2,8},{3,13},{4,10},{5,15},{6,12},{7,1},{8,14},{9,3},... | collective-permute-start | bytes 442376 | tf_op jit(solution)/shard_map/ppermute | solution.py:264
  8.9 3.6 %collective-permute-start.3 = (bf16[32,2304]{1,0:T(8,128)(2,1)}, bf16[32,2304]{1,0:T(8,128)(2,1)}, u32[]{:S(2)}, u32[]{:S(2)}) collective-permute-start(bf16[32,2304]{1,0:T(8,128)(2,1)} %shard_map.121.refs_3_.refs_5_.even_ref.odd_ref), channel_id=1, source_target_pairs={{0,4},{1,13},{2,6},{3,15},{4,8},{5,1},{6,10},{7,3},{8,12},{9,5},{1... | collective-permute-start | bytes 442376 | tf_op jit(solution)/shard_map/ppermute | solution.py:264
  13.5 4.2 %collective-permute-start.1 = (bf16[32,2304]{1,0:T(8,128)(2,1)}, bf16[32,2304]{1,0:T(8,128)(2,1)}, u32[]{:S(2)}, u32[]{:S(2)}) collective-permute-start(bf16[32,2304]{1,0:T(8,128)(2,1)} %shard_map.121.refs_3_.refs_5_.even_ref.odd_ref), channel_id=1, source_target_pairs={{0,8},{1,1},{2,10},{3,3},{4,12},{5,5},{6,14},{7,7},{8,0},{9,9},{10... | collective-permute-start | bytes 442376 | tf_op jit(solution)/shard_map/ppermute | solution.py:264
  21.8 1.6 shard_map.122
  23.4 1.7 %copy-done = bf16[2,1,256,2304]{3,2,1,0:T(8,128)(2,1)S(1)} copy-done((bf16[2,1,256,2304]{3,2,1,0:T(8,128)(2,1)S(1)}, bf16[2,1,256,2304]{3,2,1,0:T(8,128)(2,1)}, u32[]{:S(2)}) %copy-start) | copy-done | bytes 2359320
  25.1 1.3 copy-done.4
  26.4 1.4 shard_map.123
  27.8 2.1 %shard_map.124 = (bf16[128,256]{1,0:T(8,128)(2,1)S(1)}, bf16[128,256]{1,0:T(8,128)(2,1)S(1)}) custom-call(bf16[32,2304]{1,0:T(8,128)(2,1)} %collective-permute-done.1.refs_0_, bf16[32,2304]{1,0:T(8,128)(2,1)} %collective-permute-done.2.refs_1_, bf16[32,2304]{1,0:T(8,128)(2,1)} %collective-permute-done.3.refs_2_, ...), custom_call_target="tpu_custom_call" | custom-call | flops 1000 | bytes 1000 | tf_op jit(solution)/shard_map/pallas_call | solution.py:207
  33.5 3.2 %collective-permute-start.9 = (bf16[32,2304]{1,0:T(8,128)(2,1)S(1)}, bf16[32,2304]{1,0:T(8,128)(2,1)S(1)}, u32[]{:S(2)}, u32[]{:S(2)}) collective-permute-start(bf16[32,2304]{1,0:T(8,128)(2,1)S(1)} %get-tuple-element.145), channel_id=1, source_target_pairs={{0,6},{1,11},{2,8},{3,13},{4,10},{5,15},{6,12},{7,1},{8,14},{9,3},... | collective-permute-start | bytes 442376 | tf_op jit(solution)/shard_map/ppermute | solution.py:264
  36.7 1.5 collective-permute-start.10
  38.2 6.6 %collective-permute-start.12 = (bf16[32,2304]{1,0:T(8,128)(2,1)S(1)}, bf16[32,2304]{1,0:T(8,128)(2,1)S(1)}, u32[]{:S(2)}, u32[]{:S(2)}) collective-permute-start(bf16[32,2304]{1,0:T(8,128)(2,1)S(1)} %get-tuple-element.148.refs_5_.refs_3_.refs_2_), channel_id=1, source_target_pairs={{0,8},{1,1},{2,10},{3,3},{4,12},{5,5},{6,14},{7,7},{8,0},{9,9},{10... | collective-permute-start | bytes 442376 | tf_op jit(solution)/shard_map/ppermute | solution.py:264
  44.8 1.6 %shard_map.129 = (f32[2,256,256]{2,1,0:T(8,128)S(1)}, bf16[2,256,256]{2,1,0:T(8,128)(2,1)S(1)}) custom-call(bf16[3,256,256]{2,1,0:T(8,128)(2,1)S(1)} %copy-done.3, bf16[3,256,128]{2,1,0:T(8,128)(2,1)S(1)} %copy-done.7, s32[3,1,256]{2,1,0:T(1,128)S(1)} %copy-done.12, bf16[32,2304]{1,0:T(8,128)(2,1)S(1)} %get-tuple-element.148.refs_5_.refs_3_.refs_2_), custom_call_target="tpu_custom_call" | custom-call | flops 1000 | bytes 1000 | tf_op jit(solution)/shard_map/pallas_call | solution.py:195
  46.5 1.5 shard_map.127
  48.0 1.4 shard_map.128
  49.6 3.4 %collective-permute-done.11.refs_2_ = bf16[32,2304]{1,0:T(8,128)(2,1)S(1)} collective-permute-done((bf16[32,2304]{1,0:T(8,128)(2,1)S(1)}, bf16[32,2304]{1,0:T(8,128)(2,1)S(1)}, u32[]{:S(2)}, u32[]{:S(2)}) %collective-permute-start.11) | collective-permute-done | bytes 147488 | tf_op jit(solution)/shard_map/ppermute | solution.py:264
  53.2 1.6 collective-permute-done.14.b_ref
  54.7 1.8 %shard_map.132 = (bf16[32,2304]{1,0:T(8,128)(2,1)S(1)}, bf16[16,2304]{1,0:T(8,128)(2,1)}) custom-call(f32[32,2304]{1,0:T(8,128)S(1)} %shard_map.131.a_ref, f32[32,2304]{1,0:T(8,128)S(1)} %collective-permute-done.14.b_ref, bf16[32,2304]{1,0:T(8,128)(2,1)S(1)} %shard_map.130.x_ref, bf16[1,2304]{1,0:T(2,128)(2,1)S(1)} %get-tuple-element.166.gain_ref, ...), custom_call_target="tpu_custom_call" | custom-call | flops 1000 | bytes 1000 | tf_op jit(solution)/shard_map/pallas_call | solution.py:207
  56.5 1.7 %collective-permute-start.18 = (bf16[32,2304]{1,0:T(8,128)(2,1)S(1)}, bf16[32,2304]{1,0:T(8,128)(2,1)S(1)}, u32[]{:S(2)}, u32[]{:S(2)}) collective-permute-start(bf16[32,2304]{1,0:T(8,128)(2,1)S(1)} %get-tuple-element.168.refs_3_), channel_id=1, source_target_pairs={{0,246},{1,251},{2,248},{3,253},{4,250},{5,255},{6,252},{7,241},{8... | collective-permute-start | bytes 442376 | tf_op jit(solution)/shard_map/ppermute | solution.py:264
  58.2 1.9 %collective-permute-start.17 = (bf16[32,2304]{1,0:T(8,128)(2,1)S(1)}, bf16[32,2304]{1,0:T(8,128)(2,1)S(1)}, u32[]{:S(2)}, u32[]{:S(2)}) collective-permute-start(bf16[32,2304]{1,0:T(8,128)(2,1)S(1)} %get-tuple-element.168.refs_3_), channel_id=1, source_target_pairs={{0,244},{1,253},{2,246},{3,255},{4,248},{5,241},{6,250},{7,243},{8... | collective-permute-start | bytes 442376 | tf_op jit(solution)/shard_map/ppermute | solution.py:264
  60.0 2.6 %collective-permute-start.16 = (bf16[32,2304]{1,0:T(8,128)(2,1)S(1)}, bf16[32,2304]{1,0:T(8,128)(2,1)S(1)}, u32[]{:S(2)}, u32[]{:S(2)}) collective-permute-start(bf16[32,2304]{1,0:T(8,128)(2,1)S(1)} %get-tuple-element.168.refs_3_), channel_id=1, source_target_pairs={{0,242},{1,255},{2,244},{3,241},{4,246},{5,243},{6,248},{7,245},{8... | collective-permute-start | bytes 442376 | tf_op jit(solution)/shard_map/ppermute | solution.py:264
  62.6 4.2 %collective-permute-start.15 = (bf16[32,2304]{1,0:T(8,128)(2,1)S(1)}, bf16[32,2304]{1,0:T(8,128)(2,1)S(1)}, u32[]{:S(2)}, u32[]{:S(2)}) collective-permute-start(bf16[32,2304]{1,0:T(8,128)(2,1)S(1)} %get-tuple-element.168.refs_3_), channel_id=1, source_target_pairs={{0,248},{1,241},{2,250},{3,243},{4,252},{5,245},{6,254},{7,247},{8... | collective-permute-start | bytes 442376 | tf_op jit(solution)/shard_map/ppermute | solution.py:264
  66.9 1.6 shard_map.133
  68.5 1.3 collective-permute-done.18.refs_3_
  69.7 3.7 %collective-permute-done.17.refs_2_ = bf16[32,2304]{1,0:T(8,128)(2,1)S(1)} collective-permute-done((bf16[32,2304]{1,0:T(8,128)(2,1)S(1)}, bf16[32,2304]{1,0:T(8,128)(2,1)S(1)}, u32[]{:S(2)}, u32[]{:S(2)}) %collective-permute-start.17) | collective-permute-done | bytes 147488 | tf_op jit(solution)/shard_map/ppermute | solution.py:264
  73.4 5.4 %collective-permute-done.16.refs_1_ = bf16[32,2304]{1,0:T(8,128)(2,1)S(1)} collective-permute-done((bf16[32,2304]{1,0:T(8,128)(2,1)S(1)}, bf16[32,2304]{1,0:T(8,128)(2,1)S(1)}, u32[]{:S(2)}, u32[]{:S(2)}) %collective-permute-start.16) | collective-permute-done | bytes 147488 | tf_op jit(solution)/shard_map/ppermute | solution.py:264
  79.9 1.2 collective-permute-done.19.recv_ref
  83.1 3.1 %collective-permute-start.21 = (bf16[32,2304]{1,0:T(8,128)(2,1)S(1)}, bf16[32,2304]{1,0:T(8,128)(2,1)S(1)}, u32[]{:S(2)}, u32[]{:S(2)}) collective-permute-start(bf16[32,2304]{1,0:T(8,128)(2,1)S(1)} %get-tuple-element.184), channel_id=1, source_target_pairs={{0,6},{1,11},{2,8},{3,13},{4,10},{5,15},{6,12},{7,1},{8,14},{9,3},... | collective-permute-start | bytes 442376 | tf_op jit(solution)/shard_map/ppermute | solution.py:264
  86.6 3.2 %collective-permute-start.23 = (bf16[32,2304]{1,0:T(8,128)(2,1)S(1)}, bf16[32,2304]{1,0:T(8,128)(2,1)S(1)}, u32[]{:S(2)}, u32[]{:S(2)}) collective-permute-start(bf16[32,2304]{1,0:T(8,128)(2,1)S(1)} %get-tuple-element.186), channel_id=1, source_target_pairs={{0,2},{1,15},{2,4},{3,1},{4,6},{5,3},{6,8},{7,5},{8,10},{9,7},{10,... | collective-permute-start | bytes 442376 | tf_op jit(solution)/shard_map/ppermute | solution.py:264
  89.8 3.8 %collective-permute-start.24 = (bf16[32,2304]{1,0:T(8,128)(2,1)S(1)}, bf16[32,2304]{1,0:T(8,128)(2,1)S(1)}, u32[]{:S(2)}, u32[]{:S(2)}) collective-permute-start(bf16[32,2304]{1,0:T(8,128)(2,1)S(1)} %get-tuple-element.187.refs_5_.refs_2_), channel_id=1, source_target_pairs={{0,8},{1,1},{2,10},{3,3},{4,12},{5,5},{6,14},{7,7},{8,0},{9,9},{10... | collective-permute-start | bytes 442376 | tf_op jit(solution)/shard_map/ppermute | solution.py:264
  93.9 1.5 shard_map.137
  95.4 1.4 shard_map.138
  97.1 1.5 collective-permute-done.23.refs_2_
  98.6 3.3 %collective-permute-done.24.refs_3_ = bf16[32,2304]{1,0:T(8,128)(2,1)S(1)} collective-permute-done((bf16[32,2304]{1,0:T(8,128)(2,1)S(1)}, bf16[32,2304]{1,0:T(8,128)(2,1)S(1)}, u32[]{:S(2)}, u32[]{:S(2)}) %collective-permute-start.24) | collective-permute-done | bytes 147488 | tf_op jit(solution)/shard_map/ppermute | solution.py:264
  102.1 1.6 collective-permute-done.26.b_ref
  104.5 3.4 %collective-permute-start.28 = (bf16[32,2304]{1,0:T(8,128)(2,1)S(1)}, bf16[32,2304]{1,0:T(8,128)(2,1)S(1)}, u32[]{:S(2)}, u32[]{:S(2)}) collective-permute-start(bf16[32,2304]{1,0:T(8,128)(2,1)S(1)} %get-tuple-element.205), channel_id=1, source_target_pairs={{0,242},{1,255},{2,244},{3,241},{4,246},{5,243},{6,248},{7,245},{8... | collective-permute-start | bytes 442376 | tf_op jit(solution)/shard_map/ppermute | solution.py:264
  107.9 6.5 %collective-permute-start.27 = (bf16[32,2304]{1,0:T(8,128)(2,1)S(1)}, bf16[32,2304]{1,0:T(8,128)(2,1)S(1)}, u32[]{:S(2)}, u32[]{:S(2)}) collective-permute-start(bf16[32,2304]{1,0:T(8,128)(2,1)S(1)} %get-tuple-element.205), channel_id=1, source_target_pairs={{0,248},{1,241},{2,250},{3,243},{4,252},{5,245},{6,254},{7,247},{8... | collective-permute-start | bytes 442376 | tf_op jit(solution)/shard_map/ppermute | solution.py:264
  114.5 2.6 %collective-permute-done.30.refs_3_ = bf16[32,2304]{1,0:T(8,128)(2,1)S(1)} collective-permute-done((bf16[32,2304]{1,0:T(8,128)(2,1)S(1)}, bf16[32,2304]{1,0:T(8,128)(2,1)S(1)}, u32[]{:S(2)}, u32[]{:S(2)}) %collective-permute-start.30) | collective-permute-done | bytes 147488 | tf_op jit(solution)/shard_map/ppermute | solution.py:264
  117.1 5.8 %collective-permute-done.29.refs_2_ = bf16[32,2304]{1,0:T(8,128)(2,1)S(1)} collective-permute-done((bf16[32,2304]{1,0:T(8,128)(2,1)S(1)}, bf16[32,2304]{1,0:T(8,128)(2,1)S(1)}, u32[]{:S(2)}, u32[]{:S(2)}) %collective-permute-start.29) | collective-permute-done | bytes 147488 | tf_op jit(solution)/shard_map/ppermute | solution.py:264
  122.9 1.6 %collective-permute-done.28.refs_1_ = bf16[32,2304]{1,0:T(8,128)(2,1)S(1)} collective-permute-done((bf16[32,2304]{1,0:T(8,128)(2,1)S(1)}, bf16[32,2304]{1,0:T(8,128)(2,1)S(1)}, u32[]{:S(2)}, u32[]{:S(2)}) %collective-permute-start.28) | collective-permute-done | bytes 147488 | tf_op jit(solution)/shard_map/ppermute | solution.py:264
  124.5 5.2 %collective-permute-done.27.refs_0_.odd_ref = bf16[32,2304]{1,0:T(8,128)(2,1)S(1)} collective-permute-done((bf16[32,2304]{1,0:T(8,128)(2,1)S(1)}, bf16[32,2304]{1,0:T(8,128)(2,1)S(1)}, u32[]{:S(2)}, u32[]{:S(2)}) %collective-permute-start.27) | collective-permute-done | bytes 147488 | tf_op jit(solution)/shard_map/ppermute | solution.py:264
  134.0 1.6 collective-permute-start.34
  135.6 1.9 %collective-permute-start.35 = (bf16[32,2304]{1,0:T(8,128)(2,1)S(1)}, bf16[32,2304]{1,0:T(8,128)(2,1)S(1)}, u32[]{:S(2)}, u32[]{:S(2)}) collective-permute-start(bf16[32,2304]{1,0:T(8,128)(2,1)S(1)} %get-tuple-element.221), channel_id=1, source_target_pairs={{0,2},{1,15},{2,4},{3,1},{4,6},{5,3},{6,8},{7,5},{8,10},{9,7},{10,... | collective-permute-start | bytes 442376 | tf_op jit(solution)/shard_map/ppermute | solution.py:264
  137.5 6.0 %collective-permute-start.36 = (bf16[32,2304]{1,0:T(8,128)(2,1)S(1)}, bf16[32,2304]{1,0:T(8,128)(2,1)S(1)}, u32[]{:S(2)}, u32[]{:S(2)}) collective-permute-start(bf16[32,2304]{1,0:T(8,128)(2,1)S(1)} %get-tuple-element.222.refs_5_.refs_2_), channel_id=1, source_target_pairs={{0,8},{1,1},{2,10},{3,3},{4,12},{5,5},{6,14},{7,7},{8,0},{9,9},{10... | collective-permute-start | bytes 442376 | tf_op jit(solution)/shard_map/ppermute | solution.py:264
  143.5 1.5 shard_map.145
  146.7 4.7 %collective-permute-done.35.refs_2_ = bf16[32,2304]{1,0:T(8,128)(2,1)S(1)} collective-permute-done((bf16[32,2304]{1,0:T(8,128)(2,1)S(1)}, bf16[32,2304]{1,0:T(8,128)(2,1)S(1)}, u32[]{:S(2)}, u32[]{:S(2)}) %collective-permute-start.35) | collective-permute-done | bytes 147488 | tf_op jit(solution)/shard_map/ppermute | solution.py:264
  151.5 1.6 collective-permute-done.38.b_ref
  154.0 7.7 %collective-permute-done.39 = bf16[16,2304]{1,0:T(8,128)(2,1)S(1)} collective-permute-done((bf16[16,2304]{1,0:T(8,128)(2,1)S(1)}, bf16[16,2304]{1,0:T(8,128)(2,1)S(1)}, u32[]{:S(2)}, u32[]{:S(2)}) %collective-permute-start.39) | collective-permute-done | bytes 73760 | tf_op jit(solution)/shard_map/ppermute | solution.py:254
  (91 shorter events, 23.9 us)
Async XLA Ops:
  0.6 1.6 collective-permute-start
  2.2 21.2 %collective-permute-start.5 = (bf16[2,1,256,2304]{3,2,1,0:T(8,128)(2,1)}, bf16[2,1,256,2304]{3,2,1,0:T(8,128)(2,1)S(1)}, u32[]{:S(2)}, u32[]{:S(2)}) collective-permute-start(bf16[2,1,256,2304]{3,2,1,0:T(8,128)(2,1)} %refs_0_.15), channel_id=1, source_target_pairs={{0,1},{1,0},{2,3},{3,2},{4,5},{5,4},{6,7},{7,6},{8,9},{9,8},{10,11... | collective-permute-start | bytes 7077896 | tf_op jit(solution)/shard_map/ppermute | solution.py:251
  2.4 11.1 %collective-permute-start.6 = (bf16[2,1,2304,128]{3,2,1,0:T(8,128)(2,1)}, bf16[2,1,2304,128]{3,2,1,0:T(8,128)(2,1)S(1)}, u32[]{:S(2)}, u32[]{:S(2)}) collective-permute-start(bf16[2,1,2304,128]{3,2,1,0:T(8,128)(2,1)} %refs_2_.16), channel_id=1, source_target_pairs={{0,1},{1,0},{2,3},{3,2},{4,5},{5,4},{6,7},{7,6},{8,9},{9,8},{10,11... | collective-permute-start | bytes 3538952 | tf_op jit(solution)/shard_map/ppermute | solution.py:251
  4.3 23.5 %collective-permute-start.4 = (bf16[32,2304]{1,0:T(8,128)(2,1)}, bf16[32,2304]{1,0:T(8,128)(2,1)}, u32[]{:S(2)}, u32[]{:S(2)}) collective-permute-start(bf16[32,2304]{1,0:T(8,128)(2,1)} %shard_map.121.refs_3_.refs_5_.even_ref.odd_ref), channel_id=1, source_target_pairs={{0,6},{1,11},{2,8},{3,13},{4,10},{5,15},{6,12},{7,1},{8,14},{9,3},... | collective-permute-start | bytes 442376 | tf_op jit(solution)/shard_map/ppermute | solution.py:264
  8.9 18.8 %collective-permute-start.3 = (bf16[32,2304]{1,0:T(8,128)(2,1)}, bf16[32,2304]{1,0:T(8,128)(2,1)}, u32[]{:S(2)}, u32[]{:S(2)}) collective-permute-start(bf16[32,2304]{1,0:T(8,128)(2,1)} %shard_map.121.refs_3_.refs_5_.even_ref.odd_ref), channel_id=1, source_target_pairs={{0,4},{1,13},{2,6},{3,15},{4,8},{5,1},{6,10},{7,3},{8,12},{9,5},{1... | collective-permute-start | bytes 442376 | tf_op jit(solution)/shard_map/ppermute | solution.py:264
  12.5 15.3 %collective-permute-start.2 = (bf16[32,2304]{1,0:T(8,128)(2,1)}, bf16[32,2304]{1,0:T(8,128)(2,1)}, u32[]{:S(2)}, u32[]{:S(2)}) collective-permute-start(bf16[32,2304]{1,0:T(8,128)(2,1)} %shard_map.121.refs_3_.refs_5_.even_ref.odd_ref), channel_id=1, source_target_pairs={{0,2},{1,15},{2,4},{3,1},{4,6},{5,3},{6,8},{7,5},{8,10},{9,7},{10,... | collective-permute-start | bytes 442376 | tf_op jit(solution)/shard_map/ppermute | solution.py:264
  13.5 14.3 %collective-permute-start.1 = (bf16[32,2304]{1,0:T(8,128)(2,1)}, bf16[32,2304]{1,0:T(8,128)(2,1)}, u32[]{:S(2)}, u32[]{:S(2)}) collective-permute-start(bf16[32,2304]{1,0:T(8,128)(2,1)} %shard_map.121.refs_3_.refs_5_.even_ref.odd_ref), channel_id=1, source_target_pairs={{0,8},{1,1},{2,10},{3,3},{4,12},{5,5},{6,14},{7,7},{8,0},{9,9},{10... | collective-permute-start | bytes 442376 | tf_op jit(solution)/shard_map/ppermute | solution.py:264
  23.4 1.7 %copy-start = (bf16[2,1,256,2304]{3,2,1,0:T(8,128)(2,1)S(1)}, bf16[2,1,256,2304]{3,2,1,0:T(8,128)(2,1)}, u32[]{:S(2)}) copy-start(bf16[2,1,256,2304]{3,2,1,0:T(8,128)(2,1)} %refs_0_.15) | copy-start | bytes 7077892
  27.8 5.5 %copy-start.8 = (bf16[3,16,2304]{2,1,0:T(8,128)(2,1)S(1)}, bf16[3,16,2304]{2,1,0:T(8,128)(2,1)}, u32[]{:S(2)}) copy-start(bf16[3,16,2304]{2,1,0:T(8,128)(2,1)} %refs_0_.17) | copy-start | bytes 663556
  27.8 17.0 %copy-start.7 = (bf16[3,256,128]{2,1,0:T(8,128)(2,1)S(1)}, bf16[3,256,128]{2,1,0:T(8,128)(2,1)}, u32[]{:S(2)}) copy-start(bf16[3,256,128]{2,1,0:T(8,128)(2,1)} %refs_3_.5) | copy-start | bytes 589828
  27.8 18.7 %copy-start.9 = (bf16[3,256,128]{2,1,0:T(8,128)(2,1)S(1)}, bf16[3,256,128]{2,1,0:T(8,128)(2,1)}, u32[]{:S(2)}) copy-start(bf16[3,256,128]{2,1,0:T(8,128)(2,1)} %refs_4_.8) | copy-start | bytes 589828
  29.9 14.9 %copy-start.3 = (bf16[3,256,256]{2,1,0:T(8,128)(2,1)S(1)}, bf16[3,256,256]{2,1,0:T(8,128)(2,1)}, u32[]{:S(2)}) copy-start(bf16[3,256,256]{2,1,0:T(8,128)(2,1)} %refs_2_.17) | copy-start | bytes 1179652
  29.9 14.9 %copy-start.12 = (s32[3,1,256]{2,1,0:T(1,128)S(1)}, s32[3,1,256]{2,1,0:T(1,128)}, u32[]{:S(2)}) copy-start(s32[3,1,256]{2,1,0:T(1,128)} %refs_2_.14) | copy-start | bytes 9220
  29.9 1.3 collective-permute-start.7
  31.5 1.3 collective-permute-start.8
  32.8 15.2 %copy-start.1 = (bf16[2,1,256,2304]{3,2,1,0:T(8,128)(2,1)S(1)}, bf16[2,1,256,2304]{3,2,1,0:T(8,128)(2,1)}, u32[]{:S(2)}) copy-start(bf16[2,1,256,2304]{3,2,1,0:T(8,128)(2,1)} %refs_0_.15) | copy-start | bytes 7077892
  33.3 14.7 %copy-start.5 = (bf16[2,1,2304,128]{3,2,1,0:T(8,128)(2,1)S(1)}, bf16[2,1,2304,128]{3,2,1,0:T(8,128)(2,1)}, u32[]{:S(2)}) copy-start(bf16[2,1,2304,128]{3,2,1,0:T(8,128)(2,1)} %refs_2_.16) | copy-start | bytes 3538948
  33.3 16.1 %collective-permute-start.13 = (bf16[3,16,2304]{2,1,0:T(8,128)(2,1)S(1)}, bf16[3,16,2304]{2,1,0:T(8,128)(2,1)S(1)}, u32[]{:S(2)}, u32[]{:S(2)}) collective-permute-start(bf16[3,16,2304]{2,1,0:T(8,128)(2,1)S(1)} %copy-done.8), channel_id=1, source_target_pairs={{0,1},{1,0},{2,3},{3,2},{4,5},{5,4},{6,7},{7,6},{8,9},{9,8},{10,11... | collective-permute-start | bytes 663560 | tf_op jit(solution)/shard_map/ppermute | solution.py:251
  33.5 16.1 %collective-permute-start.9 = (bf16[32,2304]{1,0:T(8,128)(2,1)S(1)}, bf16[32,2304]{1,0:T(8,128)(2,1)S(1)}, u32[]{:S(2)}, u32[]{:S(2)}) collective-permute-start(bf16[32,2304]{1,0:T(8,128)(2,1)S(1)} %get-tuple-element.145), channel_id=1, source_target_pairs={{0,6},{1,11},{2,8},{3,13},{4,10},{5,15},{6,12},{7,1},{8,14},{9,3},... | collective-permute-start | bytes 442376 | tf_op jit(solution)/shard_map/ppermute | solution.py:264
  36.7 12.9 %collective-permute-start.10 = (bf16[32,2304]{1,0:T(8,128)(2,1)S(1)}, bf16[32,2304]{1,0:T(8,128)(2,1)S(1)}, u32[]{:S(2)}, u32[]{:S(2)}) collective-permute-start(bf16[32,2304]{1,0:T(8,128)(2,1)S(1)} %get-tuple-element.146), channel_id=1, source_target_pairs={{0,4},{1,13},{2,6},{3,15},{4,8},{5,1},{6,10},{7,3},{8,12},{9,5},{1... | collective-permute-start | bytes 442376 | tf_op jit(solution)/shard_map/ppermute | solution.py:264
  38.1 14.8 %collective-permute-start.11 = (bf16[32,2304]{1,0:T(8,128)(2,1)S(1)}, bf16[32,2304]{1,0:T(8,128)(2,1)S(1)}, u32[]{:S(2)}, u32[]{:S(2)}) collective-permute-start(bf16[32,2304]{1,0:T(8,128)(2,1)S(1)} %get-tuple-element.147), channel_id=1, source_target_pairs={{0,2},{1,15},{2,4},{3,1},{4,6},{5,3},{6,8},{7,5},{8,10},{9,7},{10,... | collective-permute-start | bytes 442376 | tf_op jit(solution)/shard_map/ppermute | solution.py:264
  38.2 14.8 %collective-permute-start.12 = (bf16[32,2304]{1,0:T(8,128)(2,1)S(1)}, bf16[32,2304]{1,0:T(8,128)(2,1)S(1)}, u32[]{:S(2)}, u32[]{:S(2)}) collective-permute-start(bf16[32,2304]{1,0:T(8,128)(2,1)S(1)} %get-tuple-element.148.refs_5_.refs_3_.refs_2_), channel_id=1, source_target_pairs={{0,8},{1,1},{2,10},{3,3},{4,12},{5,5},{6,14},{7,7},{8,0},{9,9},{10... | collective-permute-start | bytes 442376 | tf_op jit(solution)/shard_map/ppermute | solution.py:264
  53.1 1.7 %collective-permute-start.14 = (f32[32,2304]{1,0:T(8,128)S(1)}, f32[32,2304]{1,0:T(8,128)S(1)}, u32[]{:S(2)}, u32[]{:S(2)}) collective-permute-start(f32[32,2304]{1,0:T(8,128)S(1)} %shard_map.131.a_ref), channel_id=1, source_target_pairs={{0,1},{1,0},{2,3},{3,2},{4,5},{5,4},{6,7},{7,6},{8,9},{9,8},{10,11... | collective-permute-start | bytes 884744 | tf_op jit(solution)/shard_map/ppermute | solution.py:251
  56.5 13.2 %collective-permute-start.18 = (bf16[32,2304]{1,0:T(8,128)(2,1)S(1)}, bf16[32,2304]{1,0:T(8,128)(2,1)S(1)}, u32[]{:S(2)}, u32[]{:S(2)}) collective-permute-start(bf16[32,2304]{1,0:T(8,128)(2,1)S(1)} %get-tuple-element.168.refs_3_), channel_id=1, source_target_pairs={{0,246},{1,251},{2,248},{3,253},{4,250},{5,255},{6,252},{7,241},{8... | collective-permute-start | bytes 442376 | tf_op jit(solution)/shard_map/ppermute | solution.py:264
  58.2 15.2 %collective-permute-start.17 = (bf16[32,2304]{1,0:T(8,128)(2,1)S(1)}, bf16[32,2304]{1,0:T(8,128)(2,1)S(1)}, u32[]{:S(2)}, u32[]{:S(2)}) collective-permute-start(bf16[32,2304]{1,0:T(8,128)(2,1)S(1)} %get-tuple-element.168.refs_3_), channel_id=1, source_target_pairs={{0,244},{1,253},{2,246},{3,255},{4,248},{5,241},{6,250},{7,243},{8... | collective-permute-start | bytes 442376 | tf_op jit(solution)/shard_map/ppermute | solution.py:264
  60.0 18.8 %collective-permute-start.16 = (bf16[32,2304]{1,0:T(8,128)(2,1)S(1)}, bf16[32,2304]{1,0:T(8,128)(2,1)S(1)}, u32[]{:S(2)}, u32[]{:S(2)}) collective-permute-start(bf16[32,2304]{1,0:T(8,128)(2,1)S(1)} %get-tuple-element.168.refs_3_), channel_id=1, source_target_pairs={{0,242},{1,255},{2,244},{3,241},{4,246},{5,243},{6,248},{7,245},{8... | collective-permute-start | bytes 442376 | tf_op jit(solution)/shard_map/ppermute | solution.py:264
  62.6 16.2 %collective-permute-start.15 = (bf16[32,2304]{1,0:T(8,128)(2,1)S(1)}, bf16[32,2304]{1,0:T(8,128)(2,1)S(1)}, u32[]{:S(2)}, u32[]{:S(2)}) collective-permute-start(bf16[32,2304]{1,0:T(8,128)(2,1)S(1)} %get-tuple-element.168.refs_3_), channel_id=1, source_target_pairs={{0,248},{1,241},{2,250},{3,243},{4,252},{5,245},{6,254},{7,247},{8... | collective-permute-start | bytes 442376 | tf_op jit(solution)/shard_map/ppermute | solution.py:264
  79.8 1.3 collective-permute-start.19
  81.3 1.3 collective-permute-start.20
  81.6 15.2 %collective-permute-start.25 = (bf16[32,2304]{1,0:T(8,128)(2,1)S(1)}, bf16[32,2304]{1,0:T(8,128)(2,1)S(1)}, u32[]{:S(2)}, u32[]{:S(2)}) collective-permute-start(bf16[32,2304]{1,0:T(8,128)(2,1)S(1)} %collective-permute-done.15.refs_0_.odd_ref), channel_id=1, source_target_pairs={{0,1},{1,0},{2,3},{3,2},{4,5},{5,4},{6,7},{7,6},{8,9},{9,8},{10,11... | collective-permute-start | bytes 442376 | tf_op jit(solution)/shard_map/ppermute | solution.py:251
  83.1 13.7 %collective-permute-start.21 = (bf16[32,2304]{1,0:T(8,128)(2,1)S(1)}, bf16[32,2304]{1,0:T(8,128)(2,1)S(1)}, u32[]{:S(2)}, u32[]{:S(2)}) collective-permute-start(bf16[32,2304]{1,0:T(8,128)(2,1)S(1)} %get-tuple-element.184), channel_id=1, source_target_pairs={{0,6},{1,11},{2,8},{3,13},{4,10},{5,15},{6,12},{7,1},{8,14},{9,3},... | collective-permute-start | bytes 442376 | tf_op jit(solution)/shard_map/ppermute | solution.py:264
  86.2 10.9 %collective-permute-start.22 = (bf16[32,2304]{1,0:T(8,128)(2,1)S(1)}, bf16[32,2304]{1,0:T(8,128)(2,1)S(1)}, u32[]{:S(2)}, u32[]{:S(2)}) collective-permute-start(bf16[32,2304]{1,0:T(8,128)(2,1)S(1)} %get-tuple-element.185), channel_id=1, source_target_pairs={{0,4},{1,13},{2,6},{3,15},{4,8},{5,1},{6,10},{7,3},{8,12},{9,5},{1... | collective-permute-start | bytes 442376 | tf_op jit(solution)/shard_map/ppermute | solution.py:264
  86.6 12.0 %collective-permute-start.23 = (bf16[32,2304]{1,0:T(8,128)(2,1)S(1)}, bf16[32,2304]{1,0:T(8,128)(2,1)S(1)}, u32[]{:S(2)}, u32[]{:S(2)}) collective-permute-start(bf16[32,2304]{1,0:T(8,128)(2,1)S(1)} %get-tuple-element.186), channel_id=1, source_target_pairs={{0,2},{1,15},{2,4},{3,1},{4,6},{5,3},{6,8},{7,5},{8,10},{9,7},{10,... | collective-permute-start | bytes 442376 | tf_op jit(solution)/shard_map/ppermute | solution.py:264
  89.8 12.1 %collective-permute-start.24 = (bf16[32,2304]{1,0:T(8,128)(2,1)S(1)}, bf16[32,2304]{1,0:T(8,128)(2,1)S(1)}, u32[]{:S(2)}, u32[]{:S(2)}) collective-permute-start(bf16[32,2304]{1,0:T(8,128)(2,1)S(1)} %get-tuple-element.187.refs_5_.refs_2_), channel_id=1, source_target_pairs={{0,8},{1,1},{2,10},{3,3},{4,12},{5,5},{6,14},{7,7},{8,0},{9,9},{10... | collective-permute-start | bytes 442376 | tf_op jit(solution)/shard_map/ppermute | solution.py:264
  102.0 1.7 %collective-permute-start.26 = (f32[32,2304]{1,0:T(8,128)S(1)}, f32[32,2304]{1,0:T(8,128)S(1)}, u32[]{:S(2)}, u32[]{:S(2)}) collective-permute-start(f32[32,2304]{1,0:T(8,128)S(1)} %shard_map.140.a_ref), channel_id=1, source_target_pairs={{0,1},{1,0},{2,3},{3,2},{4,5},{5,4},{6,7},{7,6},{8,9},{9,8},{10,11... | collective-permute-start | bytes 884744 | tf_op jit(solution)/shard_map/ppermute | solution.py:251
  104.5 12.6 %collective-permute-start.30 = (bf16[32,2304]{1,0:T(8,128)(2,1)S(1)}, bf16[32,2304]{1,0:T(8,128)(2,1)S(1)}, u32[]{:S(2)}, u32[]{:S(2)}) collective-permute-start(bf16[32,2304]{1,0:T(8,128)(2,1)S(1)} %get-tuple-element.205), channel_id=1, source_target_pairs={{0,246},{1,251},{2,248},{3,253},{4,250},{5,255},{6,252},{7,241},{8... | collective-permute-start | bytes 442376 | tf_op jit(solution)/shard_map/ppermute | solution.py:264
  104.5 18.4 %collective-permute-start.29 = (bf16[32,2304]{1,0:T(8,128)(2,1)S(1)}, bf16[32,2304]{1,0:T(8,128)(2,1)S(1)}, u32[]{:S(2)}, u32[]{:S(2)}) collective-permute-start(bf16[32,2304]{1,0:T(8,128)(2,1)S(1)} %get-tuple-element.205), channel_id=1, source_target_pairs={{0,244},{1,253},{2,246},{3,255},{4,248},{5,241},{6,250},{7,243},{8... | collective-permute-start | bytes 442376 | tf_op jit(solution)/shard_map/ppermute | solution.py:264
  104.5 20.1 %collective-permute-start.28 = (bf16[32,2304]{1,0:T(8,128)(2,1)S(1)}, bf16[32,2304]{1,0:T(8,128)(2,1)S(1)}, u32[]{:S(2)}, u32[]{:S(2)}) collective-permute-start(bf16[32,2304]{1,0:T(8,128)(2,1)S(1)} %get-tuple-element.205), channel_id=1, source_target_pairs={{0,242},{1,255},{2,244},{3,241},{4,246},{5,243},{6,248},{7,245},{8... | collective-permute-start | bytes 442376 | tf_op jit(solution)/shard_map/ppermute | solution.py:264
  107.9 21.8 %collective-permute-start.27 = (bf16[32,2304]{1,0:T(8,128)(2,1)S(1)}, bf16[32,2304]{1,0:T(8,128)(2,1)S(1)}, u32[]{:S(2)}, u32[]{:S(2)}) collective-permute-start(bf16[32,2304]{1,0:T(8,128)(2,1)S(1)} %get-tuple-element.205), channel_id=1, source_target_pairs={{0,248},{1,241},{2,250},{3,243},{4,252},{5,245},{6,254},{7,247},{8... | collective-permute-start | bytes 442376 | tf_op jit(solution)/shard_map/ppermute | solution.py:264
  130.6 1.3 collective-permute-start.31
  132.2 1.3 collective-permute-start.32
  132.4 14.2 %collective-permute-start.37 = (bf16[32,2304]{1,0:T(8,128)(2,1)S(1)}, bf16[32,2304]{1,0:T(8,128)(2,1)S(1)}, u32[]{:S(2)}, u32[]{:S(2)}) collective-permute-start(bf16[32,2304]{1,0:T(8,128)(2,1)S(1)} %collective-permute-done.27.refs_0_.odd_ref), channel_id=1, source_target_pairs={{0,1},{1,0},{2,3},{3,2},{4,5},{5,4},{6,7},{7,6},{8,9},{9,8},{10,11... | collective-permute-start | bytes 442376 | tf_op jit(solution)/shard_map/ppermute | solution.py:251
  133.9 12.7 %collective-permute-start.33 = (bf16[32,2304]{1,0:T(8,128)(2,1)S(1)}, bf16[32,2304]{1,0:T(8,128)(2,1)S(1)}, u32[]{:S(2)}, u32[]{:S(2)}) collective-permute-start(bf16[32,2304]{1,0:T(8,128)(2,1)S(1)} %get-tuple-element.219), channel_id=1, source_target_pairs={{0,6},{1,11},{2,8},{3,13},{4,10},{5,15},{6,12},{7,1},{8,14},{9,3},... | collective-permute-start | bytes 442376 | tf_op jit(solution)/shard_map/ppermute | solution.py:264
  134.0 12.6 %collective-permute-start.34 = (bf16[32,2304]{1,0:T(8,128)(2,1)S(1)}, bf16[32,2304]{1,0:T(8,128)(2,1)S(1)}, u32[]{:S(2)}, u32[]{:S(2)}) collective-permute-start(bf16[32,2304]{1,0:T(8,128)(2,1)S(1)} %get-tuple-element.220), channel_id=1, source_target_pairs={{0,4},{1,13},{2,6},{3,15},{4,8},{5,1},{6,10},{7,3},{8,12},{9,5},{1... | collective-permute-start | bytes 442376 | tf_op jit(solution)/shard_map/ppermute | solution.py:264
  135.6 15.8 %collective-permute-start.35 = (bf16[32,2304]{1,0:T(8,128)(2,1)S(1)}, bf16[32,2304]{1,0:T(8,128)(2,1)S(1)}, u32[]{:S(2)}, u32[]{:S(2)}) collective-permute-start(bf16[32,2304]{1,0:T(8,128)(2,1)S(1)} %get-tuple-element.221), channel_id=1, source_target_pairs={{0,2},{1,15},{2,4},{3,1},{4,6},{5,3},{6,8},{7,5},{8,10},{9,7},{10,... | collective-permute-start | bytes 442376 | tf_op jit(solution)/shard_map/ppermute | solution.py:264
  137.5 13.9 %collective-permute-start.36 = (bf16[32,2304]{1,0:T(8,128)(2,1)S(1)}, bf16[32,2304]{1,0:T(8,128)(2,1)S(1)}, u32[]{:S(2)}, u32[]{:S(2)}) collective-permute-start(bf16[32,2304]{1,0:T(8,128)(2,1)S(1)} %get-tuple-element.222.refs_5_.refs_2_), channel_id=1, source_target_pairs={{0,8},{1,1},{2,10},{3,3},{4,12},{5,5},{6,14},{7,7},{8,0},{9,9},{10... | collective-permute-start | bytes 442376 | tf_op jit(solution)/shard_map/ppermute | solution.py:264
  151.4 1.7 %collective-permute-start.38 = (f32[32,2304]{1,0:T(8,128)S(1)}, f32[32,2304]{1,0:T(8,128)S(1)}, u32[]{:S(2)}, u32[]{:S(2)}) collective-permute-start(f32[32,2304]{1,0:T(8,128)S(1)} %shard_map.147.a_ref), channel_id=1, source_target_pairs={{0,1},{1,0},{2,3},{3,2},{4,5},{5,4},{6,7},{7,6},{8,9},{9,8},{10,11... | collective-permute-start | bytes 884744 | tf_op jit(solution)/shard_map/ppermute | solution.py:251
  154.0 7.7 %collective-permute-start.39 = (bf16[16,2304]{1,0:T(8,128)(2,1)S(1)}, bf16[16,2304]{1,0:T(8,128)(2,1)S(1)}, u32[]{:S(2)}, u32[]{:S(2)}) collective-permute-start(bf16[16,2304]{1,0:T(8,128)(2,1)S(1)} %get-tuple-element.238), channel_id=1, source_target_pairs={{0,240},{16,0},{32,16},{48,32},{64,48},{80,64},{96,80},{112,96},{1... | collective-permute-start | bytes 221192 | tf_op jit(solution)/shard_map/ppermute | solution.py:254
  (5 other events, 4.8 us)

commit v5 on v4

--- a/solution.py
+++ b/solution.py
@@ -92,9 +92,9 @@
 
 
 def out_kernel(*refs):
-    edge_ref, *near, own_ref, pair_ref, keep_ref, send_ref, mine_ref = refs
-    size = edge_ref.shape[0]
-    for i, part in enumerate((edge_ref, *near[::-1])):
+    *parts, own_ref, pair_ref, keep_ref, send_ref, mine_ref = refs
+    size = parts[0].shape[0]
+    for i, part in enumerate(parts):
         mine_ref[i * size : (i + 1) * size] = part[...]
     send_ref[...] = dot_t(mine_ref[...], pair_ref[...]).astype(jnp.bfloat16)
     keep_ref[...] = dot_t(mine_ref[...], own_ref[...]).astype(jnp.bfloat16)
@@ -117,16 +117,24 @@
     total = total.astype(jnp.bfloat16)
     size = outs[0].shape[0]
     for i, out in enumerate(outs):
-        at = (i + 1) % len(outs) * size
+        at = (len(outs) - 1 - i) * size
         out[...] = total[at : at + size]
 
 
+def add_kernel(own_ref, relayed_ref, total_ref):
+    first = lax.axis_index("tensor") % 2 == 0
+    own = own_ref[...].astype(jnp.float32)
+    relayed = relayed_ref[...].astype(jnp.float32)
+    total_ref[...] = (own + jnp.where(first, relayed, 0.0)).astype(jnp.bfloat16)
+
+
 def sum_kernel(*refs):
-    *parts, total_ref = refs
-    total = parts[0][...].astype(jnp.float32)
-    for ref in parts[1:]:
+    *near, edge_ref, total_ref = refs
+    first = lax.axis_index("tensor") % 2 == 0
+    total = jnp.where(first, 0.0, edge_ref[...].astype(jnp.float32))
+    for ref in near:
         total = total + ref[...].astype(jnp.float32)
-    total_ref[...] = total
+    total_ref[...] = total.astype(total_ref.dtype)
 
 
 def lines_kernel(wait, own_ref, other_ref, pair_ref):
@@ -139,7 +147,8 @@
     first = lax.axis_index("tensor") % 2 == 0
     inputs = x_ref[...].astype(jnp.float32)
     inverse = lax.rsqrt(jnp.mean(inputs * inputs, -1, keepdims=True) + EPS)
-    scaled = (a_ref[...] + b_ref[...]) * gain_ref[...].astype(jnp.float32)
+    scaled = a_ref[...].astype(jnp.float32) + b_ref[...].astype(jnp.float32)
+    scaled = scaled * gain_ref[...].astype(jnp.float32)
     inner = jnp.mean(scaled * inputs, -1, keepdims=True)
     current = jnp.where(first, even_ref[...], odd_ref[...]).astype(jnp.float32)
     updated = (
@@ -169,8 +178,9 @@
 
 def choose_kernel(tick, plan_ref, *refs):
     chosen = plan_ref[tick, 0]
-    count = (len(refs) - 2) // 2
-    sources, outs, sems = refs[:count], refs[count + 1 : -1], refs[-1]
+    count = (len(refs) - 3) // 2
+    sources, outs, mark, sems = refs[:count], refs[count + 1 : -2], refs[-2], refs[-1]
+    mark[...] = jnp.zeros_like(mark)
     copies = []
     for i, (source, out) in enumerate(zip(sources, outs)):
         view = source.at[chosen, 0] if len(source.shape) == 4 else source.at[chosen]
@@ -217,6 +227,7 @@
 
 def choose(tick, plan, weights, gate):
     shapes = [jax.ShapeDtypeStruct(item.shape[-2:], item.dtype) for item in weights]
+    shapes.append(jax.ShapeDtypeStruct((8, 128), jnp.float32))
     return pl.pallas_call(
         functools.partial(choose_kernel, tick),
         out_shape=shapes,
@@ -281,25 +292,30 @@
         )
 
     def gather(pair, back, done):
-        moved = [hop(pair, k, back) for k in (far, *range(1, far))]
+        moved = [hop(pair, k, back) for k in range(far, 0, -1)]
         return hold((moved, done))
 
     def scatter(blocks, done):
-        steps = list(range(far - 1, 0, -1)) + [far]
-        moved = [hop(block, k, 0) for block, k in zip(blocks, steps)]
-        return hold((moved, done))
+        *near, edge = blocks
+        relayed = lax.ppermute(
+            edge, "tensor", [(2 * z, 2 * ((z + 1) % chips)) for z in range(chips)]
+        )
+        near[-1] = on_core(add_kernel, [bf16(2 * rows, width)], (near[-1], relayed))[0]
+        moved = [hop(block, 1 + i, 0) for i, block in enumerate(near)]
+        return hold((moved + [edge], done))
 
     other = swap(cot_in)
     other, *later = hold((other, w_value, w_out))
     away_value, away_out = (swap(item) for item in later)
     pair = on_core(order_kernel, [bf16(2 * rows, width)], (cot_in, other))[0]
-    weights = [w_out, away_out, w_value, away_value, norm_gain]
+    weights = [w_out, away_out, w_value, away_value]
     query_list = []
     key_list = []
     for tick in range(TICKS):
         last = tick == TICKS - 1
         if tick == 0:
-            done = attention_ready(0, pair), choose(0, plan, weights, pair)
+            chosen = choose(0, plan, weights, pair)
+            done = attention_ready(0, chosen[-1]), chosen
         elif tick == 1:
             done = attention_ready(2, pair)
         else:
@@ -309,7 +325,7 @@
             ready, chosen = done
         elif tick == 1:
             ready_last = done
-        own_out, pair_out, own_value, pair_value, gain = chosen
+        own_out, pair_out, own_value, pair_value, _ = chosen
         chance, low_t = ready
         keep, send = on_core(
             out_kernel,
@@ -322,19 +338,19 @@
             [bf16(length, heads * HD), bf16(half, HD), bf16(half, HD)],
             (keep, swap(send), low_t),
         )
+        if tick:
+            odd = parts[0]
+            value_away, even = hold((swap(value_send), swap(odd)))
+        else:
+            even = odd = pair
+            value_away, inputs_away = hold((swap(value_send), swap(saved_inputs)))
         blocks = on_core(
             partial_kernel,
             [bf16(2 * rows, width)] * far,
-            (value_keep, swap(value_send), own_value, pair_value),
+            (value_keep, value_away, own_value, pair_value),
         )
         gate = blocks[-1]
         found = grads(chance, grad_out, tick, gate)
-        if tick:
-            even, odd = swap(parts[0]), parts[0]
-        else:
-            even = odd = pair
-            later, _ = hold((saved_inputs, gate))
-            inputs_away = swap(later)
         lines = staged(
             lines_kernel,
             [bf16(2 * rows, width)],
@@ -347,9 +363,10 @@
             done = found, choose(1, plan, weights, gate), attention_ready(1, gate), inputs_away
         else:
             done = found, choose(2, plan, weights, gate)
-        done = done, lines, even
-        terms, (done, lines, even) = scatter(blocks, done)
-        total = on_core(sum_kernel, [f32(2 * rows, width)], terms)[0]
+        gain = choose(tick, plan, [norm_gain], gate)[0]
+        done = done, lines, even, gain
+        terms, (done, lines, even, gain) = scatter(blocks, done)
+        total = on_core(sum_kernel, [bf16(2 * rows, width)], terms)[0]
         if last:
             query, key = done
         else:

time: 163 us -> 159 us (0.975)
  starting transfers between devices: 68 us -> 52.2 us
  waiting for transfers between devices: 58.8 us -> 67 us
  Pallas kernels: 24.3 us -> 31.5 us
  local copies, waits for them, and re-layouts: 8.55 us -> 5.24 us
    ppermute x24 -> x21, starting transfers between devices: 65.1 us -> 40.7 us  [hop(): return lax.ppermute(block, ('section', 'tensor'), pairs)]
    ppermute x0 -> x3, waiting for transfers between devices: none -> 8.08 us  [scatter(): lax.ppermute(edge, 'tensor', [(2 * z, 2 * ((z + 1) % chips)) for z in ran...]
    ppermute x0 -> x3, starting transfers between devices: none -> 8.07 us  [scatter(): lax.ppermute(edge, 'tensor', [(2 * z, 2 * ((z + 1) % chips)) for z in ran...]
    pallas_call x3 -> x6, Pallas kernels: 4.07 us -> 8.74 us  [choose(): pl.pallas_call(functools.partial(choose_kernel, tick), out_shape=shapes,...]
    unnamed x29 -> x23, local copies, waits for them, and re-layouts: 8.55 us -> 5.24 us
    pallas_call x9, Pallas kernels: 9.89 us -> 12.3 us  [staged(): pl.pallas_call(functools.partial(staged_kernel, kernel, picks, len(shapes...]
    ppermute x24 -> x21, waiting for transfers between devices: 38.8 us -> 39.9 us  [hop(): return lax.ppermute(block, ('section', 'tensor'), pairs)]
    pallas_call x16 -> x19, Pallas kernels: 10.3 us -> 10.5 us  [on_core(): pl.pallas_call(kernel, out_shape=shapes, in_specs=[VMEM] * len(operands),...]
  transfers between devices with their start and end apart: 40 -> 40, of which waited for: 23 -> 24; matrix products, arithmetic and copies ran while one was open for 2% -> 1% of each run, Pallas kernels for 10% -> 17%
where the time goes in v5:
time: 159 us
  waiting for transfers between devices  67 us (42%)
  starting transfers between devices  52.2 us (33%)
  Pallas kernels  31.5 us (20%)
  local copies, waits for them, and re-layouts  5.24 us (3%)
    ppermute x21, starting transfers between devices, hop(): return lax.ppermute(block, ('section', 'tensor'), pairs)  40.7 us
    ppermute x21, waiting for transfers between devices, hop(): return lax.ppermute(block, ('section', 'tensor'), pairs)  39.9 us
    pallas_call x9, Pallas kernels, staged(): pl.pallas_call(functools.partial(staged_kernel, kernel, picks, len(shapes...  12.3 us
    ppermute x15, waiting for transfers between devices, swap(): return lax.ppermute(block, 'tensor', [(t, t ^ 1) for t in range(members)])  11.4 us
    pallas_call x19, Pallas kernels, on_core(): pl.pallas_call(kernel, out_shape=shapes, in_specs=[VMEM] * len(operands),...  10.5 us
    pallas_call x6, Pallas kernels, choose(): pl.pallas_call(functools.partial(choose_kernel, tick), out_shape=shapes,...  8.74 us
    ppermute x3, waiting for transfers between devices, scatter(): lax.ppermute(edge, 'tensor', [(2 * z, 2 * ((z + 1) % chips)) for z in ran...  8.08 us
    ppermute x3, starting transfers between devices, scatter(): lax.ppermute(edge, 'tensor', [(2 * z, 2 * ((z + 1) % chips)) for z in ran...  8.07 us
  transfers between devices with their start and end apart: 40, of which 24 were waited for; matrix products, arithmetic and copies ran while one was open for 1% of the time, Pallas kernels for 17%

profile of v5, /device:TPU:30, one launch (start us, length us, event | category | flops | bytes accessed | tf_op | source)
XLA Modules:
  0.0 158.5 jit_solution(17063663860809403795)
XLA Ops:
  0.7 1.5 collective-permute-done.b_ref
  4.3 1.9 %collective-permute-start.4 = (bf16[32,2304]{1,0:T(8,128)(2,1)}, bf16[32,2304]{1,0:T(8,128)(2,1)}, u32[]{:S(2)}, u32[]{:S(2)}) collective-permute-start(bf16[32,2304]{1,0:T(8,128)(2,1)} %shard_map.121.refs_4_.even_ref.odd_ref), channel_id=1, source_target_pairs={{0,2},{1,15},{2,4},{3,1},{4,6},{5,3},{6,8},{7,5},{8,10},{9,7},{10,... | collective-permute-start | bytes 442376 | tf_op jit(solution)/shard_map/ppermute | solution.py:275
  6.2 3.3 %collective-permute-start.3 = (bf16[32,2304]{1,0:T(8,128)(2,1)}, bf16[32,2304]{1,0:T(8,128)(2,1)}, u32[]{:S(2)}, u32[]{:S(2)}) collective-permute-start(bf16[32,2304]{1,0:T(8,128)(2,1)} %shard_map.121.refs_4_.even_ref.odd_ref), channel_id=1, source_target_pairs={{0,4},{1,13},{2,6},{3,15},{4,8},{5,1},{6,10},{7,3},{8,12},{9,5},{1... | collective-permute-start | bytes 442376 | tf_op jit(solution)/shard_map/ppermute | solution.py:275
  9.5 4.0 %collective-permute-start.2 = (bf16[32,2304]{1,0:T(8,128)(2,1)}, bf16[32,2304]{1,0:T(8,128)(2,1)}, u32[]{:S(2)}, u32[]{:S(2)}) collective-permute-start(bf16[32,2304]{1,0:T(8,128)(2,1)} %shard_map.121.refs_4_.even_ref.odd_ref), channel_id=1, source_target_pairs={{0,6},{1,11},{2,8},{3,13},{4,10},{5,15},{6,12},{7,1},{8,14},{9,3},... | collective-permute-start | bytes 442376 | tf_op jit(solution)/shard_map/ppermute | solution.py:275
  13.5 4.2 %collective-permute-start.1 = (bf16[32,2304]{1,0:T(8,128)(2,1)}, bf16[32,2304]{1,0:T(8,128)(2,1)}, u32[]{:S(2)}, u32[]{:S(2)}) collective-permute-start(bf16[32,2304]{1,0:T(8,128)(2,1)} %shard_map.121.refs_4_.even_ref.odd_ref), channel_id=1, source_target_pairs={{0,8},{1,1},{2,10},{3,3},{4,12},{5,5},{6,14},{7,7},{8,0},{9,9},{10... | collective-permute-start | bytes 442376 | tf_op jit(solution)/shard_map/ppermute | solution.py:275
  18.6 1.7 %copy-done = bf16[2,1,256,2304]{3,2,1,0:T(8,128)(2,1)S(1)} copy-done((bf16[2,1,256,2304]{3,2,1,0:T(8,128)(2,1)S(1)}, bf16[2,1,256,2304]{3,2,1,0:T(8,128)(2,1)}, u32[]{:S(2)}) %copy-start) | copy-done | bytes 2359320
  20.2 1.3 copy-done.3
  21.5 1.3 shard_map.122
  22.9 1.6 %shard_map.123 = (f32[2,256,256]{2,1,0:T(8,128)S(1)}, bf16[2,256,256]{2,1,0:T(8,128)(2,1)S(1)}) custom-call(bf16[3,256,256]{2,1,0:T(8,128)(2,1)S(1)} %copy-done.2, bf16[3,256,128]{2,1,0:T(8,128)(2,1)S(1)} %copy-done.4, s32[3,1,256]{2,1,0:T(1,128)S(1)} %copy-done.8, f32[8,128]{1,0:T(8,128)S(1)} %get-tuple-element.131.refs_3_), custom_call_target="tpu_custom_call" | custom-call | flops 1000 | bytes 1000 | tf_op jit(solution)/shard_map/pallas_call | solution.py:205
  25.7 2.0 %shard_map.124 = (bf16[128,256]{1,0:T(8,128)(2,1)S(1)}, bf16[128,256]{1,0:T(8,128)(2,1)S(1)}) custom-call(bf16[32,2304]{1,0:T(8,128)(2,1)} %collective-permute-done.1.refs_0_, bf16[32,2304]{1,0:T(8,128)(2,1)} %collective-permute-done.2.refs_1_, bf16[32,2304]{1,0:T(8,128)(2,1)} %collective-permute-done.3.refs_2_, ...), custom_call_target="tpu_custom_call" | custom-call | flops 1000 | bytes 1000 | tf_op jit(solution)/shard_map/pallas_call | solution.py:217
  27.9 1.2 collective-permute-done.7.recv_ref
  31.1 3.9 %collective-permute-start.12 = (bf16[32,2304]{1,0:T(8,128)(2,1)S(1)}, bf16[32,2304]{1,0:T(8,128)(2,1)S(1)}, u32[]{:S(2)}, u32[]{:S(2)}) collective-permute-start(bf16[32,2304]{1,0:T(8,128)(2,1)S(1)} %get-tuple-element.171.refs_5_.refs_4_.refs_3_.refs_2_.refs_1_), channel_id=1, source_target_pairs={{0,2},{2,4},{4,6},{6,8},{8,10},{10,12},{12,14},{14,0},{16,18},{18,... | collective-permute-start | bytes 442376 | tf_op jit(solution)/shard_map/ppermute | solution.py:300
  35.0 1.9 %collective-permute-start.10 = (bf16[32,2304]{1,0:T(8,128)(2,1)S(1)}, bf16[32,2304]{1,0:T(8,128)(2,1)S(1)}, u32[]{:S(2)}, u32[]{:S(2)}) collective-permute-start(bf16[32,2304]{1,0:T(8,128)(2,1)S(1)} %get-tuple-element.152), channel_id=1, source_target_pairs={{0,2},{1,15},{2,4},{3,1},{4,6},{5,3},{6,8},{7,5},{8,10},{9,7},{10,... | collective-permute-start | bytes 442376 | tf_op jit(solution)/shard_map/ppermute | solution.py:275
  37.2 2.4 %collective-permute-done.12.relayed_ref = bf16[32,2304]{1,0:T(8,128)(2,1)S(1)} collective-permute-done((bf16[32,2304]{1,0:T(8,128)(2,1)S(1)}, bf16[32,2304]{1,0:T(8,128)(2,1)S(1)}, u32[]{:S(2)}, u32[]{:S(2)}) %collective-permute-start.12) | collective-permute-done | bytes 147488 | tf_op jit(solution)/shard_map/ppermute | solution.py:300
  39.6 1.6 %collective-permute-start.13 = (bf16[32,2304]{1,0:T(8,128)(2,1)S(1)}, bf16[32,2304]{1,0:T(8,128)(2,1)S(1)}, u32[]{:S(2)}, u32[]{:S(2)}) collective-permute-start(bf16[32,2304]{1,0:T(8,128)(2,1)S(1)} %shard_map.127), channel_id=1, source_target_pairs={{0,6},{1,11},{2,8},{3,13},{4,10},{5,15},{6,12},{7,1},{8,14},{9,3},... | collective-permute-start | bytes 442376 | tf_op jit(solution)/shard_map/ppermute | solution.py:275
  41.2 1.6 %shard_map.130 = (f32[2,256,256]{2,1,0:T(8,128)S(1)}, bf16[2,256,256]{2,1,0:T(8,128)(2,1)S(1)}) custom-call(bf16[3,256,256]{2,1,0:T(8,128)(2,1)S(1)} %copy-done.2, bf16[3,256,128]{2,1,0:T(8,128)(2,1)S(1)} %copy-done.4, s32[3,1,256]{2,1,0:T(1,128)S(1)} %copy-done.8, bf16[32,2304]{1,0:T(8,128)(2,1)S(1)} %get-tuple-element.171.refs_5_.refs_4_.refs_3_.refs_2_.refs_1_), custom_call_target="tpu_custom_call" | custom-call | flops 1000 | bytes 1000 | tf_op jit(solution)/shard_map/pallas_call | solution.py:205
  42.9 1.2 shard_map.132
  45.1 1.5 shard_map.128
  46.6 1.9 %shard_map.129 = (bf16[256,2304]{1,0:T(8,128)(2,1)S(1)}, bf16[256,2304]{1,0:T(8,128)(2,1)S(1)}, bf16[2304,128]{1,0:T(8,128)(2,1)S(1)}, bf16[2304,128]{1,0:T(8,128)(2,1)S(1)}, f32[8,128]{1,0:T(8,128)}) custom-call(s32[3,1]{1,0:T(4,128)S(1)} %copy.13.plan_ref, bf16[2,1,256,2304]{3,2,1,0:T(8,128)(2,1)S(1)} %copy-done.1, ...), custom_call_target="tpu_custom_call" | custom-call | flops 1000 | bytes 1000 | tf_op jit(solution)/shard_map/pallas_call | solution.py:231
  48.6 2.5 %collective-permute-done.13.refs_2_ = bf16[32,2304]{1,0:T(8,128)(2,1)S(1)} collective-permute-done((bf16[32,2304]{1,0:T(8,128)(2,1)S(1)}, bf16[32,2304]{1,0:T(8,128)(2,1)S(1)}, u32[]{:S(2)}, u32[]{:S(2)}) %collective-permute-start.13) | collective-permute-done | bytes 147488 | tf_op jit(solution)/shard_map/ppermute | solution.py:275
  51.3 1.4 collective-permute-done.14.b_ref
  52.6 1.8 %shard_map.134 = (bf16[32,2304]{1,0:T(8,128)(2,1)S(1)}, bf16[16,2304]{1,0:T(8,128)(2,1)}) custom-call(bf16[32,2304]{1,0:T(8,128)(2,1)S(1)} %shard_map.133.a_ref, bf16[32,2304]{1,0:T(8,128)(2,1)S(1)} %collective-permute-done.14.b_ref, bf16[32,2304]{1,0:T(8,128)(2,1)S(1)} %shard_map.131.x_ref, bf16[1,2304]{1,0:T(2,128)(2,1)S(1)} %get-tuple-element.173.gain_ref, ...), custom_call_target="tpu_custom_call" | custom-call | flops 1000 | bytes 1000 | tf_op jit(solution)/shard_map/pallas_call | solution.py:217
  54.7 1.6 collective-permute-start.17
  56.3 1.9 %collective-permute-start.16 = (bf16[32,2304]{1,0:T(8,128)(2,1)S(1)}, bf16[32,2304]{1,0:T(8,128)(2,1)S(1)}, u32[]{:S(2)}, u32[]{:S(2)}) collective-permute-start(bf16[32,2304]{1,0:T(8,128)(2,1)S(1)} %get-tuple-element.175.refs_3_), channel_id=1, source_target_pairs={{0,246},{1,251},{2,248},{3,253},{4,250},{5,255},{6,252},{7,241},{8... | collective-permute-start | bytes 442376 | tf_op jit(solution)/shard_map/ppermute | solution.py:275
  58.2 4.9 %collective-permute-start.15 = (bf16[32,2304]{1,0:T(8,128)(2,1)S(1)}, bf16[32,2304]{1,0:T(8,128)(2,1)S(1)}, u32[]{:S(2)}, u32[]{:S(2)}) collective-permute-start(bf16[32,2304]{1,0:T(8,128)(2,1)S(1)} %get-tuple-element.175.refs_3_), channel_id=1, source_target_pairs={{0,248},{1,241},{2,250},{3,243},{4,252},{5,245},{6,254},{7,247},{8... | collective-permute-start | bytes 442376 | tf_op jit(solution)/shard_map/ppermute | solution.py:275
  63.1 1.6 %shard_map.135 = (f32[2,256,256]{2,1,0:T(8,128)S(1)}, bf16[2,256,256]{2,1,0:T(8,128)(2,1)S(1)}) custom-call(bf16[3,256,256]{2,1,0:T(8,128)(2,1)S(1)} %copy-done.2, bf16[3,256,128]{2,1,0:T(8,128)(2,1)S(1)} %copy-done.4, s32[3,1,256]{2,1,0:T(1,128)S(1)} %copy-done.8, bf16[32,2304]{1,0:T(8,128)(2,1)S(1)} %get-tuple-element.175.refs_3_), custom_call_target="tpu_custom_call" | custom-call | flops 1000 | bytes 1000 | tf_op jit(solution)/shard_map/pallas_call | solution.py:205
  64.7 3.6 %collective-permute-done.18.refs_3_ = bf16[32,2304]{1,0:T(8,128)(2,1)S(1)} collective-permute-done((bf16[32,2304]{1,0:T(8,128)(2,1)S(1)}, bf16[32,2304]{1,0:T(8,128)(2,1)S(1)}, u32[]{:S(2)}, u32[]{:S(2)}) %collective-permute-start.18) | collective-permute-done | bytes 147488 | tf_op jit(solution)/shard_map/ppermute | solution.py:275
  68.3 8.3 %collective-permute-done.16.refs_1_ = bf16[32,2304]{1,0:T(8,128)(2,1)S(1)} collective-permute-done((bf16[32,2304]{1,0:T(8,128)(2,1)S(1)}, bf16[32,2304]{1,0:T(8,128)(2,1)S(1)}, u32[]{:S(2)}, u32[]{:S(2)}) %collective-permute-start.16) | collective-permute-done | bytes 147488 | tf_op jit(solution)/shard_map/ppermute | solution.py:275
  81.1 2.2 %collective-permute-start.24 = (bf16[32,2304]{1,0:T(8,128)(2,1)S(1)}, bf16[32,2304]{1,0:T(8,128)(2,1)S(1)}, u32[]{:S(2)}, u32[]{:S(2)}) collective-permute-start(bf16[32,2304]{1,0:T(8,128)(2,1)S(1)} %get-tuple-element.210.refs_5_.refs_4_.refs_2_.refs_1_.refs_3_), channel_id=1, source_target_pairs={{0,2},{2,4},{4,6},{6,8},{8,10},{10,12},{12,14},{14,0},{16,18},{18,... | collective-permute-start | bytes 442376 | tf_op jit(solution)/shard_map/ppermute | solution.py:300
  83.3 2.7 %collective-permute-start.22 = (bf16[32,2304]{1,0:T(8,128)(2,1)S(1)}, bf16[32,2304]{1,0:T(8,128)(2,1)S(1)}, u32[]{:S(2)}, u32[]{:S(2)}) collective-permute-start(bf16[32,2304]{1,0:T(8,128)(2,1)S(1)} %get-tuple-element.192), channel_id=1, source_target_pairs={{0,2},{1,15},{2,4},{3,1},{4,6},{5,3},{6,8},{7,5},{8,10},{9,7},{10,... | collective-permute-start | bytes 442376 | tf_op jit(solution)/shard_map/ppermute | solution.py:275
  87.1 2.2 %collective-permute-done.24.relayed_ref = bf16[32,2304]{1,0:T(8,128)(2,1)S(1)} collective-permute-done((bf16[32,2304]{1,0:T(8,128)(2,1)S(1)}, bf16[32,2304]{1,0:T(8,128)(2,1)S(1)}, u32[]{:S(2)}, u32[]{:S(2)}) %collective-permute-start.24) | collective-permute-done | bytes 147488 | tf_op jit(solution)/shard_map/ppermute | solution.py:300
  92.5 1.5 shard_map.140
  94.0 1.9 %shard_map.141 = (bf16[256,2304]{1,0:T(8,128)(2,1)S(1)}, bf16[256,2304]{1,0:T(8,128)(2,1)S(1)}, bf16[2304,128]{1,0:T(8,128)(2,1)S(1)}, bf16[2304,128]{1,0:T(8,128)(2,1)S(1)}, f32[8,128]{1,0:T(8,128)}) custom-call(s32[3,1]{1,0:T(4,128)S(1)} %copy.13.plan_ref, bf16[2,1,256,2304]{3,2,1,0:T(8,128)(2,1)S(1)} %copy-done.1, ...), custom_call_target="tpu_custom_call" | custom-call | flops 1000 | bytes 1000 | tf_op jit(solution)/shard_map/pallas_call | solution.py:231
  96.0 4.2 %collective-permute-done.25.refs_2_ = bf16[32,2304]{1,0:T(8,128)(2,1)S(1)} collective-permute-done((bf16[32,2304]{1,0:T(8,128)(2,1)S(1)}, bf16[32,2304]{1,0:T(8,128)(2,1)S(1)}, u32[]{:S(2)}, u32[]{:S(2)}) %collective-permute-start.25) | collective-permute-done | bytes 147488 | tf_op jit(solution)/shard_map/ppermute | solution.py:275
  100.4 1.4 collective-permute-done.26.b_ref
  102.6 1.4 collective-permute-start.28
  104.0 7.3 %collective-permute-start.27 = (bf16[32,2304]{1,0:T(8,128)(2,1)S(1)}, bf16[32,2304]{1,0:T(8,128)(2,1)S(1)}, u32[]{:S(2)}, u32[]{:S(2)}) collective-permute-start(bf16[32,2304]{1,0:T(8,128)(2,1)S(1)} %get-tuple-element.214), channel_id=1, source_target_pairs={{0,248},{1,241},{2,250},{3,243},{4,252},{5,245},{6,254},{7,247},{8... | collective-permute-start | bytes 442376 | tf_op jit(solution)/shard_map/ppermute | solution.py:275
  111.3 2.6 %collective-permute-done.30.refs_3_ = bf16[32,2304]{1,0:T(8,128)(2,1)S(1)} collective-permute-done((bf16[32,2304]{1,0:T(8,128)(2,1)S(1)}, bf16[32,2304]{1,0:T(8,128)(2,1)S(1)}, u32[]{:S(2)}, u32[]{:S(2)}) %collective-permute-start.30) | collective-permute-done | bytes 147488 | tf_op jit(solution)/shard_map/ppermute | solution.py:275
  113.9 4.6 %collective-permute-done.29.refs_2_ = bf16[32,2304]{1,0:T(8,128)(2,1)S(1)} collective-permute-done((bf16[32,2304]{1,0:T(8,128)(2,1)S(1)}, bf16[32,2304]{1,0:T(8,128)(2,1)S(1)}, u32[]{:S(2)}, u32[]{:S(2)}) %collective-permute-start.29) | collective-permute-done | bytes 147488 | tf_op jit(solution)/shard_map/ppermute | solution.py:275
  118.5 7.2 %collective-permute-done.27.refs_0_.odd_ref = bf16[32,2304]{1,0:T(8,128)(2,1)S(1)} collective-permute-done((bf16[32,2304]{1,0:T(8,128)(2,1)S(1)}, bf16[32,2304]{1,0:T(8,128)(2,1)S(1)}, u32[]{:S(2)}, u32[]{:S(2)}) %collective-permute-start.27) | collective-permute-done | bytes 147488 | tf_op jit(solution)/shard_map/ppermute | solution.py:275
  130.1 1.9 %collective-permute-start.36 = (bf16[32,2304]{1,0:T(8,128)(2,1)S(1)}, bf16[32,2304]{1,0:T(8,128)(2,1)S(1)}, u32[]{:S(2)}, u32[]{:S(2)}) collective-permute-start(bf16[32,2304]{1,0:T(8,128)(2,1)S(1)} %get-tuple-element.246.refs_5_.refs_2_.refs_1_.refs_3_), channel_id=1, source_target_pairs={{0,2},{2,4},{4,6},{6,8},{8,10},{10,12},{12,14},{14,0},{16,18},{18,... | collective-permute-start | bytes 442376 | tf_op jit(solution)/shard_map/ppermute | solution.py:300
  132.1 1.3 collective-permute-start.35
  133.4 1.5 shard_map.150
  134.9 3.5 %collective-permute-done.36.relayed_ref = bf16[32,2304]{1,0:T(8,128)(2,1)S(1)} collective-permute-done((bf16[32,2304]{1,0:T(8,128)(2,1)S(1)}, bf16[32,2304]{1,0:T(8,128)(2,1)S(1)}, u32[]{:S(2)}, u32[]{:S(2)}) %collective-permute-start.36) | collective-permute-done | bytes 147488 | tf_op jit(solution)/shard_map/ppermute | solution.py:300
  142.2 2.4 %collective-permute-done.35.refs_1_ = bf16[32,2304]{1,0:T(8,128)(2,1)S(1)} collective-permute-done((bf16[32,2304]{1,0:T(8,128)(2,1)S(1)}, bf16[32,2304]{1,0:T(8,128)(2,1)S(1)}, u32[]{:S(2)}, u32[]{:S(2)}) %collective-permute-start.35) | collective-permute-done | bytes 147488 | tf_op jit(solution)/shard_map/ppermute | solution.py:275
  144.6 3.1 %collective-permute-done.37.refs_2_ = bf16[32,2304]{1,0:T(8,128)(2,1)S(1)} collective-permute-done((bf16[32,2304]{1,0:T(8,128)(2,1)S(1)}, bf16[32,2304]{1,0:T(8,128)(2,1)S(1)}, u32[]{:S(2)}, u32[]{:S(2)}) %collective-permute-start.37) | collective-permute-done | bytes 147488 | tf_op jit(solution)/shard_map/ppermute | solution.py:275
  148.0 1.4 collective-permute-done.38.b_ref
  150.2 7.7 %collective-permute-done.39 = bf16[16,2304]{1,0:T(8,128)(2,1)S(1)} collective-permute-done((bf16[16,2304]{1,0:T(8,128)(2,1)S(1)}, bf16[16,2304]{1,0:T(8,128)(2,1)S(1)}, u32[]{:S(2)}, u32[]{:S(2)}) %collective-permute-start.39) | collective-permute-done | bytes 73760 | tf_op jit(solution)/shard_map/ppermute | solution.py:265
  (91 shorter events, 27.6 us)
Async XLA Ops:
  0.6 1.6 collective-permute-start
  2.2 15.5 %collective-permute-start.5 = (bf16[2,1,256,2304]{3,2,1,0:T(8,128)(2,1)}, bf16[2,1,256,2304]{3,2,1,0:T(8,128)(2,1)S(1)}, u32[]{:S(2)}, u32[]{:S(2)}) collective-permute-start(bf16[2,1,256,2304]{3,2,1,0:T(8,128)(2,1)} %refs_0_.18), channel_id=1, source_target_pairs={{0,1},{1,0},{2,3},{3,2},{4,5},{5,4},{6,7},{7,6},{8,9},{9,8},{10,11... | collective-permute-start | bytes 7077896 | tf_op jit(solution)/shard_map/ppermute | solution.py:262
  2.4 11.1 %collective-permute-start.6 = (bf16[2,1,2304,128]{3,2,1,0:T(8,128)(2,1)}, bf16[2,1,2304,128]{3,2,1,0:T(8,128)(2,1)S(1)}, u32[]{:S(2)}, u32[]{:S(2)}) collective-permute-start(bf16[2,1,2304,128]{3,2,1,0:T(8,128)(2,1)} %refs_2_.16), channel_id=1, source_target_pairs={{0,1},{1,0},{2,3},{3,2},{4,5},{5,4},{6,7},{7,6},{8,9},{9,8},{10,11... | collective-permute-start | bytes 3538952 | tf_op jit(solution)/shard_map/ppermute | solution.py:262
  4.3 20.3 %collective-permute-start.4 = (bf16[32,2304]{1,0:T(8,128)(2,1)}, bf16[32,2304]{1,0:T(8,128)(2,1)}, u32[]{:S(2)}, u32[]{:S(2)}) collective-permute-start(bf16[32,2304]{1,0:T(8,128)(2,1)} %shard_map.121.refs_4_.even_ref.odd_ref), channel_id=1, source_target_pairs={{0,2},{1,15},{2,4},{3,1},{4,6},{5,3},{6,8},{7,5},{8,10},{9,7},{10,... | collective-permute-start | bytes 442376 | tf_op jit(solution)/shard_map/ppermute | solution.py:275
  6.2 18.4 %collective-permute-start.3 = (bf16[32,2304]{1,0:T(8,128)(2,1)}, bf16[32,2304]{1,0:T(8,128)(2,1)}, u32[]{:S(2)}, u32[]{:S(2)}) collective-permute-start(bf16[32,2304]{1,0:T(8,128)(2,1)} %shard_map.121.refs_4_.even_ref.odd_ref), channel_id=1, source_target_pairs={{0,4},{1,13},{2,6},{3,15},{4,8},{5,1},{6,10},{7,3},{8,12},{9,5},{1... | collective-permute-start | bytes 442376 | tf_op jit(solution)/shard_map/ppermute | solution.py:275
  9.5 15.1 %collective-permute-start.2 = (bf16[32,2304]{1,0:T(8,128)(2,1)}, bf16[32,2304]{1,0:T(8,128)(2,1)}, u32[]{:S(2)}, u32[]{:S(2)}) collective-permute-start(bf16[32,2304]{1,0:T(8,128)(2,1)} %shard_map.121.refs_4_.even_ref.odd_ref), channel_id=1, source_target_pairs={{0,6},{1,11},{2,8},{3,13},{4,10},{5,15},{6,12},{7,1},{8,14},{9,3},... | collective-permute-start | bytes 442376 | tf_op jit(solution)/shard_map/ppermute | solution.py:275
  13.5 12.2 %collective-permute-start.1 = (bf16[32,2304]{1,0:T(8,128)(2,1)}, bf16[32,2304]{1,0:T(8,128)(2,1)}, u32[]{:S(2)}, u32[]{:S(2)}) collective-permute-start(bf16[32,2304]{1,0:T(8,128)(2,1)} %shard_map.121.refs_4_.even_ref.odd_ref), channel_id=1, source_target_pairs={{0,8},{1,1},{2,10},{3,3},{4,12},{5,5},{6,14},{7,7},{8,0},{9,9},{10... | collective-permute-start | bytes 442376 | tf_op jit(solution)/shard_map/ppermute | solution.py:275
  17.7 11.9 %collective-permute-start.9 = (bf16[3,16,2304]{2,1,0:T(8,128)(2,1)}, bf16[3,16,2304]{2,1,0:T(8,128)(2,1)}, u32[]{:S(2)}, u32[]{:S(2)}) collective-permute-start(bf16[3,16,2304]{2,1,0:T(8,128)(2,1)} %refs_0_.20), channel_id=1, source_target_pairs={{0,1},{1,0},{2,3},{3,2},{4,5},{5,4},{6,7},{7,6},{8,9},{9,8},{10,11... | collective-permute-start | bytes 663560 | tf_op jit(solution)/shard_map/ppermute | solution.py:262
  18.6 1.7 %copy-start = (bf16[2,1,256,2304]{3,2,1,0:T(8,128)(2,1)S(1)}, bf16[2,1,256,2304]{3,2,1,0:T(8,128)(2,1)}, u32[]{:S(2)}) copy-start(bf16[2,1,256,2304]{3,2,1,0:T(8,128)(2,1)} %refs_0_.18) | copy-start | bytes 7077892
  21.5 1.4 copy-start.2
  21.5 1.4 copy-start.4
  21.5 1.4 copy-start.8
  27.8 13.5 %copy-start.9 = (bf16[2,1,2304]{2,0,1:T(2,128)(2,1)S(1)}, bf16[2,1,2304]{2,0,1:T(2,128)(2,1)}, u32[]{:S(2)}) copy-start(bf16[2,1,2304]{2,0,1:T(2,128)(2,1)} %param.19) | copy-start | bytes 27652
  27.8 1.3 collective-permute-start.7
  29.3 1.3 collective-permute-start.8
  30.6 13.5 %copy-start.5 = (bf16[3,16,2304]{2,1,0:T(8,128)(2,1)S(1)}, bf16[3,16,2304]{2,1,0:T(8,128)(2,1)}, u32[]{:S(2)}) copy-start(bf16[3,16,2304]{2,1,0:T(8,128)(2,1)} %refs_0_.20) | copy-start | bytes 663556
  31.1 14.0 %copy-start.6 = (bf16[3,256,128]{2,1,0:T(8,128)(2,1)S(1)}, bf16[3,256,128]{2,1,0:T(8,128)(2,1)}, u32[]{:S(2)}) copy-start(bf16[3,256,128]{2,1,0:T(8,128)(2,1)} %refs_4_.5) | copy-start | bytes 589828
  31.1 8.4 %collective-permute-start.12 = (bf16[32,2304]{1,0:T(8,128)(2,1)S(1)}, bf16[32,2304]{1,0:T(8,128)(2,1)S(1)}, u32[]{:S(2)}, u32[]{:S(2)}) collective-permute-start(bf16[32,2304]{1,0:T(8,128)(2,1)S(1)} %get-tuple-element.171.refs_5_.refs_4_.refs_3_.refs_2_.refs_1_), channel_id=1, source_target_pairs={{0,2},{2,4},{4,6},{6,8},{8,10},{10,12},{12,14},{14,0},{16,18},{18,... | collective-permute-start | bytes 442376 | tf_op jit(solution)/shard_map/ppermute | solution.py:300
  35.0 13.5 %collective-permute-start.10 = (bf16[32,2304]{1,0:T(8,128)(2,1)S(1)}, bf16[32,2304]{1,0:T(8,128)(2,1)S(1)}, u32[]{:S(2)}, u32[]{:S(2)}) collective-permute-start(bf16[32,2304]{1,0:T(8,128)(2,1)S(1)} %get-tuple-element.152), channel_id=1, source_target_pairs={{0,2},{1,15},{2,4},{3,1},{4,6},{5,3},{6,8},{7,5},{8,10},{9,7},{10,... | collective-permute-start | bytes 442376 | tf_op jit(solution)/shard_map/ppermute | solution.py:275
  37.0 11.6 %collective-permute-start.11 = (bf16[32,2304]{1,0:T(8,128)(2,1)S(1)}, bf16[32,2304]{1,0:T(8,128)(2,1)S(1)}, u32[]{:S(2)}, u32[]{:S(2)}) collective-permute-start(bf16[32,2304]{1,0:T(8,128)(2,1)S(1)} %get-tuple-element.153), channel_id=1, source_target_pairs={{0,4},{1,13},{2,6},{3,15},{4,8},{5,1},{6,10},{7,3},{8,12},{9,5},{1... | collective-permute-start | bytes 442376 | tf_op jit(solution)/shard_map/ppermute | solution.py:275
  39.6 11.5 %collective-permute-start.13 = (bf16[32,2304]{1,0:T(8,128)(2,1)S(1)}, bf16[32,2304]{1,0:T(8,128)(2,1)S(1)}, u32[]{:S(2)}, u32[]{:S(2)}) collective-permute-start(bf16[32,2304]{1,0:T(8,128)(2,1)S(1)} %shard_map.127), channel_id=1, source_target_pairs={{0,6},{1,11},{2,8},{3,13},{4,10},{5,15},{6,12},{7,1},{8,14},{9,3},... | collective-permute-start | bytes 442376 | tf_op jit(solution)/shard_map/ppermute | solution.py:275
  42.9 3.7 %copy-start.1 = (bf16[2,1,256,2304]{3,2,1,0:T(8,128)(2,1)S(1)}, bf16[2,1,256,2304]{3,2,1,0:T(8,128)(2,1)}, u32[]{:S(2)}) copy-start(bf16[2,1,256,2304]{3,2,1,0:T(8,128)(2,1)} %refs_0_.18) | copy-start | bytes 7077892
  51.2 1.5 collective-permute-start.14
  54.5 13.8 %collective-permute-start.18 = (bf16[32,2304]{1,0:T(8,128)(2,1)S(1)}, bf16[32,2304]{1,0:T(8,128)(2,1)S(1)}, u32[]{:S(2)}, u32[]{:S(2)}) collective-permute-start(bf16[32,2304]{1,0:T(8,128)(2,1)S(1)} %get-tuple-element.175.refs_3_), channel_id=1, source_target_pairs={{0,242},{1,255},{2,244},{3,241},{4,246},{5,243},{6,248},{7,245},{8... | collective-permute-start | bytes 442376 | tf_op jit(solution)/shard_map/ppermute | solution.py:275
  54.7 13.6 %collective-permute-start.17 = (bf16[32,2304]{1,0:T(8,128)(2,1)S(1)}, bf16[32,2304]{1,0:T(8,128)(2,1)S(1)}, u32[]{:S(2)}, u32[]{:S(2)}) collective-permute-start(bf16[32,2304]{1,0:T(8,128)(2,1)S(1)} %get-tuple-element.175.refs_3_), channel_id=1, source_target_pairs={{0,244},{1,253},{2,246},{3,255},{4,248},{5,241},{6,250},{7,243},{8... | collective-permute-start | bytes 442376 | tf_op jit(solution)/shard_map/ppermute | solution.py:275
  56.3 20.3 %collective-permute-start.16 = (bf16[32,2304]{1,0:T(8,128)(2,1)S(1)}, bf16[32,2304]{1,0:T(8,128)(2,1)S(1)}, u32[]{:S(2)}, u32[]{:S(2)}) collective-permute-start(bf16[32,2304]{1,0:T(8,128)(2,1)S(1)} %get-tuple-element.175.refs_3_), channel_id=1, source_target_pairs={{0,246},{1,251},{2,248},{3,253},{4,250},{5,255},{6,252},{7,241},{8... | collective-permute-start | bytes 442376 | tf_op jit(solution)/shard_map/ppermute | solution.py:275
  58.2 18.5 %collective-permute-start.15 = (bf16[32,2304]{1,0:T(8,128)(2,1)S(1)}, bf16[32,2304]{1,0:T(8,128)(2,1)S(1)}, u32[]{:S(2)}, u32[]{:S(2)}) collective-permute-start(bf16[32,2304]{1,0:T(8,128)(2,1)S(1)} %get-tuple-element.175.refs_3_), channel_id=1, source_target_pairs={{0,248},{1,241},{2,250},{3,243},{4,252},{5,245},{6,254},{7,247},{8... | collective-permute-start | bytes 442376 | tf_op jit(solution)/shard_map/ppermute | solution.py:275
  76.7 3.9 %collective-permute-start.21 = (bf16[32,2304]{1,0:T(8,128)(2,1)S(1)}, bf16[32,2304]{1,0:T(8,128)(2,1)S(1)}, u32[]{:S(2)}, u32[]{:S(2)}) collective-permute-start(bf16[32,2304]{1,0:T(8,128)(2,1)S(1)} %collective-permute-done.15.refs_0_.odd_ref), channel_id=1, source_target_pairs={{0,1},{1,0},{2,3},{3,2},{4,5},{5,4},{6,7},{7,6},{8,9},{9,8},{10,11... | collective-permute-start | bytes 442376 | tf_op jit(solution)/shard_map/ppermute | solution.py:262
  77.6 1.5 collective-permute-start.19
  79.3 1.3 collective-permute-start.20
  81.1 8.2 %collective-permute-start.24 = (bf16[32,2304]{1,0:T(8,128)(2,1)S(1)}, bf16[32,2304]{1,0:T(8,128)(2,1)S(1)}, u32[]{:S(2)}, u32[]{:S(2)}) collective-permute-start(bf16[32,2304]{1,0:T(8,128)(2,1)S(1)} %get-tuple-element.210.refs_5_.refs_4_.refs_2_.refs_1_.refs_3_), channel_id=1, source_target_pairs={{0,2},{2,4},{4,6},{6,8},{8,10},{10,12},{12,14},{14,0},{16,18},{18,... | collective-permute-start | bytes 442376 | tf_op jit(solution)/shard_map/ppermute | solution.py:300
  83.3 12.6 %collective-permute-start.22 = (bf16[32,2304]{1,0:T(8,128)(2,1)S(1)}, bf16[32,2304]{1,0:T(8,128)(2,1)S(1)}, u32[]{:S(2)}, u32[]{:S(2)}) collective-permute-start(bf16[32,2304]{1,0:T(8,128)(2,1)S(1)} %get-tuple-element.192), channel_id=1, source_target_pairs={{0,2},{1,15},{2,4},{3,1},{4,6},{5,3},{6,8},{7,5},{8,10},{9,7},{10,... | collective-permute-start | bytes 442376 | tf_op jit(solution)/shard_map/ppermute | solution.py:275
  86.0 9.9 %collective-permute-start.23 = (bf16[32,2304]{1,0:T(8,128)(2,1)S(1)}, bf16[32,2304]{1,0:T(8,128)(2,1)S(1)}, u32[]{:S(2)}, u32[]{:S(2)}) collective-permute-start(bf16[32,2304]{1,0:T(8,128)(2,1)S(1)} %get-tuple-element.193), channel_id=1, source_target_pairs={{0,4},{1,13},{2,6},{3,15},{4,8},{5,1},{6,10},{7,3},{8,12},{9,5},{1... | collective-permute-start | bytes 442376 | tf_op jit(solution)/shard_map/ppermute | solution.py:275
  89.4 10.8 %collective-permute-start.25 = (bf16[32,2304]{1,0:T(8,128)(2,1)S(1)}, bf16[32,2304]{1,0:T(8,128)(2,1)S(1)}, u32[]{:S(2)}, u32[]{:S(2)}) collective-permute-start(bf16[32,2304]{1,0:T(8,128)(2,1)S(1)} %shard_map.139), channel_id=1, source_target_pairs={{0,6},{1,11},{2,8},{3,13},{4,10},{5,15},{6,12},{7,1},{8,14},{9,3},... | collective-permute-start | bytes 442376 | tf_op jit(solution)/shard_map/ppermute | solution.py:275
  100.3 1.5 collective-permute-start.26
  102.6 11.3 %collective-permute-start.30 = (bf16[32,2304]{1,0:T(8,128)(2,1)S(1)}, bf16[32,2304]{1,0:T(8,128)(2,1)S(1)}, u32[]{:S(2)}, u32[]{:S(2)}) collective-permute-start(bf16[32,2304]{1,0:T(8,128)(2,1)S(1)} %get-tuple-element.214), channel_id=1, source_target_pairs={{0,242},{1,255},{2,244},{3,241},{4,246},{5,243},{6,248},{7,245},{8... | collective-permute-start | bytes 442376 | tf_op jit(solution)/shard_map/ppermute | solution.py:275
  102.6 15.9 %collective-permute-start.29 = (bf16[32,2304]{1,0:T(8,128)(2,1)S(1)}, bf16[32,2304]{1,0:T(8,128)(2,1)S(1)}, u32[]{:S(2)}, u32[]{:S(2)}) collective-permute-start(bf16[32,2304]{1,0:T(8,128)(2,1)S(1)} %get-tuple-element.214), channel_id=1, source_target_pairs={{0,244},{1,253},{2,246},{3,255},{4,248},{5,241},{6,250},{7,243},{8... | collective-permute-start | bytes 442376 | tf_op jit(solution)/shard_map/ppermute | solution.py:275
  102.6 15.9 %collective-permute-start.28 = (bf16[32,2304]{1,0:T(8,128)(2,1)S(1)}, bf16[32,2304]{1,0:T(8,128)(2,1)S(1)}, u32[]{:S(2)}, u32[]{:S(2)}) collective-permute-start(bf16[32,2304]{1,0:T(8,128)(2,1)S(1)} %get-tuple-element.214), channel_id=1, source_target_pairs={{0,246},{1,251},{2,248},{3,253},{4,250},{5,255},{6,252},{7,241},{8... | collective-permute-start | bytes 442376 | tf_op jit(solution)/shard_map/ppermute | solution.py:275
  104.0 21.7 %collective-permute-start.27 = (bf16[32,2304]{1,0:T(8,128)(2,1)S(1)}, bf16[32,2304]{1,0:T(8,128)(2,1)S(1)}, u32[]{:S(2)}, u32[]{:S(2)}) collective-permute-start(bf16[32,2304]{1,0:T(8,128)(2,1)S(1)} %get-tuple-element.214), channel_id=1, source_target_pairs={{0,248},{1,241},{2,250},{3,243},{4,252},{5,245},{6,254},{7,247},{8... | collective-permute-start | bytes 442376 | tf_op jit(solution)/shard_map/ppermute | solution.py:275
  125.7 3.9 %collective-permute-start.33 = (bf16[32,2304]{1,0:T(8,128)(2,1)S(1)}, bf16[32,2304]{1,0:T(8,128)(2,1)S(1)}, u32[]{:S(2)}, u32[]{:S(2)}) collective-permute-start(bf16[32,2304]{1,0:T(8,128)(2,1)S(1)} %collective-permute-done.27.refs_0_.odd_ref), channel_id=1, source_target_pairs={{0,1},{1,0},{2,3},{3,2},{4,5},{5,4},{6,7},{7,6},{8,9},{9,8},{10,11... | collective-permute-start | bytes 442376 | tf_op jit(solution)/shard_map/ppermute | solution.py:262
  126.6 1.5 collective-permute-start.31
  128.3 1.3 collective-permute-start.32
  130.1 8.2 %collective-permute-start.36 = (bf16[32,2304]{1,0:T(8,128)(2,1)S(1)}, bf16[32,2304]{1,0:T(8,128)(2,1)S(1)}, u32[]{:S(2)}, u32[]{:S(2)}) collective-permute-start(bf16[32,2304]{1,0:T(8,128)(2,1)S(1)} %get-tuple-element.246.refs_5_.refs_2_.refs_1_.refs_3_), channel_id=1, source_target_pairs={{0,2},{2,4},{4,6},{6,8},{8,10},{10,12},{12,14},{14,0},{16,18},{18,... | collective-permute-start | bytes 442376 | tf_op jit(solution)/shard_map/ppermute | solution.py:300
  132.1 10.1 %collective-permute-start.34 = (bf16[32,2304]{1,0:T(8,128)(2,1)S(1)}, bf16[32,2304]{1,0:T(8,128)(2,1)S(1)}, u32[]{:S(2)}, u32[]{:S(2)}) collective-permute-start(bf16[32,2304]{1,0:T(8,128)(2,1)S(1)} %get-tuple-element.229), channel_id=1, source_target_pairs={{0,2},{1,15},{2,4},{3,1},{4,6},{5,3},{6,8},{7,5},{8,10},{9,7},{10,... | collective-permute-start | bytes 442376 | tf_op jit(solution)/shard_map/ppermute | solution.py:275
  132.1 12.5 %collective-permute-start.35 = (bf16[32,2304]{1,0:T(8,128)(2,1)S(1)}, bf16[32,2304]{1,0:T(8,128)(2,1)S(1)}, u32[]{:S(2)}, u32[]{:S(2)}) collective-permute-start(bf16[32,2304]{1,0:T(8,128)(2,1)S(1)} %get-tuple-element.230), channel_id=1, source_target_pairs={{0,4},{1,13},{2,6},{3,15},{4,8},{5,1},{6,10},{7,3},{8,12},{9,5},{1... | collective-permute-start | bytes 442376 | tf_op jit(solution)/shard_map/ppermute | solution.py:275
  138.4 9.4 %collective-permute-start.37 = (bf16[32,2304]{1,0:T(8,128)(2,1)S(1)}, bf16[32,2304]{1,0:T(8,128)(2,1)S(1)}, u32[]{:S(2)}, u32[]{:S(2)}) collective-permute-start(bf16[32,2304]{1,0:T(8,128)(2,1)S(1)} %shard_map.149), channel_id=1, source_target_pairs={{0,6},{1,11},{2,8},{3,13},{4,10},{5,15},{6,12},{7,1},{8,14},{9,3},... | collective-permute-start | bytes 442376 | tf_op jit(solution)/shard_map/ppermute | solution.py:275
  147.9 1.5 collective-permute-start.38
  150.2 7.7 %collective-permute-start.39 = (bf16[16,2304]{1,0:T(8,128)(2,1)S(1)}, bf16[16,2304]{1,0:T(8,128)(2,1)S(1)}, u32[]{:S(2)}, u32[]{:S(2)}) collective-permute-start(bf16[16,2304]{1,0:T(8,128)(2,1)S(1)} %get-tuple-element.250), channel_id=1, source_target_pairs={{0,240},{16,0},{32,16},{48,32},{64,48},{80,64},{96,80},{112,96},{1... | collective-permute-start | bytes 221192 | tf_op jit(solution)/shard_map/ppermute | solution.py:265
  (2 other events, 2.2 us)

commit v6 on v5

--- a/solution.py
+++ b/solution.py
@@ -91,13 +91,15 @@
     pair_ref[rows:] = jnp.where(first, b_ref[...], a_ref[...])
 
 
-def out_kernel(*refs):
-    *parts, own_ref, pair_ref, keep_ref, send_ref, mine_ref = refs
+def out_kernel(count, *refs):
+    *refs, mine_ref = refs
+    parts, rest = refs[:count], refs[count:]
     size = parts[0].shape[0]
     for i, part in enumerate(parts):
         mine_ref[i * size : (i + 1) * size] = part[...]
-    send_ref[...] = dot_t(mine_ref[...], pair_ref[...]).astype(jnp.bfloat16)
-    keep_ref[...] = dot_t(mine_ref[...], own_ref[...]).astype(jnp.bfloat16)
+    products = len(rest) // 2
+    for weight, out in zip(rest[:products], rest[products:]):
+        out[...] = dot_t(mine_ref[...], weight[...]).astype(jnp.bfloat16)
 
 
 def value_kernel(keep_ref, recv_ref, low_t_ref, go_ref, own_ref, away_ref):
@@ -194,6 +196,7 @@
 FAR = pl.BlockSpec(memory_space=pltpu.HBM)
 LIGHT = pl.CostEstimate(flops=1000, bytes_accessed=1000, transcendentals=0)
 PARAMS = pltpu.CompilerParams(vmem_limit_bytes=24 * 1024 * 1024)
+WIDE = pltpu.CompilerParams(vmem_limit_bytes=56 * 1024 * 1024)
 
 
 def staged(kernel, shapes, operands, gate):
@@ -213,7 +216,7 @@
     )(*arrays, gate)
 
 
-def on_core(kernel, shapes, operands, scratch=()):
+def on_core(kernel, shapes, operands, scratch=(), params=PARAMS):
     return pl.pallas_call(
         kernel,
         out_shape=shapes,
@@ -221,7 +224,7 @@
         out_specs=[VMEM] * len(shapes),
         scratch_shapes=list(scratch),
         cost_estimate=LIGHT,
-        compiler_params=PARAMS,
+        compiler_params=params,
     )(*operands)
 
 
@@ -297,17 +300,13 @@
 
     def scatter(blocks, done):
         *near, edge = blocks
-        relayed = lax.ppermute(
-            edge, "tensor", [(2 * z, 2 * ((z + 1) % chips)) for z in range(chips)]
-        )
-        near[-1] = on_core(add_kernel, [bf16(2 * rows, width)], (near[-1], relayed))[0]
         moved = [hop(block, 1 + i, 0) for i, block in enumerate(near)]
         return hold((moved + [edge], done))
 
     other = swap(cot_in)
     other, *later = hold((other, w_value, w_out))
     away_value, away_out = (swap(item) for item in later)
-    pair = on_core(order_kernel, [bf16(2 * rows, width)], (cot_in, other))[0]
+    pair = on_core(order_kernel, [bf16(2 * rows, width)], (cot_in, other), params=WIDE)[0]
     weights = [w_out, away_out, w_value, away_value]
     query_list = []
     key_list = []
@@ -327,19 +326,24 @@
             ready_last = done
         own_out, pair_out, own_value, pair_value, _ = chosen
         chance, low_t = ready
-        keep, send = on_core(
-            out_kernel,
-            [bf16(half, heads * HD)] * 2,
-            [*parts, own_out, pair_out],
-            [pltpu.VMEM((half, width), jnp.bfloat16)],
-        )
+        groups = [[pair_out], [own_out]] if tick else [[pair_out, own_out]]
+        send, keep = [
+            product
+            for group in groups
+            for product in on_core(
+                functools.partial(out_kernel, len(parts)),
+                [bf16(half, heads * HD)] * len(group),
+                [*parts, *group],
+                [pltpu.VMEM((half, width), jnp.bfloat16)],
+            )
+        ]
         grad_out, value_keep, value_send = on_core(
             value_kernel,
             [bf16(length, heads * HD), bf16(half, HD), bf16(half, HD)],
             (keep, swap(send), low_t),
         )
         if tick:
-            odd = parts[0]
+            odd, value_send = hold((parts[0], value_send))
             value_away, even = hold((swap(value_send), swap(odd)))
         else:
             even = odd = pair
@@ -349,7 +353,12 @@
             [bf16(2 * rows, width)] * far,
             (value_keep, value_away, own_value, pair_value),
         )
-        gate = blocks[-1]
+        *near, edge = blocks
+        relayed = lax.ppermute(
+            edge, "tensor", [(2 * z, 2 * ((z + 1) % chips)) for z in range(chips)]
+        )
+        near[-1] = on_core(add_kernel, [bf16(2 * rows, width)], (near[-1], relayed))[0]
+        gate = near[-1]
         found = grads(chance, grad_out, tick, gate)
         lines = staged(
             lines_kernel,
@@ -365,7 +374,7 @@
             done = found, choose(2, plan, weights, gate)
         gain = choose(tick, plan, [norm_gain], gate)[0]
         done = done, lines, even, gain
-        terms, (done, lines, even, gain) = scatter(blocks, done)
+        terms, (done, lines, even, gain) = scatter([*near, edge], done)
         total = on_core(sum_kernel, [bf16(2 * rows, width)], terms)[0]
         if last:
             query, key = done

time: 159 us -> 157 us (0.987)
  waiting for transfers between devices: 67 us -> 57.3 us
  starting transfers between devices: 52.2 us -> 59.4 us
    ppermute x21, waiting for transfers between devices: 39.9 us -> 34.5 us  [hop(): return lax.ppermute(block, ('section', 'tensor'), pairs)]
    ppermute x21, starting transfers between devices: 40.7 us -> 45.8 us  [hop(): return lax.ppermute(block, ('section', 'tensor'), pairs)]
    ppermute x3, waiting for transfers between devices: 8.08 us -> 4.3 us  [on_device(): lax.ppermute(edge, 'tensor', [(2 * z, 2 * ((z + 1) % chips)) for z in ran...]
    ppermute x3, starting transfers between devices: 8.07 us -> 10.2 us  [on_device(): lax.ppermute(edge, 'tensor', [(2 * z, 2 * ((z + 1) % chips)) for z in ran...]
    pallas_call x19 -> x21, Pallas kernels: 10.5 us -> 10.8 us  [on_core(): pl.pallas_call(kernel, out_shape=shapes, in_specs=[VMEM] * len(operands),...]
    unnamed x23 -> x27, local copies, waits for them, and re-layouts: 5.24 us -> 5.4 us
  transfers between devices with their start and end apart: 40 -> 40, of which waited for: 24 -> 25; matrix products, arithmetic and copies ran while one was open for 1% -> 1% of each run, Pallas kernels for 17% -> 17%
where the time goes in v6:
time: 157 us
  starting transfers between devices  59.4 us (38%)
  waiting for transfers between devices  57.3 us (36%)
  Pallas kernels  31.8 us (20%)
  local copies, waits for them, and re-layouts  5.4 us (3%)
    ppermute x21, starting transfers between devices, hop(): return lax.ppermute(block, ('section', 'tensor'), pairs)  45.8 us
    ppermute x21, waiting for transfers between devices, hop(): return lax.ppermute(block, ('section', 'tensor'), pairs)  34.5 us
    pallas_call x9, Pallas kernels, staged(): pl.pallas_call(functools.partial(staged_kernel, kernel, picks, len(shapes...  12.3 us
    pallas_call x21, Pallas kernels, on_core(): pl.pallas_call(kernel, out_shape=shapes, in_specs=[VMEM] * len(operands),...  10.8 us
    ppermute x15, waiting for transfers between devices, swap(): return lax.ppermute(block, 'tensor', [(t, t ^ 1) for t in range(members)])  10.8 us
    ppermute x3, starting transfers between devices, on_device(): lax.ppermute(edge, 'tensor', [(2 * z, 2 * ((z + 1) % chips)) for z in ran...  10.2 us
    pallas_call x6, Pallas kernels, choose(): pl.pallas_call(functools.partial(choose_kernel, tick), out_shape=shapes,...  8.74 us
    ppermute x1, waiting for transfers between devices, along(): lax.ppermute(block, 'section', [(s, (s + by) % phases) for s in range(pha...  7.67 us
  transfers between devices with their start and end apart: 40, of which 25 were waited for; matrix products, arithmetic and copies ran while one was open for 1% of the time, Pallas kernels for 17%

profile of v6, /device:TPU:30, one launch (start us, length us, event | category | flops | bytes accessed | tf_op | source)
XLA Modules:
  0.0 156.5 jit_solution(3789627021165580585)
XLA Ops:
  0.7 1.5 collective-permute-done.b_ref
  2.8 1.6 %shard_map.121.refs_4_.even_ref.odd_ref = bf16[32,2304]{1,0:T(8,128)(2,1)} custom-call(bf16[16,2304]{1,0:T(8,128)(2,1)} %a_ref.1, bf16[16,2304]{1,0:T(8,128)(2,1)} %copy-done.10), custom_call_target="tpu_custom_call" | custom-call | flops 1000 | bytes 1000 | tf_op jit(solution)/shard_map/pallas_call | solution.py:220
  4.4 1.9 %collective-permute-start.4 = (bf16[32,2304]{1,0:T(8,128)(2,1)}, bf16[32,2304]{1,0:T(8,128)(2,1)}, u32[]{:S(2)}, u32[]{:S(2)}) collective-permute-start(bf16[32,2304]{1,0:T(8,128)(2,1)} %shard_map.121.refs_4_.even_ref.odd_ref), channel_id=1, source_target_pairs={{0,2},{1,15},{2,4},{3,1},{4,6},{5,3},{6,8},{7,5},{8,10},{9,7},{10,... | collective-permute-start | bytes 442376 | tf_op jit(solution)/shard_map/ppermute | solution.py:278
  6.3 3.3 %collective-permute-start.3 = (bf16[32,2304]{1,0:T(8,128)(2,1)}, bf16[32,2304]{1,0:T(8,128)(2,1)}, u32[]{:S(2)}, u32[]{:S(2)}) collective-permute-start(bf16[32,2304]{1,0:T(8,128)(2,1)} %shard_map.121.refs_4_.even_ref.odd_ref), channel_id=1, source_target_pairs={{0,4},{1,13},{2,6},{3,15},{4,8},{5,1},{6,10},{7,3},{8,12},{9,5},{1... | collective-permute-start | bytes 442376 | tf_op jit(solution)/shard_map/ppermute | solution.py:278
  9.6 4.0 %collective-permute-start.2 = (bf16[32,2304]{1,0:T(8,128)(2,1)}, bf16[32,2304]{1,0:T(8,128)(2,1)}, u32[]{:S(2)}, u32[]{:S(2)}) collective-permute-start(bf16[32,2304]{1,0:T(8,128)(2,1)} %shard_map.121.refs_4_.even_ref.odd_ref), channel_id=1, source_target_pairs={{0,6},{1,11},{2,8},{3,13},{4,10},{5,15},{6,12},{7,1},{8,14},{9,3},... | collective-permute-start | bytes 442376 | tf_op jit(solution)/shard_map/ppermute | solution.py:278
  13.7 4.1 %collective-permute-start.1 = (bf16[32,2304]{1,0:T(8,128)(2,1)}, bf16[32,2304]{1,0:T(8,128)(2,1)}, u32[]{:S(2)}, u32[]{:S(2)}) collective-permute-start(bf16[32,2304]{1,0:T(8,128)(2,1)} %shard_map.121.refs_4_.even_ref.odd_ref), channel_id=1, source_target_pairs={{0,8},{1,1},{2,10},{3,3},{4,12},{5,5},{6,14},{7,7},{8,0},{9,9},{10... | collective-permute-start | bytes 442376 | tf_op jit(solution)/shard_map/ppermute | solution.py:278
  18.6 1.7 %copy-done = bf16[2,1,256,2304]{3,2,1,0:T(8,128)(2,1)S(1)} copy-done((bf16[2,1,256,2304]{3,2,1,0:T(8,128)(2,1)S(1)}, bf16[2,1,256,2304]{3,2,1,0:T(8,128)(2,1)}, u32[]{:S(2)}) %copy-start) | copy-done | bytes 2359320
  20.3 1.3 copy-done.3
  22.4 1.3 shard_map.122
  23.8 1.6 %shard_map.123 = (f32[2,256,256]{2,1,0:T(8,128)S(1)}, bf16[2,256,256]{2,1,0:T(8,128)(2,1)S(1)}) custom-call(bf16[3,256,256]{2,1,0:T(8,128)(2,1)S(1)} %copy-done.2, bf16[3,256,128]{2,1,0:T(8,128)(2,1)S(1)} %copy-done.4, s32[3,1,256]{2,1,0:T(1,128)S(1)} %copy-done.9, f32[8,128]{1,0:T(8,128)S(1)} %get-tuple-element.131.refs_3_), custom_call_target="tpu_custom_call" | custom-call | flops 1000 | bytes 1000 | tf_op jit(solution)/shard_map/pallas_call | solution.py:208
  25.9 2.0 %shard_map.124 = (bf16[128,256]{1,0:T(8,128)(2,1)S(1)}, bf16[128,256]{1,0:T(8,128)(2,1)S(1)}) custom-call(bf16[32,2304]{1,0:T(8,128)(2,1)} %collective-permute-done.1.refs_0_, bf16[32,2304]{1,0:T(8,128)(2,1)} %collective-permute-done.2.refs_1_, bf16[32,2304]{1,0:T(8,128)(2,1)} %collective-permute-done.3.refs_2_, ...), custom_call_target="tpu_custom_call" | custom-call | flops 1000 | bytes 1000 | tf_op jit(solution)/shard_map/pallas_call | solution.py:220
  31.3 3.9 %collective-permute-start.12 = (bf16[32,2304]{1,0:T(8,128)(2,1)S(1)}, bf16[32,2304]{1,0:T(8,128)(2,1)S(1)}, u32[]{:S(2)}, u32[]{:S(2)}) collective-permute-start(bf16[32,2304]{1,0:T(8,128)(2,1)S(1)} %get-tuple-element.171.refs_3_), channel_id=1, source_target_pairs={{0,2},{2,4},{4,6},{6,8},{8,10},{10,12},{12,14},{14,0},{16,18},{18,... | collective-permute-start | bytes 442376 | tf_op jit(solution)/shard_map/ppermute | solution.py:357
  35.2 1.9 %collective-permute-start.10 = (bf16[32,2304]{1,0:T(8,128)(2,1)S(1)}, bf16[32,2304]{1,0:T(8,128)(2,1)S(1)}, u32[]{:S(2)}, u32[]{:S(2)}) collective-permute-start(bf16[32,2304]{1,0:T(8,128)(2,1)S(1)} %get-tuple-element.152), channel_id=1, source_target_pairs={{0,2},{1,15},{2,4},{3,1},{4,6},{5,3},{6,8},{7,5},{8,10},{9,7},{10,... | collective-permute-start | bytes 442376 | tf_op jit(solution)/shard_map/ppermute | solution.py:278
  38.1 1.6 %collective-permute-done.12.relayed_ref = bf16[32,2304]{1,0:T(8,128)(2,1)S(1)} collective-permute-done((bf16[32,2304]{1,0:T(8,128)(2,1)S(1)}, bf16[32,2304]{1,0:T(8,128)(2,1)S(1)}, u32[]{:S(2)}, u32[]{:S(2)}) %collective-permute-start.12) | collective-permute-done | bytes 147488 | tf_op jit(solution)/shard_map/ppermute | solution.py:357
  39.7 2.1 %collective-permute-start.13 = (bf16[32,2304]{1,0:T(8,128)(2,1)S(1)}, bf16[32,2304]{1,0:T(8,128)(2,1)S(1)}, u32[]{:S(2)}, u32[]{:S(2)}) collective-permute-start(bf16[32,2304]{1,0:T(8,128)(2,1)S(1)} %shard_map.127.refs_5_.refs_4_.refs_3_.refs_2_.refs_1_), channel_id=1, source_target_pairs={{0,6},{1,11},{2,8},{3,13},{4,10},{5,15},{6,12},{7,1},{8,14},{9,3},... | collective-permute-start | bytes 442376 | tf_op jit(solution)/shard_map/ppermute | solution.py:278
  41.8 1.6 %shard_map.130 = (f32[2,256,256]{2,1,0:T(8,128)S(1)}, bf16[2,256,256]{2,1,0:T(8,128)(2,1)S(1)}) custom-call(bf16[3,256,256]{2,1,0:T(8,128)(2,1)S(1)} %copy-done.2, bf16[3,256,128]{2,1,0:T(8,128)(2,1)S(1)} %copy-done.4, s32[3,1,256]{2,1,0:T(1,128)S(1)} %copy-done.9, bf16[32,2304]{1,0:T(8,128)(2,1)S(1)} %shard_map.127.refs_5_.refs_4_.refs_3_.refs_2_.refs_1_), custom_call_target="tpu_custom_call" | custom-call | flops 1000 | bytes 1000 | tf_op jit(solution)/shard_map/pallas_call | solution.py:208
  43.5 1.2 shard_map.132
  45.7 1.5 shard_map.128
  47.2 1.9 %shard_map.129 = (bf16[256,2304]{1,0:T(8,128)(2,1)S(1)}, bf16[256,2304]{1,0:T(8,128)(2,1)S(1)}, bf16[2304,128]{1,0:T(8,128)(2,1)S(1)}, bf16[2304,128]{1,0:T(8,128)(2,1)S(1)}, f32[8,128]{1,0:T(8,128)}) custom-call(s32[3,1]{1,0:T(4,128)S(1)} %copy.13.plan_ref, bf16[2,1,256,2304]{3,2,1,0:T(8,128)(2,1)S(1)} %copy-done.1, ...), custom_call_target="tpu_custom_call" | custom-call | flops 1000 | bytes 1000 | tf_op jit(solution)/shard_map/pallas_call | solution.py:234
  49.2 2.0 %collective-permute-done.13.refs_2_ = bf16[32,2304]{1,0:T(8,128)(2,1)S(1)} collective-permute-done((bf16[32,2304]{1,0:T(8,128)(2,1)S(1)}, bf16[32,2304]{1,0:T(8,128)(2,1)S(1)}, u32[]{:S(2)}, u32[]{:S(2)}) %collective-permute-start.13) | collective-permute-done | bytes 147488 | tf_op jit(solution)/shard_map/ppermute | solution.py:278
  51.4 1.4 collective-permute-done.14.b_ref
  54.3 1.2 collective-permute-start.17
  55.5 1.9 %collective-permute-start.16 = (bf16[32,2304]{1,0:T(8,128)(2,1)S(1)}, bf16[32,2304]{1,0:T(8,128)(2,1)S(1)}, u32[]{:S(2)}, u32[]{:S(2)}) collective-permute-start(bf16[32,2304]{1,0:T(8,128)(2,1)S(1)} %get-tuple-element.175.refs_3_), channel_id=1, source_target_pairs={{0,246},{1,251},{2,248},{3,253},{4,250},{5,255},{6,252},{7,241},{8... | collective-permute-start | bytes 442376 | tf_op jit(solution)/shard_map/ppermute | solution.py:278
  57.4 4.9 %collective-permute-start.15 = (bf16[32,2304]{1,0:T(8,128)(2,1)S(1)}, bf16[32,2304]{1,0:T(8,128)(2,1)S(1)}, u32[]{:S(2)}, u32[]{:S(2)}) collective-permute-start(bf16[32,2304]{1,0:T(8,128)(2,1)S(1)} %get-tuple-element.175.refs_3_), channel_id=1, source_target_pairs={{0,248},{1,241},{2,250},{3,243},{4,252},{5,245},{6,254},{7,247},{8... | collective-permute-start | bytes 442376 | tf_op jit(solution)/shard_map/ppermute | solution.py:278
  62.3 1.6 %shard_map.135 = (f32[2,256,256]{2,1,0:T(8,128)S(1)}, bf16[2,256,256]{2,1,0:T(8,128)(2,1)S(1)}) custom-call(bf16[3,256,256]{2,1,0:T(8,128)(2,1)S(1)} %copy-done.2, bf16[3,256,128]{2,1,0:T(8,128)(2,1)S(1)} %copy-done.4, s32[3,1,256]{2,1,0:T(1,128)S(1)} %copy-done.9, bf16[32,2304]{1,0:T(8,128)(2,1)S(1)} %get-tuple-element.175.refs_3_), custom_call_target="tpu_custom_call" | custom-call | flops 1000 | bytes 1000 | tf_op jit(solution)/shard_map/pallas_call | solution.py:208
  64.9 2.5 %collective-permute-done.17.refs_2_ = bf16[32,2304]{1,0:T(8,128)(2,1)S(1)} collective-permute-done((bf16[32,2304]{1,0:T(8,128)(2,1)S(1)}, bf16[32,2304]{1,0:T(8,128)(2,1)S(1)}, u32[]{:S(2)}, u32[]{:S(2)}) %collective-permute-start.17) | collective-permute-done | bytes 147488 | tf_op jit(solution)/shard_map/ppermute | solution.py:278
  67.4 7.7 %collective-permute-done.16.refs_1_ = bf16[32,2304]{1,0:T(8,128)(2,1)S(1)} collective-permute-done((bf16[32,2304]{1,0:T(8,128)(2,1)S(1)}, bf16[32,2304]{1,0:T(8,128)(2,1)S(1)}, u32[]{:S(2)}, u32[]{:S(2)}) %collective-permute-start.16) | collective-permute-done | bytes 147488 | tf_op jit(solution)/shard_map/ppermute | solution.py:278
  79.2 2.9 %collective-permute-start.24 = (bf16[32,2304]{1,0:T(8,128)(2,1)S(1)}, bf16[32,2304]{1,0:T(8,128)(2,1)S(1)}, u32[]{:S(2)}, u32[]{:S(2)}) collective-permute-start(bf16[32,2304]{1,0:T(8,128)(2,1)S(1)} %get-tuple-element.210.refs_3_), channel_id=1, source_target_pairs={{0,2},{2,4},{4,6},{6,8},{8,10},{10,12},{12,14},{14,0},{16,18},{18,... | collective-permute-start | bytes 442376 | tf_op jit(solution)/shard_map/ppermute | solution.py:357
  82.2 2.4 %collective-permute-start.22 = (bf16[32,2304]{1,0:T(8,128)(2,1)S(1)}, bf16[32,2304]{1,0:T(8,128)(2,1)S(1)}, u32[]{:S(2)}, u32[]{:S(2)}) collective-permute-start(bf16[32,2304]{1,0:T(8,128)(2,1)S(1)} %get-tuple-element.192), channel_id=1, source_target_pairs={{0,2},{1,15},{2,4},{3,1},{4,6},{5,3},{6,8},{7,5},{8,10},{9,7},{10,... | collective-permute-start | bytes 442376 | tf_op jit(solution)/shard_map/ppermute | solution.py:278
  85.7 1.8 %collective-permute-done.24.relayed_ref = bf16[32,2304]{1,0:T(8,128)(2,1)S(1)} collective-permute-done((bf16[32,2304]{1,0:T(8,128)(2,1)S(1)}, bf16[32,2304]{1,0:T(8,128)(2,1)S(1)}, u32[]{:S(2)}, u32[]{:S(2)}) %collective-permute-start.24) | collective-permute-done | bytes 147488 | tf_op jit(solution)/shard_map/ppermute | solution.py:357
  87.5 1.3 collective-permute-start.25
  91.0 1.5 shard_map.141
  92.5 1.9 %shard_map.142 = (bf16[256,2304]{1,0:T(8,128)(2,1)S(1)}, bf16[256,2304]{1,0:T(8,128)(2,1)S(1)}, bf16[2304,128]{1,0:T(8,128)(2,1)S(1)}, bf16[2304,128]{1,0:T(8,128)(2,1)S(1)}, f32[8,128]{1,0:T(8,128)}) custom-call(s32[3,1]{1,0:T(4,128)S(1)} %copy.13.plan_ref, bf16[2,1,256,2304]{3,2,1,0:T(8,128)(2,1)S(1)} %copy-done.1, ...), custom_call_target="tpu_custom_call" | custom-call | flops 1000 | bytes 1000 | tf_op jit(solution)/shard_map/pallas_call | solution.py:234
  94.5 4.5 %collective-permute-done.25.refs_2_ = bf16[32,2304]{1,0:T(8,128)(2,1)S(1)} collective-permute-done((bf16[32,2304]{1,0:T(8,128)(2,1)S(1)}, bf16[32,2304]{1,0:T(8,128)(2,1)S(1)}, u32[]{:S(2)}, u32[]{:S(2)}) %collective-permute-start.25) | collective-permute-done | bytes 147488 | tf_op jit(solution)/shard_map/ppermute | solution.py:278
  99.2 1.4 collective-permute-done.26.b_ref
  101.4 1.3 collective-permute-start.28
  102.7 5.6 %collective-permute-start.27 = (bf16[32,2304]{1,0:T(8,128)(2,1)S(1)}, bf16[32,2304]{1,0:T(8,128)(2,1)S(1)}, u32[]{:S(2)}, u32[]{:S(2)}) collective-permute-start(bf16[32,2304]{1,0:T(8,128)(2,1)S(1)} %get-tuple-element.214), channel_id=1, source_target_pairs={{0,248},{1,241},{2,250},{3,243},{4,252},{5,245},{6,254},{7,247},{8... | collective-permute-start | bytes 442376 | tf_op jit(solution)/shard_map/ppermute | solution.py:278
  108.3 4.0 %collective-permute-done.30.refs_3_ = bf16[32,2304]{1,0:T(8,128)(2,1)S(1)} collective-permute-done((bf16[32,2304]{1,0:T(8,128)(2,1)S(1)}, bf16[32,2304]{1,0:T(8,128)(2,1)S(1)}, u32[]{:S(2)}, u32[]{:S(2)}) %collective-permute-start.30) | collective-permute-done | bytes 147488 | tf_op jit(solution)/shard_map/ppermute | solution.py:278
  112.3 3.8 %collective-permute-done.29.refs_2_ = bf16[32,2304]{1,0:T(8,128)(2,1)S(1)} collective-permute-done((bf16[32,2304]{1,0:T(8,128)(2,1)S(1)}, bf16[32,2304]{1,0:T(8,128)(2,1)S(1)}, u32[]{:S(2)}, u32[]{:S(2)}) %collective-permute-start.29) | collective-permute-done | bytes 147488 | tf_op jit(solution)/shard_map/ppermute | solution.py:278
  116.1 1.9 %collective-permute-done.28.refs_1_ = bf16[32,2304]{1,0:T(8,128)(2,1)S(1)} collective-permute-done((bf16[32,2304]{1,0:T(8,128)(2,1)S(1)}, bf16[32,2304]{1,0:T(8,128)(2,1)S(1)}, u32[]{:S(2)}, u32[]{:S(2)}) %collective-permute-start.28) | collective-permute-done | bytes 147488 | tf_op jit(solution)/shard_map/ppermute | solution.py:278
  118.0 2.1 %collective-permute-done.27.refs_0_.odd_ref = bf16[32,2304]{1,0:T(8,128)(2,1)S(1)} collective-permute-done((bf16[32,2304]{1,0:T(8,128)(2,1)S(1)}, bf16[32,2304]{1,0:T(8,128)(2,1)S(1)}, u32[]{:S(2)}, u32[]{:S(2)}) %collective-permute-start.27) | collective-permute-done | bytes 147488 | tf_op jit(solution)/shard_map/ppermute | solution.py:278
  124.7 3.3 %collective-permute-start.36 = (bf16[32,2304]{1,0:T(8,128)(2,1)S(1)}, bf16[32,2304]{1,0:T(8,128)(2,1)S(1)}, u32[]{:S(2)}, u32[]{:S(2)}) collective-permute-start(bf16[32,2304]{1,0:T(8,128)(2,1)S(1)} %get-tuple-element.246.refs_3_), channel_id=1, source_target_pairs={{0,2},{2,4},{4,6},{6,8},{8,10},{10,12},{12,14},{14,0},{16,18},{18,... | collective-permute-start | bytes 442376 | tf_op jit(solution)/shard_map/ppermute | solution.py:357
  128.0 4.0 %collective-permute-start.34 = (bf16[32,2304]{1,0:T(8,128)(2,1)S(1)}, bf16[32,2304]{1,0:T(8,128)(2,1)S(1)}, u32[]{:S(2)}, u32[]{:S(2)}) collective-permute-start(bf16[32,2304]{1,0:T(8,128)(2,1)S(1)} %get-tuple-element.229), channel_id=1, source_target_pairs={{0,2},{1,15},{2,4},{3,1},{4,6},{5,3},{6,8},{7,5},{8,10},{9,7},{10,... | collective-permute-start | bytes 442376 | tf_op jit(solution)/shard_map/ppermute | solution.py:278
  133.1 3.1 %collective-permute-start.37 = (bf16[32,2304]{1,0:T(8,128)(2,1)S(1)}, bf16[32,2304]{1,0:T(8,128)(2,1)S(1)}, u32[]{:S(2)}, u32[]{:S(2)}) collective-permute-start(bf16[32,2304]{1,0:T(8,128)(2,1)S(1)} %shard_map.151.refs_5_.refs_2_.refs_1_), channel_id=1, source_target_pairs={{0,6},{1,11},{2,8},{3,13},{4,10},{5,15},{6,12},{7,1},{8,14},{9,3},... | collective-permute-start | bytes 442376 | tf_op jit(solution)/shard_map/ppermute | solution.py:278
  136.1 1.5 shard_map.152
  141.3 4.5 %collective-permute-done.37.refs_2_ = bf16[32,2304]{1,0:T(8,128)(2,1)S(1)} collective-permute-done((bf16[32,2304]{1,0:T(8,128)(2,1)S(1)}, bf16[32,2304]{1,0:T(8,128)(2,1)S(1)}, u32[]{:S(2)}, u32[]{:S(2)}) %collective-permute-start.37) | collective-permute-done | bytes 147488 | tf_op jit(solution)/shard_map/ppermute | solution.py:278
  146.0 1.4 collective-permute-done.38.b_ref
  148.2 7.7 %collective-permute-done.39 = bf16[16,2304]{1,0:T(8,128)(2,1)S(1)} collective-permute-done((bf16[16,2304]{1,0:T(8,128)(2,1)S(1)}, bf16[16,2304]{1,0:T(8,128)(2,1)S(1)}, u32[]{:S(2)}, u32[]{:S(2)}) %collective-permute-start.39) | collective-permute-done | bytes 73760 | tf_op jit(solution)/shard_map/ppermute | solution.py:268
  (97 shorter events, 30.5 us)
Async XLA Ops:
  0.6 1.6 collective-permute-start
  2.2 15.5 %collective-permute-start.5 = (bf16[2,1,256,2304]{3,2,1,0:T(8,128)(2,1)}, bf16[2,1,256,2304]{3,2,1,0:T(8,128)(2,1)S(1)}, u32[]{:S(2)}, u32[]{:S(2)}) collective-permute-start(bf16[2,1,256,2304]{3,2,1,0:T(8,128)(2,1)} %refs_0_.18), channel_id=1, source_target_pairs={{0,1},{1,0},{2,3},{3,2},{4,5},{5,4},{6,7},{7,6},{8,9},{9,8},{10,11... | collective-permute-start | bytes 7077896 | tf_op jit(solution)/shard_map/ppermute | solution.py:265
  2.4 11.3 %collective-permute-start.6 = (bf16[2,1,2304,128]{3,2,1,0:T(8,128)(2,1)}, bf16[2,1,2304,128]{3,2,1,0:T(8,128)(2,1)S(1)}, u32[]{:S(2)}, u32[]{:S(2)}) collective-permute-start(bf16[2,1,2304,128]{3,2,1,0:T(8,128)(2,1)} %refs_2_.16), channel_id=1, source_target_pairs={{0,1},{1,0},{2,3},{3,2},{4,5},{5,4},{6,7},{7,6},{8,9},{9,8},{10,11... | collective-permute-start | bytes 3538952 | tf_op jit(solution)/shard_map/ppermute | solution.py:265
  4.4 21.0 %collective-permute-start.4 = (bf16[32,2304]{1,0:T(8,128)(2,1)}, bf16[32,2304]{1,0:T(8,128)(2,1)}, u32[]{:S(2)}, u32[]{:S(2)}) collective-permute-start(bf16[32,2304]{1,0:T(8,128)(2,1)} %shard_map.121.refs_4_.even_ref.odd_ref), channel_id=1, source_target_pairs={{0,2},{1,15},{2,4},{3,1},{4,6},{5,3},{6,8},{7,5},{8,10},{9,7},{10,... | collective-permute-start | bytes 442376 | tf_op jit(solution)/shard_map/ppermute | solution.py:278
  6.3 19.1 %collective-permute-start.3 = (bf16[32,2304]{1,0:T(8,128)(2,1)}, bf16[32,2304]{1,0:T(8,128)(2,1)}, u32[]{:S(2)}, u32[]{:S(2)}) collective-permute-start(bf16[32,2304]{1,0:T(8,128)(2,1)} %shard_map.121.refs_4_.even_ref.odd_ref), channel_id=1, source_target_pairs={{0,4},{1,13},{2,6},{3,15},{4,8},{5,1},{6,10},{7,3},{8,12},{9,5},{1... | collective-permute-start | bytes 442376 | tf_op jit(solution)/shard_map/ppermute | solution.py:278
  9.6 15.9 %collective-permute-start.2 = (bf16[32,2304]{1,0:T(8,128)(2,1)}, bf16[32,2304]{1,0:T(8,128)(2,1)}, u32[]{:S(2)}, u32[]{:S(2)}) collective-permute-start(bf16[32,2304]{1,0:T(8,128)(2,1)} %shard_map.121.refs_4_.even_ref.odd_ref), channel_id=1, source_target_pairs={{0,6},{1,11},{2,8},{3,13},{4,10},{5,15},{6,12},{7,1},{8,14},{9,3},... | collective-permute-start | bytes 442376 | tf_op jit(solution)/shard_map/ppermute | solution.py:278
  13.7 12.2 %collective-permute-start.1 = (bf16[32,2304]{1,0:T(8,128)(2,1)}, bf16[32,2304]{1,0:T(8,128)(2,1)}, u32[]{:S(2)}, u32[]{:S(2)}) collective-permute-start(bf16[32,2304]{1,0:T(8,128)(2,1)} %shard_map.121.refs_4_.even_ref.odd_ref), channel_id=1, source_target_pairs={{0,8},{1,1},{2,10},{3,3},{4,12},{5,5},{6,14},{7,7},{8,0},{9,9},{10... | collective-permute-start | bytes 442376 | tf_op jit(solution)/shard_map/ppermute | solution.py:278
  17.7 12.0 %collective-permute-start.9 = (bf16[3,16,2304]{2,1,0:T(8,128)(2,1)}, bf16[3,16,2304]{2,1,0:T(8,128)(2,1)}, u32[]{:S(2)}, u32[]{:S(2)}) collective-permute-start(bf16[3,16,2304]{2,1,0:T(8,128)(2,1)} %refs_0_.20), channel_id=1, source_target_pairs={{0,1},{1,0},{2,3},{3,2},{4,5},{5,4},{6,7},{7,6},{8,9},{9,8},{10,11... | collective-permute-start | bytes 663560 | tf_op jit(solution)/shard_map/ppermute | solution.py:265
  18.6 1.7 %copy-start = (bf16[2,1,256,2304]{3,2,1,0:T(8,128)(2,1)S(1)}, bf16[2,1,256,2304]{3,2,1,0:T(8,128)(2,1)}, u32[]{:S(2)}) copy-start(bf16[2,1,256,2304]{3,2,1,0:T(8,128)(2,1)} %refs_0_.18) | copy-start | bytes 7077892
  22.4 1.4 copy-start.4
  22.4 1.4 copy-start.9
  27.9 13.9 %copy-start.11 = (bf16[2,1,2304]{2,0,1:T(2,128)(2,1)S(1)}, bf16[2,1,2304]{2,0,1:T(2,128)(2,1)}, u32[]{:S(2)}) copy-start(bf16[2,1,2304]{2,0,1:T(2,128)(2,1)} %param.19) | copy-start | bytes 27652
  27.9 1.3 collective-permute-start.7
  29.5 1.3 collective-permute-start.8
  30.8 13.9 %copy-start.7 = (bf16[3,16,2304]{2,1,0:T(8,128)(2,1)S(1)}, bf16[3,16,2304]{2,1,0:T(8,128)(2,1)}, u32[]{:S(2)}) copy-start(bf16[3,16,2304]{2,1,0:T(8,128)(2,1)} %refs_0_.20) | copy-start | bytes 663556
  31.3 14.5 %copy-start.8 = (bf16[3,256,128]{2,1,0:T(8,128)(2,1)S(1)}, bf16[3,256,128]{2,1,0:T(8,128)(2,1)}, u32[]{:S(2)}) copy-start(bf16[3,256,128]{2,1,0:T(8,128)(2,1)} %refs_4_.5) | copy-start | bytes 589828
  31.3 8.4 %collective-permute-start.12 = (bf16[32,2304]{1,0:T(8,128)(2,1)S(1)}, bf16[32,2304]{1,0:T(8,128)(2,1)S(1)}, u32[]{:S(2)}, u32[]{:S(2)}) collective-permute-start(bf16[32,2304]{1,0:T(8,128)(2,1)S(1)} %get-tuple-element.171.refs_3_), channel_id=1, source_target_pairs={{0,2},{2,4},{4,6},{6,8},{8,10},{10,12},{12,14},{14,0},{16,18},{18,... | collective-permute-start | bytes 442376 | tf_op jit(solution)/shard_map/ppermute | solution.py:357
  35.2 14.0 %collective-permute-start.10 = (bf16[32,2304]{1,0:T(8,128)(2,1)S(1)}, bf16[32,2304]{1,0:T(8,128)(2,1)S(1)}, u32[]{:S(2)}, u32[]{:S(2)}) collective-permute-start(bf16[32,2304]{1,0:T(8,128)(2,1)S(1)} %get-tuple-element.152), channel_id=1, source_target_pairs={{0,2},{1,15},{2,4},{3,1},{4,6},{5,3},{6,8},{7,5},{8,10},{9,7},{10,... | collective-permute-start | bytes 442376 | tf_op jit(solution)/shard_map/ppermute | solution.py:278
  37.1 12.1 %collective-permute-start.11 = (bf16[32,2304]{1,0:T(8,128)(2,1)S(1)}, bf16[32,2304]{1,0:T(8,128)(2,1)S(1)}, u32[]{:S(2)}, u32[]{:S(2)}) collective-permute-start(bf16[32,2304]{1,0:T(8,128)(2,1)S(1)} %get-tuple-element.153), channel_id=1, source_target_pairs={{0,4},{1,13},{2,6},{3,15},{4,8},{5,1},{6,10},{7,3},{8,12},{9,5},{1... | collective-permute-start | bytes 442376 | tf_op jit(solution)/shard_map/ppermute | solution.py:278
  39.7 11.5 %collective-permute-start.13 = (bf16[32,2304]{1,0:T(8,128)(2,1)S(1)}, bf16[32,2304]{1,0:T(8,128)(2,1)S(1)}, u32[]{:S(2)}, u32[]{:S(2)}) collective-permute-start(bf16[32,2304]{1,0:T(8,128)(2,1)S(1)} %shard_map.127.refs_5_.refs_4_.refs_3_.refs_2_.refs_1_), channel_id=1, source_target_pairs={{0,6},{1,11},{2,8},{3,13},{4,10},{5,15},{6,12},{7,1},{8,14},{9,3},... | collective-permute-start | bytes 442376 | tf_op jit(solution)/shard_map/ppermute | solution.py:278
  43.5 3.7 %copy-start.1 = (bf16[2,1,256,2304]{3,2,1,0:T(8,128)(2,1)S(1)}, bf16[2,1,256,2304]{3,2,1,0:T(8,128)(2,1)}, u32[]{:S(2)}) copy-start(bf16[2,1,256,2304]{3,2,1,0:T(8,128)(2,1)} %refs_0_.18) | copy-start | bytes 7077892
  47.2 5.5 %copy-start.6 = (bf16[32,2304]{1,0:T(8,128)(2,1)S(1)}, bf16[32,2304]{1,0:T(8,128)(2,1)}, u32[]{:S(2)}) copy-start(bf16[32,2304]{1,0:T(8,128)(2,1)} %shard_map.121.refs_4_.even_ref.odd_ref) | copy-start | bytes 442372
  51.3 1.5 collective-permute-start.14
  53.6 11.3 %collective-permute-start.18 = (bf16[32,2304]{1,0:T(8,128)(2,1)S(1)}, bf16[32,2304]{1,0:T(8,128)(2,1)S(1)}, u32[]{:S(2)}, u32[]{:S(2)}) collective-permute-start(bf16[32,2304]{1,0:T(8,128)(2,1)S(1)} %get-tuple-element.175.refs_3_), channel_id=1, source_target_pairs={{0,242},{1,255},{2,244},{3,241},{4,246},{5,243},{6,248},{7,245},{8... | collective-permute-start | bytes 442376 | tf_op jit(solution)/shard_map/ppermute | solution.py:278
  54.3 13.1 %collective-permute-start.17 = (bf16[32,2304]{1,0:T(8,128)(2,1)S(1)}, bf16[32,2304]{1,0:T(8,128)(2,1)S(1)}, u32[]{:S(2)}, u32[]{:S(2)}) collective-permute-start(bf16[32,2304]{1,0:T(8,128)(2,1)S(1)} %get-tuple-element.175.refs_3_), channel_id=1, source_target_pairs={{0,244},{1,253},{2,246},{3,255},{4,248},{5,241},{6,250},{7,243},{8... | collective-permute-start | bytes 442376 | tf_op jit(solution)/shard_map/ppermute | solution.py:278
  55.5 19.6 %collective-permute-start.16 = (bf16[32,2304]{1,0:T(8,128)(2,1)S(1)}, bf16[32,2304]{1,0:T(8,128)(2,1)S(1)}, u32[]{:S(2)}, u32[]{:S(2)}) collective-permute-start(bf16[32,2304]{1,0:T(8,128)(2,1)S(1)} %get-tuple-element.175.refs_3_), channel_id=1, source_target_pairs={{0,246},{1,251},{2,248},{3,253},{4,250},{5,255},{6,252},{7,241},{8... | collective-permute-start | bytes 442376 | tf_op jit(solution)/shard_map/ppermute | solution.py:278
  57.4 17.7 %collective-permute-start.15 = (bf16[32,2304]{1,0:T(8,128)(2,1)S(1)}, bf16[32,2304]{1,0:T(8,128)(2,1)S(1)}, u32[]{:S(2)}, u32[]{:S(2)}) collective-permute-start(bf16[32,2304]{1,0:T(8,128)(2,1)S(1)} %get-tuple-element.175.refs_3_), channel_id=1, source_target_pairs={{0,248},{1,241},{2,250},{3,243},{4,252},{5,245},{6,254},{7,247},{8... | collective-permute-start | bytes 442376 | tf_op jit(solution)/shard_map/ppermute | solution.py:278
  75.7 1.3 collective-permute-start.19
  77.2 1.5 collective-permute-start.21
  77.5 1.3 collective-permute-start.20
  79.2 8.2 %collective-permute-start.24 = (bf16[32,2304]{1,0:T(8,128)(2,1)S(1)}, bf16[32,2304]{1,0:T(8,128)(2,1)S(1)}, u32[]{:S(2)}, u32[]{:S(2)}) collective-permute-start(bf16[32,2304]{1,0:T(8,128)(2,1)S(1)} %get-tuple-element.210.refs_3_), channel_id=1, source_target_pairs={{0,2},{2,4},{4,6},{6,8},{8,10},{10,12},{12,14},{14,0},{16,18},{18,... | collective-permute-start | bytes 442376 | tf_op jit(solution)/shard_map/ppermute | solution.py:357
  82.2 12.3 %collective-permute-start.22 = (bf16[32,2304]{1,0:T(8,128)(2,1)S(1)}, bf16[32,2304]{1,0:T(8,128)(2,1)S(1)}, u32[]{:S(2)}, u32[]{:S(2)}) collective-permute-start(bf16[32,2304]{1,0:T(8,128)(2,1)S(1)} %get-tuple-element.192), channel_id=1, source_target_pairs={{0,2},{1,15},{2,4},{3,1},{4,6},{5,3},{6,8},{7,5},{8,10},{9,7},{10,... | collective-permute-start | bytes 442376 | tf_op jit(solution)/shard_map/ppermute | solution.py:278
  84.5 9.9 %collective-permute-start.23 = (bf16[32,2304]{1,0:T(8,128)(2,1)S(1)}, bf16[32,2304]{1,0:T(8,128)(2,1)S(1)}, u32[]{:S(2)}, u32[]{:S(2)}) collective-permute-start(bf16[32,2304]{1,0:T(8,128)(2,1)S(1)} %get-tuple-element.193), channel_id=1, source_target_pairs={{0,4},{1,13},{2,6},{3,15},{4,8},{5,1},{6,10},{7,3},{8,12},{9,5},{1... | collective-permute-start | bytes 442376 | tf_op jit(solution)/shard_map/ppermute | solution.py:278
  87.5 11.5 %collective-permute-start.25 = (bf16[32,2304]{1,0:T(8,128)(2,1)S(1)}, bf16[32,2304]{1,0:T(8,128)(2,1)S(1)}, u32[]{:S(2)}, u32[]{:S(2)}) collective-permute-start(bf16[32,2304]{1,0:T(8,128)(2,1)S(1)} %shard_map.140.refs_5_.refs_4_.refs_2_.refs_1_), channel_id=1, source_target_pairs={{0,6},{1,11},{2,8},{3,13},{4,10},{5,15},{6,12},{7,1},{8,14},{9,3},... | collective-permute-start | bytes 442376 | tf_op jit(solution)/shard_map/ppermute | solution.py:278
  99.1 1.5 collective-permute-start.26
  101.4 10.9 %collective-permute-start.30 = (bf16[32,2304]{1,0:T(8,128)(2,1)S(1)}, bf16[32,2304]{1,0:T(8,128)(2,1)S(1)}, u32[]{:S(2)}, u32[]{:S(2)}) collective-permute-start(bf16[32,2304]{1,0:T(8,128)(2,1)S(1)} %get-tuple-element.214), channel_id=1, source_target_pairs={{0,242},{1,255},{2,244},{3,241},{4,246},{5,243},{6,248},{7,245},{8... | collective-permute-start | bytes 442376 | tf_op jit(solution)/shard_map/ppermute | solution.py:278
  101.4 14.7 %collective-permute-start.29 = (bf16[32,2304]{1,0:T(8,128)(2,1)S(1)}, bf16[32,2304]{1,0:T(8,128)(2,1)S(1)}, u32[]{:S(2)}, u32[]{:S(2)}) collective-permute-start(bf16[32,2304]{1,0:T(8,128)(2,1)S(1)} %get-tuple-element.214), channel_id=1, source_target_pairs={{0,244},{1,253},{2,246},{3,255},{4,248},{5,241},{6,250},{7,243},{8... | collective-permute-start | bytes 442376 | tf_op jit(solution)/shard_map/ppermute | solution.py:278
  101.4 16.6 %collective-permute-start.28 = (bf16[32,2304]{1,0:T(8,128)(2,1)S(1)}, bf16[32,2304]{1,0:T(8,128)(2,1)S(1)}, u32[]{:S(2)}, u32[]{:S(2)}) collective-permute-start(bf16[32,2304]{1,0:T(8,128)(2,1)S(1)} %get-tuple-element.214), channel_id=1, source_target_pairs={{0,246},{1,251},{2,248},{3,253},{4,250},{5,255},{6,252},{7,241},{8... | collective-permute-start | bytes 442376 | tf_op jit(solution)/shard_map/ppermute | solution.py:278
  102.7 17.4 %collective-permute-start.27 = (bf16[32,2304]{1,0:T(8,128)(2,1)S(1)}, bf16[32,2304]{1,0:T(8,128)(2,1)S(1)}, u32[]{:S(2)}, u32[]{:S(2)}) collective-permute-start(bf16[32,2304]{1,0:T(8,128)(2,1)S(1)} %get-tuple-element.214), channel_id=1, source_target_pairs={{0,248},{1,241},{2,250},{3,243},{4,252},{5,245},{6,254},{7,247},{8... | collective-permute-start | bytes 442376 | tf_op jit(solution)/shard_map/ppermute | solution.py:278
  120.6 1.7 %collective-permute-start.31 = (bf16[128,256]{1,0:T(8,128)(2,1)S(1)}, bf16[128,256]{1,0:T(8,128)(2,1)S(1)}, u32[]{:S(2)}, u32[]{:S(2)}) collective-permute-start(bf16[128,256]{1,0:T(8,128)(2,1)S(1)} %shard_map.148), channel_id=1, source_target_pairs={{0,1},{1,0},{2,3},{3,2},{4,5},{5,4},{6,7},{7,6},{8,9},{9,8},{10,11... | collective-permute-start | bytes 196616 | tf_op jit(solution)/shard_map/ppermute | solution.py:265
  122.6 1.7 %collective-permute-start.33 = (bf16[32,2304]{1,0:T(8,128)(2,1)S(1)}, bf16[32,2304]{1,0:T(8,128)(2,1)S(1)}, u32[]{:S(2)}, u32[]{:S(2)}) collective-permute-start(bf16[32,2304]{1,0:T(8,128)(2,1)S(1)} %collective-permute-done.27.refs_0_.odd_ref), channel_id=1, source_target_pairs={{0,1},{1,0},{2,3},{3,2},{4,5},{5,4},{6,7},{7,6},{8,9},{9,8},{10,11... | collective-permute-start | bytes 442376 | tf_op jit(solution)/shard_map/ppermute | solution.py:265
  123.0 1.2 collective-permute-start.32
  124.7 8.3 %collective-permute-start.36 = (bf16[32,2304]{1,0:T(8,128)(2,1)S(1)}, bf16[32,2304]{1,0:T(8,128)(2,1)S(1)}, u32[]{:S(2)}, u32[]{:S(2)}) collective-permute-start(bf16[32,2304]{1,0:T(8,128)(2,1)S(1)} %get-tuple-element.246.refs_3_), channel_id=1, source_target_pairs={{0,2},{2,4},{4,6},{6,8},{8,10},{10,12},{12,14},{14,0},{16,18},{18,... | collective-permute-start | bytes 442376 | tf_op jit(solution)/shard_map/ppermute | solution.py:357
  128.0 13.2 %collective-permute-start.34 = (bf16[32,2304]{1,0:T(8,128)(2,1)S(1)}, bf16[32,2304]{1,0:T(8,128)(2,1)S(1)}, u32[]{:S(2)}, u32[]{:S(2)}) collective-permute-start(bf16[32,2304]{1,0:T(8,128)(2,1)S(1)} %get-tuple-element.229), channel_id=1, source_target_pairs={{0,2},{1,15},{2,4},{3,1},{4,6},{5,3},{6,8},{7,5},{8,10},{9,7},{10,... | collective-permute-start | bytes 442376 | tf_op jit(solution)/shard_map/ppermute | solution.py:278
  132.0 9.2 %collective-permute-start.35 = (bf16[32,2304]{1,0:T(8,128)(2,1)S(1)}, bf16[32,2304]{1,0:T(8,128)(2,1)S(1)}, u32[]{:S(2)}, u32[]{:S(2)}) collective-permute-start(bf16[32,2304]{1,0:T(8,128)(2,1)S(1)} %get-tuple-element.230), channel_id=1, source_target_pairs={{0,4},{1,13},{2,6},{3,15},{4,8},{5,1},{6,10},{7,3},{8,12},{9,5},{1... | collective-permute-start | bytes 442376 | tf_op jit(solution)/shard_map/ppermute | solution.py:278
  133.1 12.7 %collective-permute-start.37 = (bf16[32,2304]{1,0:T(8,128)(2,1)S(1)}, bf16[32,2304]{1,0:T(8,128)(2,1)S(1)}, u32[]{:S(2)}, u32[]{:S(2)}) collective-permute-start(bf16[32,2304]{1,0:T(8,128)(2,1)S(1)} %shard_map.151.refs_5_.refs_2_.refs_1_), channel_id=1, source_target_pairs={{0,6},{1,11},{2,8},{3,13},{4,10},{5,15},{6,12},{7,1},{8,14},{9,3},... | collective-permute-start | bytes 442376 | tf_op jit(solution)/shard_map/ppermute | solution.py:278
  145.9 1.5 collective-permute-start.38
  148.2 7.7 %collective-permute-start.39 = (bf16[16,2304]{1,0:T(8,128)(2,1)S(1)}, bf16[16,2304]{1,0:T(8,128)(2,1)S(1)}, u32[]{:S(2)}, u32[]{:S(2)}) collective-permute-start(bf16[16,2304]{1,0:T(8,128)(2,1)S(1)} %get-tuple-element.250), channel_id=1, source_target_pairs={{0,240},{16,0},{32,16},{48,32},{64,48},{80,64},{96,80},{112,96},{1... | collective-permute-start | bytes 221192 | tf_op jit(solution)/shard_map/ppermute | solution.py:268
  (4 other events, 4.2 us)
